TPU v7x, 256 devices: a whole 4x4x8 slice. The times are simulated.
256 devices in a mesh: wide: 64 (over x, z, core), grp: 4 (over y).
Axes of the slice: x: 4, y: 4, z: 8, core: 2. Of those that a mesh axis runs over, the one named last changes fastest.
Arguments:
- inst_rows: bfloat16 [262144, 768], P(('wide', 'grp')), may hold values from -6 to 6
- inst_labels: int32 [262144, 8], P(('wide', 'grp')), may hold values from 0 to 2047
- seed_labels: int32 [32], replicated, may hold values from 0 to 524287
- coarse_first: int32 [524288], P(('wide', 'grp')), may hold values from 0 to 31
- coarse_second: int32 [524288, 1], P(('wide', 'grp')), may hold values from 0 to 31; in each aligned block of 2048 rows (0 to 2047, 2048 to 4095, ...) at most 80 rows name the same one
- sub_assign: int32 [524288], P(('wide', 'grp')), may hold values from 0 to 15
- group_map: int32 [32], replicated, may hold values from 0 to 63, as said below
Outputs:
- label_vectors: bfloat16 [524288, 768], P(('wide', 'grp'))
- coarse_centroids: float32 [32, 768], replicated
- sub_centroids: float32 [64, 16, 768], P('wide')
Inputs may be any that keep to these rules, and one draw needn't show every extreme that they name: `inst_labels`: entries of block j of a device's rows name labels of the device with wide index j and the same grp index. `coarse_second`: among the 2048 labels of one device no cluster is named more than 80 times. `group_map`: no group hosts more than 1 clusters; one hosts exactly 1.
All inputs are finite; a program needn't handle non-finite values.
Results may differ from a plain program's by a relative error of at most 0.0054.
Values may be sent and summed in bfloat16 or wider, within the bound.
No kernel may reach another device: no remote copies, remote signals or barrier semaphores. Data moves between devices by JAX's collectives and lax.ppermute only.
A program may use at most 64 MiB of HBM per device.

v0:
```python
import jax
import jax.numpy as jnp
from jax import lax
from jax.sharding import PartitionSpec as P

SUB = 16


EPSILON = 1e-06
CONCENTRATION = 16.0


def rms_rows(matrix):
    return matrix * lax.rsqrt(jnp.mean(matrix * matrix, axis=-1, keepdims=True) + EPSILON)


def one_hot(labels_here, cluster_total):
    return labels_here[:, None] == lax.broadcasted_iota(jnp.int32, (1, cluster_total), 1)


def column_sums(weights, rows_here):
    return lax.dot_general(
        weights, rows_here, (((0,), (0,)), ((), ())), preferred_element_type=jnp.float32
    )


def weighted_sums(rows_here, centroids, labels_here, cluster_total):
    cent_bf = centroids.astype(jnp.bfloat16)
    scores = lax.dot_general(
        rows_here, cent_bf, (((1,), (1,)), ((), ())), preferred_element_type=jnp.float32
    )
    member = one_hot(labels_here, cluster_total)
    cosine = jnp.sum(jnp.where(member, scores, 0.0), axis=1) / rows_here.shape[1]
    weight = jnp.exp(CONCENTRATION * cosine)
    return column_sums(jnp.where(member, weight[:, None], 0.0).astype(jnp.bfloat16), rows_here)


def global_total(partial_value):
    return lax.psum(partial_value, ("wide", "grp"))


def group_total(partial_value):
    return lax.psum(partial_value, "grp")


def shards(inst_rows, inst_labels, seed_labels, coarse_first, coarse_second, sub_assign, group_map):
    n_wide = lax.axis_size("wide")
    n_grp = lax.axis_size("grp")
    lab_dev = coarse_first.shape[0]
    feature_width = inst_rows.shape[1]
    coarse_count = group_map.shape[0]
    sub_count = SUB
    received_rows, received_labels = (
        lax.all_to_all(inst_rows, "wide", split_axis=0, concat_axis=0, tiled=True),
        lax.all_to_all(inst_labels, "wide", split_axis=0, concat_axis=0, tiled=True),
    )
    tile_rows = min(512, lab_dev)

    def one_tile(tile_start):
        label_index = tile_start + lax.broadcasted_iota(jnp.int32, (tile_rows, 1), 0)
        counts = jnp.zeros((tile_rows, received_labels.shape[0]), jnp.int32)
        for column in range(received_labels.shape[1]):
            counts = counts + (received_labels[:, column][None, :] == label_index).astype(jnp.int32)
        return jnp.dot(
            counts.astype(jnp.bfloat16), received_rows, preferred_element_type=jnp.float32
        )

    tile_starts = jnp.arange(lab_dev // tile_rows, dtype=jnp.int32) * tile_rows
    label_sums = lax.map(one_tile, tile_starts).reshape(lab_dev, feature_width)
    label_vectors = rms_rows(label_sums).astype(jnp.bfloat16)
    label_base = (lax.axis_index("wide") * n_grp + lax.axis_index("grp")) * lab_dev
    seed_pick = one_hot(seed_labels - label_base, lab_dev).astype(jnp.bfloat16)
    seed_part = jnp.dot(seed_pick, label_vectors, preferred_element_type=jnp.float32)
    start_cent = rms_rows(lax.psum(seed_part, ("wide", "grp")))
    first_cent = rms_rows(
        global_total(weighted_sums(label_vectors, start_cent, coarse_first, coarse_count))
    )
    second = coarse_second[:, 0]
    coarse_centroids = rms_rows(
        global_total(weighted_sums(label_vectors, first_cent, second, coarse_count))
    )
    cluster_ids = lax.broadcasted_iota(jnp.int32, (coarse_count,), 0)
    same_host = group_map[:, None] == group_map[None, :]
    host_rank = jnp.sum(same_host & (cluster_ids[None, :] < cluster_ids[:, None]), axis=1)
    host_slots = max(1, 2 * coarse_count // n_wide)
    capacity = 5 * lab_dev // (4 * coarse_count)
    member = one_hot(second, coarse_count).astype(jnp.int32)
    cluster_rank = jnp.sum((jnp.cumsum(member, axis=0) - member) * member, axis=1)
    host_index = jnp.sum(member * group_map[None, :], axis=1)
    slot_rank = jnp.sum(member * host_rank[None, :], axis=1)
    slot_index = (host_index * host_slots + slot_rank) * capacity + cluster_rank
    buffer = (
        jnp.zeros((n_wide * host_slots * capacity, feature_width), jnp.bfloat16)
        .at[slot_index]
        .set(label_vectors)
    )
    code_list = (
        jnp.full((n_wide * host_slots * capacity,), -1, jnp.int32)
        .at[slot_index]
        .set(slot_rank * sub_count + sub_assign)
    )
    gathered, gathered_codes = (
        lax.all_to_all(buffer, "wide", split_axis=0, concat_axis=0, tiled=True),
        lax.all_to_all(code_list, "wide", split_axis=0, concat_axis=0, tiled=True),
    )
    local_count = host_slots * sub_count
    sub_start = rms_rows(
        group_total(
            column_sums(one_hot(gathered_codes, local_count).astype(jnp.bfloat16), gathered)
        )
    )
    hosted = rms_rows(group_total(weighted_sums(gathered, sub_start, gathered_codes, local_count)))
    return (
        label_vectors,
        coarse_centroids,
        hosted.reshape(1, host_slots * sub_count, feature_width),
    )


def solution(mesh):
    in_specs = (
        P(("wide", "grp"), None),
        P(("wide", "grp"), None),
        P(),
        P(("wide", "grp")),
        P(("wide", "grp"), None),
        P(("wide", "grp")),
        P(),
    )
    out_specs = (P(("wide", "grp"), None), P(), P("wide", None, None))
    return jax.shard_map(shards, mesh=mesh, in_specs=in_specs, out_specs=out_specs, check_vma=False)
```

profile of v0, /device:TPU:6, one launch (start us, length us, event | category | flops | bytes accessed | tf_op | source)
XLA Modules:
  0.0 952.6 jit_solution(5471221497382422234)
XLA Ops:
  8.4 19.5 %all_to_all.45 = s32[64,1,128]{2,1,0:T(1,128)S(1)} all-to-all(s32[64,1,128]{2,1,0:T(1,128)S(1)} %reshape.191), channel_id=1, replica_groups=mesh['wide'=64,'grp'=4] {'wide'}, dimensions={0} | all-to-all | bytes 65536 | tf_op jit(solution)/shard_map/all_to_all | solution.py:55
  28.0 6.6 all-to-all-start.1
  34.6 9.1 reduce-window.6
  44.8 8.1 scatter_custom_fusion
  55.2 16.9 %all-to-all-done.1 = bf16[64,16,768]{2,1,0:T(8,128)(2,1)S(1)} async-done(((bf16[64,16,768]{2,1,0:T(8,128)(2,1)}), bf16[64,16,768]{2,1,0:T(8,128)(2,1)S(1)}, u32[]{:S(2)}, u32[]{:S(2)}) %all-to-all-start.1) | async-done | bytes 1572896 | tf_op jit(solution)/shard_map/all_to_all | solution.py:54
  72.1 8.4 all-to-all-start.2
  80.5 19.4 %while.10 = (s32[]{:T(128)}, f32[4,512,768]{2,1,0:T(8,128)}, s32[1024,8]{0,1:T(8,128)S(1)}, s32[4]{0:T(128)S(1)}, bf16[1024,768]{1,0:T(8,128)(2,1)S(1)}, /*index=5*/s32[]{:T(128)}) while((s32[]{:T(128)}, f32[4,512,768]{2,1,0:T(8,128)}, s32[1024,8]{0,1:T(8,128)S(1)}, s32[4]{0:T(128)S(1)}, bf16[1024,768]{1,0:T(8,128)(2,1)S(1)}, ...), condition=%wide.region_1.2_spmd, body=%wide.region_0.1_spmd.sunk | while | flops 817889792 | bytes 3248725 | solution.py:69
  81.8 3.6 bitcast_dynamic-update-slice_fusion.2
  86.6 3.6 bitcast_dynamic-update-slice_fusion.2
  91.5 3.6 bitcast_dynamic-update-slice_fusion.2
  96.3 3.6 bitcast_dynamic-update-slice_fusion.2
  99.9 3.4 multiply_reduce_fusion
  104.9 14.4 %scatter_custom_fusion.1 = bf16[5120,768]{1,0:T(8,128)(2,1)} fusion(s32[2048]{0:T(1024)S(1)} %bitcast.112, bf16[2048,768]{1,0:T(8,128)(2,1)S(1)} %fusion.9, bf16[]{:T(256)} %constant.68.clone.1), kind=kCustom, calls=%fused_computation.18 | custom fusion | bytes 7864322 | tf_op jit(solution)/shard_map/scatter | solution.py:95
  119.3 10.6 %all-to-all-start.3 = ((bf16[64,80,768]{2,1,0:T(8,128)(2,1)}), bf16[64,80,768]{2,1,0:T(8,128)(2,1)}, u32[]{:S(2)}, u32[]{:S(2)}) async-start(bf16[64,80,768]{2,1,0:T(8,128)(2,1)} %bitcast.89), calls=%async_computation.3 | async-start | bytes 15728640 | tf_op jit(solution)/shard_map/all_to_all | solution.py:103
  131.4 280.0 %all-reduce.4.cloned.1.call-done = f32[32,768]{1,0:T(8,128)} async-done(((f32[32,768]{1,0:T(8,128)}), f32[32,768]{1,0:T(8,128)}) %all-reduce.4.cloned.1.call-update) | async-done | bytes 98320 | tf_op jit(solution)/shard_map/psum | solution.py:74
  412.4 1.9 fusion.13
  416.0 238.3 %all-reduce.6.cloned.1.call-done = f32[32,768]{1,0:T(8,128)} async-done(((f32[32,768]{1,0:T(8,128)}), f32[32,768]{1,0:T(8,128)}) %all-reduce.6.cloned.1.call-update) | async-done | bytes 98320 | tf_op jit(solution)/shard_map/psum | solution.py:39
  655.3 1.9 fusion.14
  659.9 237.2 %all-reduce.8.cloned.1.call-done = f32[32,768]{1,0:T(8,128)} async-done(((f32[32,768]{1,0:T(8,128)}), f32[32,768]{1,0:T(8,128)}) %all-reduce.8.cloned.1.call-update) | async-done | bytes 98320 | tf_op jit(solution)/shard_map/psum | solution.py:39
  899.7 4.4 fusion.15
  904.1 16.3 %psum.38 = f32[16,768]{1,0:T(8,128)S(1)} all-reduce(f32[16,768]{1,0:T(8,128)S(1)} %fusion.15), channel_id=1, replica_groups=mesh['wide'=64,'grp'=4] {'grp'}, use_global_device_ids=true, to_apply=%region_19.20 | all-reduce | flops 12288 | bytes 98304 | tf_op jit(solution)/shard_map/psum | solution.py:43
  920.6 5.4 fusion.12
  926.0 4.4 fusion.21
  930.4 14.9 %psum.39 = f32[16,768]{1,0:T(8,128)S(1)} all-reduce(f32[16,768]{1,0:T(8,128)S(1)} %fusion.21), channel_id=1, replica_groups=mesh['wide'=64,'grp'=4] {'grp'}, use_global_device_ids=true, to_apply=%region_22.23 | all-reduce | flops 12288 | bytes 98304 | tf_op jit(solution)/shard_map/psum | solution.py:43
  (79 shorter events, 22.5 us)
Async XLA Ops:
  7.2 27.4 %copy-start.2 = (s32[2048,1]{0,1:T(1,128)S(1)}, s32[2048,1]{0,1:T(1,128)}, u32[]{:S(2)}) copy-start(s32[2048,1]{0,1:T(1,128)} %param.13) | copy-start | bytes 24580
  7.2 37.1 %copy-start.5 = (s32[32]{0:T(128)S(1)}, s32[32]{0:T(128)}, u32[]{:S(2)}) copy-start(s32[32]{0:T(128)} %param.15) | copy-start | bytes 388
  8.1 36.7 %copy-start.4 = (s32[2048]{0:T(1024)S(1)}, s32[2048]{0:T(1024)}, u32[]{:S(2)}) copy-start(s32[2048]{0:T(1024)} %param.14) | copy-start | bytes 24580
  28.0 44.2 %all-to-all-start.1 = ((bf16[64,16,768]{2,1,0:T(8,128)(2,1)}), bf16[64,16,768]{2,1,0:T(8,128)(2,1)S(1)}, u32[]{:S(2)}, u32[]{:S(2)}) async-start(bf16[64,16,768]{2,1,0:T(8,128)(2,1)} %bitcast.90), calls=%async_computation.1 | async-start | bytes 3145728 | tf_op jit(solution)/shard_map/all_to_all | solution.py:54
  72.1 47.2 %all-to-all-start.2 = ((s32[64,80,1]{1,2,0:T(1,128)}), s32[64,80,1]{1,2,0:T(1,128)S(1)}, u32[]{:S(2)}, u32[]{:S(2)}) async-start(s32[64,80,1]{1,2,0:T(1,128)} %bitcast.20), calls=%async_computation.2 | async-start | bytes 65536 | tf_op jit(solution)/shard_map/all_to_all | solution.py:104
  99.9 4.6 copy-start.1
  104.9 552.3 %copy-start = (bf16[2048,768]{1,0:T(8,128)(2,1)}, bf16[2048,768]{1,0:T(8,128)(2,1)S(1)}, u32[]{:S(2)}) copy-start(bf16[2048,768]{1,0:T(8,128)(2,1)S(1)} %fusion.9) | copy-start | bytes 9437188
  119.3 10.7 %copy-start.6 = (s32[32]{0:T(128)S(1)}, s32[32]{0:T(128)}, u32[]{:S(2)}) copy-start(s32[32]{0:T(128)} %param.11) | copy-start | bytes 388
  119.3 780.4 %all-to-all-start.3 = ((bf16[64,80,768]{2,1,0:T(8,128)(2,1)}), bf16[64,80,768]{2,1,0:T(8,128)(2,1)}, u32[]{:S(2)}, u32[]{:S(2)}) async-start(bf16[64,80,768]{2,1,0:T(8,128)(2,1)} %bitcast.89), calls=%async_computation.3 | async-start | bytes 15728640 | tf_op jit(solution)/shard_map/all_to_all | solution.py:103
  129.9 282.5 %copy-start.3 = (s32[2048]{0:T(1024)S(1)}, s32[2048]{0:T(1024)}, u32[]{:S(2)}) copy-start(s32[2048]{0:T(1024)} %param.12) | copy-start | bytes 24580
  129.9 281.5 %all-reduce.4.cloned.1.call-start = ((), (), s32[]{:S(2)}) async-start(), calls=%async_computation.4 | async-start | bytes 196608 | tf_op jit(solution)/shard_map/psum | solution.py:74
  131.4 522.9 %all-reduce.6.cloned.1.call-start = ((), (), s32[]{:S(2)}) async-start(), calls=%async_computation.5 | async-start | bytes 196608 | tf_op jit(solution)/shard_map/psum | solution.py:39
  415.7 481.4 %all-reduce.8.cloned.1.call-start = ((), (), s32[]{:S(2)}) async-start(), calls=%async_computation.6 | async-start | bytes 196608 | tf_op jit(solution)/shard_map/psum | solution.py:39
Sparse Core Ops, SparseCore 0:
  136.9 274.5 all-reduce.3
  417.5 236.7 all-reduce.5
  660.3 236.7 all-reduce.7
where the time goes:
time: 954 us; the launch traced here: 953 us
  waiting for transfers between devices  772 us (81%)
  blocking collectives  50.8 us (5%)
  matrix products  36.2 us (4%)
  local copies, waits for them, and re-layouts  29.8 us (3%)
  starting transfers between devices  25.9 us (3%)
  other arithmetic  23.3 us (2%)
  between operations  14.1 us (1%)
    psum x2, waiting for transfers between devices, global_total(): return lax.psum(partial_value, ('wide', 'grp'))  476 us
    psum x1, waiting for transfers between devices, shards(): start_cent = rms_rows(lax.psum(seed_part, ('wide', 'grp')))  280 us
    psum x2, blocking collectives, group_total(): return lax.psum(partial_value, 'grp')  31.2 us
    all_to_all x1, blocking collectives, shards(): lax.all_to_all(inst_labels, 'wide', split_axis=0, concat_axis=0, tiled=True)  19.5 us
  transfers between devices with their start and end apart: 6, of which 4 were waited for; matrix products, arithmetic and copies ran while one was open for 7% of the time, Pallas kernels for 0%

commit v1 on v0

v1 whole, which is shorter than its diff:
```python
import jax
import jax.numpy as jnp
from jax import lax
from jax.experimental import pallas as pl
from jax.experimental.pallas import tpu as pltpu
from jax.sharding import PartitionSpec as P

SUB = 16
EPSILON = 1e-06
CONCENTRATION = 16.0
TILE = 256
VMEM_LIMIT = 56 * 1024 * 1024

F32 = jnp.float32
BF16 = jnp.bfloat16


def rms_rows(matrix):
    return matrix * lax.rsqrt(jnp.mean(matrix * matrix, axis=-1, keepdims=True) + EPSILON)


def params():
    return pltpu.CompilerParams(
        dimension_semantics=("arbitrary",), vmem_limit_bytes=VMEM_LIMIT
    )


def whole(shape):
    return pl.BlockSpec(shape, lambda i: (0,) * len(shape))


def counts_kernel(labels_ref, out_ref):
    tile = pl.program_id(0)
    shape = out_ref.shape
    label = tile * shape[0] + lax.broadcasted_iota(jnp.int32, shape, 0)
    total = jnp.zeros(shape, F32)
    for slot in range(labels_ref.shape[0]):
        total = total + jnp.where(labels_ref[slot : slot + 1, :] == label, 1.0, 0.0)
    out_ref[...] = total.astype(BF16)


def label_counts(labels_by_slot, lab_dev):
    slots, rows = labels_by_slot.shape
    return pl.pallas_call(
        counts_kernel,
        grid=(lab_dev // TILE,),
        in_specs=[whole((slots, rows))],
        out_specs=pl.BlockSpec((TILE, rows), lambda i: (i, 0)),
        out_shape=jax.ShapeDtypeStruct((lab_dev, rows), BF16),
        compiler_params=params(),
        cost_estimate=pl.CostEstimate(
            flops=3 * slots * rows * lab_dev, bytes_accessed=2 * rows * lab_dev, transcendentals=0
        ),
        name="label_counts",
    )(labels_by_slot)


def weighted_part(centroids, vectors, ids_row, width):
    scores = lax.dot_general(
        centroids, vectors, (((1,), (1,)), ((), ())), preferred_element_type=F32
    )
    member = ids_row == lax.broadcasted_iota(jnp.int32, scores.shape, 0)
    cosine = jnp.sum(jnp.where(member, scores, 0.0), axis=0, keepdims=True) / width
    weight = jnp.exp(CONCENTRATION * cosine)
    weights = jnp.where(member, weight, 0.0).astype(BF16)
    return jnp.dot(weights, vectors, preferred_element_type=F32)


def label_kernel(counts_ref, rows_ref, start_ref, first_ref, sub_ref, lv_ref, m_ref, s_ref, s_acc):
    tile = pl.program_id(0)

    @pl.when(tile == 0)
    def _():
        m_ref[...] = jnp.zeros_like(m_ref)
        s_acc[...] = jnp.zeros_like(s_acc)

    sums = jnp.dot(counts_ref[...], rows_ref[...], preferred_element_type=F32)
    vectors = rms_rows(sums).astype(BF16)
    lv_ref[...] = vectors
    sub_member = sub_ref[0] == lax.broadcasted_iota(jnp.int32, (s_acc.shape[0], TILE), 0)
    s_acc[...] += jnp.dot(
        jnp.where(sub_member, 1.0, 0.0).astype(BF16), vectors, preferred_element_type=F32
    )
    m_ref[...] += weighted_part(start_ref[...], vectors, first_ref[0], vectors.shape[1])

    @pl.when(tile == pl.num_programs(0) - 1)
    def _():
        s_ref[...] = s_acc[...].astype(BF16)


def label_pass(counts, rows, start, first, sub, sub_total):
    lab_dev, row_total = counts.shape
    width = rows.shape[1]
    coarse = start.shape[0]
    return pl.pallas_call(
        label_kernel,
        grid=(lab_dev // TILE,),
        in_specs=[
            pl.BlockSpec((TILE, row_total), lambda i: (i, 0)),
            whole((row_total, width)),
            whole((coarse, width)),
            pl.BlockSpec((1, 1, TILE), lambda i: (i, 0, 0)),
            pl.BlockSpec((1, 1, TILE), lambda i: (i, 0, 0)),
        ],
        out_specs=[
            pl.BlockSpec((TILE, width), lambda i: (i, 0)),
            whole((coarse, width)),
            whole((sub_total, width)),
        ],
        out_shape=[
            jax.ShapeDtypeStruct((lab_dev, width), BF16),
            jax.ShapeDtypeStruct((coarse, width), F32),
            jax.ShapeDtypeStruct((sub_total, width), BF16),
        ],
        scratch_shapes=[pltpu.VMEM((sub_total, width), F32)],
        compiler_params=params(),
        name="label_pass",
    )(counts, rows, start, first, sub)


def pass_kernel(cent_ref, lv_ref, ids_ref, out_ref, acc):
    tile = pl.program_id(0)

    @pl.when(tile == 0)
    def _():
        acc[...] = jnp.zeros_like(acc)

    vectors = lv_ref[...]
    acc[...] += weighted_part(cent_ref[...], vectors, ids_ref[0], vectors.shape[1])

    @pl.when(tile == pl.num_programs(0) - 1)
    def _():
        out_ref[...] = acc[...].astype(out_ref.dtype)


def weighted_sums(centroids, vectors, ids, kind, name):
    lab_dev, width = vectors.shape
    total = centroids.shape[0]
    return pl.pallas_call(
        pass_kernel,
        grid=(lab_dev // TILE,),
        in_specs=[
            whole((total, width)),
            pl.BlockSpec((TILE, width), lambda i: (i, 0)),
            pl.BlockSpec((1, 1, TILE), lambda i: (i, 0, 0)),
        ],
        out_specs=whole((total, width)),
        out_shape=jax.ShapeDtypeStruct((total, width), kind),
        scratch_shapes=[pltpu.VMEM((total, width), F32)],
        compiler_params=params(),
        cost_estimate=pl.CostEstimate(
            flops=4 * total * lab_dev * width, bytes_accessed=2 * lab_dev * width, transcendentals=0
        ),
        name=name,
    )(centroids, vectors, ids)


def to_all(blocks):
    return lax.all_to_all(blocks, "wide", split_axis=0, concat_axis=0, tiled=True)


def spread(piece, n_wide):
    return jnp.broadcast_to(piece[None], (n_wide,) + piece.shape)


def grp_shift(value, step):
    n = lax.axis_size("grp")
    return lax.ppermute(value, "grp", [(i, (i + step) % n) for i in range(n)])


def grp_sum(value):
    others = [grp_shift(value, step) for step in range(1, lax.axis_size("grp"))]
    total = value.astype(F32)
    for other in others:
        total = total + other.astype(F32)
    return total


def grp_gather(value):
    n = lax.axis_size("grp")
    pieces = [value] + [grp_shift(value, n - step) for step in range(1, n)]
    return jnp.roll(jnp.stack(pieces), lax.axis_index("grp"), axis=0)


def grp_scatter(blocks):
    n = lax.axis_size("grp")
    me = lax.axis_index("grp")
    total = lax.dynamic_index_in_dim(blocks, me, 0, keepdims=False).astype(F32)
    for step in range(1, n):
        block = lax.dynamic_index_in_dim(blocks, lax.rem(me + step, n), 0, keepdims=False)
        total = total + grp_shift(block, step).astype(F32)
    return total


def halves(value):
    high = lax.reduce_precision(value, 8, 7)
    return high.astype(BF16), (value - high).astype(BF16)


def shards(inst_rows, inst_labels, seed_labels, coarse_first, coarse_second, sub_assign, group_map):
    n_wide = lax.axis_size("wide")
    n_grp = lax.axis_size("grp")
    lab_dev = coarse_first.shape[0]
    row_total, width = inst_rows.shape
    slots = inst_labels.shape[1]
    coarse = group_map.shape[0]
    per_dest = row_total // n_wide
    quarter = SUB // n_grp
    piece = coarse * width // n_wide
    me_grp = lax.axis_index("grp")
    lanes = 128

    block_base = (jnp.arange(row_total, dtype=jnp.int32) // per_dest * n_grp + me_grp) * lab_dev
    wanted = seed_labels[None, :] - block_base[:, None]
    seed_counts = jnp.zeros((row_total, coarse), F32)
    for slot in range(slots):
        seed_counts = seed_counts + (inst_labels[:, slot][:, None] == wanted)
    seed_part = lax.dot_general(
        seed_counts.astype(BF16), inst_rows, (((0,), (0,)), ((), ())), preferred_element_type=F32
    )
    by_slot = inst_labels.reshape(n_wide, per_dest, slots).transpose(0, 2, 1)
    sent = jnp.concatenate(
        [
            seed_part.reshape(n_wide, piece),
            by_slot.reshape(n_wide, slots * per_dest).astype(F32),
        ],
        axis=1,
    )
    early = to_all(sent)
    rows_in, early = lax.optimization_barrier((inst_rows, early))
    received = to_all(rows_in.reshape(n_wide, per_dest, width)).reshape(row_total, width)
    labels_by_slot = (
        early[:, piece:]
        .astype(jnp.int32)
        .reshape(n_wide, slots, per_dest)
        .transpose(1, 0, 2)
        .reshape(slots, row_total)
    )
    counts = label_counts(labels_by_slot, lab_dev)
    seed_piece = grp_sum(jnp.sum(early[:, :piece], axis=0))

    n_x, n_z, n_c = 4, 8, 2
    me_wide = lax.axis_index("wide")
    place = (me_wide // (n_z * n_c), me_wide // n_c % n_z, me_wide % n_c)
    gathered = seed_piece[None]
    for size, unit, here in ((n_c, 1, place[2]), (n_x, n_z * n_c, place[0]), (n_z, n_c, place[1])):
        pieces = [gathered]
        for step in range(1, size):
            pairs = []
            for source in range(n_wide):
                digit = source // unit % size
                pairs.append((source, source + ((digit - step) % size - digit) * unit))
            pieces.append(lax.ppermute(gathered, "wide", pairs))
        gathered = jnp.roll(jnp.stack(pieces), here, axis=0)
    seed_sums = gathered.reshape(n_z, n_x, n_c, piece).transpose(1, 0, 2, 3).reshape(coarse, width)
    start = rms_rows(lax.reduce_precision(rms_rows(seed_sums), 8, 7)).astype(BF16)

    second = coarse_second.reshape(lab_dev)
    sub_total = coarse * SUB
    sub_ids = (sub_assign // quarter) * (coarse * quarter) + second * quarter + sub_assign % quarter
    tiles = lab_dev // TILE
    first_ids = coarse_first.reshape(tiles, 1, TILE)
    second_ids = second.reshape(tiles, 1, TILE)
    sub_ids = sub_ids.reshape(tiles, 1, TILE)
    label_vectors, m_one, sub_part = label_pass(
        counts, received, start, first_ids, sub_ids, sub_total
    )

    m_one = grp_sum(m_one.astype(BF16))
    sub_mine = grp_scatter(sub_part.reshape(n_grp, coarse * quarter, width))
    chunk_m, chunk_s = piece // lanes, 2 * width // lanes
    pad = (-(chunk_m + chunk_s)) % 16
    sent = jnp.concatenate(
        [
            sub_mine.astype(BF16).reshape(n_wide, chunk_s, lanes),
            m_one.astype(BF16).reshape(n_wide, chunk_m, lanes),
            jnp.zeros((n_wide, pad, lanes), BF16),
        ],
        axis=1,
    )
    got = jnp.sum(to_all(sent).astype(F32), axis=0)

    sub_rows = rms_rows(got[:chunk_s].reshape(2, width)).astype(BF16)
    sent = jnp.concatenate(
        [
            sub_rows.reshape(chunk_s, lanes),
            got[chunk_s : chunk_s + chunk_m].astype(BF16),
            jnp.zeros((pad, lanes), BF16),
        ],
        axis=0,
    )
    got = to_all(spread(sent, n_wide))
    first = rms_rows(
        got[:, chunk_s : chunk_s + chunk_m].reshape(coarse, width).astype(F32)
    ).astype(BF16)
    sub_quarter = got[:, :chunk_s].reshape(coarse * quarter, width)

    m_two = weighted_sums(first, label_vectors, second_ids, F32, "second_pass")
    m_two = grp_sum(m_two)
    two_piece = jnp.sum(to_all(m_two.reshape(n_wide, piece)), axis=0)

    sub_start = grp_gather(sub_quarter).reshape(sub_total, width)
    w_sub = weighted_sums(sub_start, label_vectors, sub_ids, BF16, "sub_pass")
    w_mine = grp_scatter(w_sub.reshape(n_grp, coarse * quarter, width)).astype(BF16)
    host = (
        group_map[None, :] == lax.broadcasted_iota(jnp.int32, (n_wide, coarse), 0)
    ).astype(BF16)
    to_hosts = jnp.dot(
        host, w_mine.reshape(coarse, quarter * width), preferred_element_type=F32
    ).astype(BF16)
    chunk_w = quarter * width // lanes
    high, low = halves(two_piece.reshape(chunk_m, lanes))
    pad = (-(2 * chunk_m + chunk_w)) % 16
    sent = jnp.concatenate(
        [
            to_hosts.reshape(n_wide, chunk_w, lanes),
            spread(jnp.concatenate([high, low, jnp.zeros((pad, lanes), BF16)]), n_wide),
        ],
        axis=1,
    )
    got = to_all(sent)
    last = got[:, chunk_w : chunk_w + 2 * chunk_m].astype(F32)
    coarse_centroids = rms_rows(
        (last[:, :chunk_m] + last[:, chunk_m:]).reshape(coarse, width)
    )
    hosted = rms_rows(
        jnp.sum(got[:, :chunk_w].astype(F32), axis=0).reshape(quarter, width)
    )
    sub_centroids = grp_gather(hosted).reshape(1, SUB, width)
    return label_vectors, coarse_centroids, sub_centroids


def solution(mesh):
    in_specs = (
        P(("wide", "grp"), None),
        P(("wide", "grp"), None),
        P(),
        P(("wide", "grp")),
        P(("wide", "grp"), None),
        P(("wide", "grp")),
        P(),
    )
    out_specs = (P(("wide", "grp"), None), P(), P("wide", None, None))
    return jax.shard_map(shards, mesh=mesh, in_specs=in_specs, out_specs=out_specs, check_vma=False)
```

time: 954 us -> 266 us (0.28)
  waiting for transfers between devices: 772 us -> 52.3 us
  starting transfers between devices: 25.9 us -> 92.3 us
  Pallas kernels: 0 us -> 42 us
  matrix products: 36.2 us -> 2.1 us
  local copies, waits for them, and re-layouts: 29.8 us -> 12.2 us
  between operations: 14.1 us -> 1.36 us
  other arithmetic: 23.3 us -> 11.6 us
    psum x3 -> x0, waiting for transfers between devices: 756 us -> none  [the longest x2 476 us: global_total(): return lax.psum(partial_value, ('wide', 'grp'))]
    ppermute x0 -> x32, starting transfers between devices: none -> 60.9 us  [the longest x21 41.6 us: grp_shift(): return lax.ppermute(value, 'grp', [(i, (i + step) % n) for i in range(n)])]
    pallas_call x0 -> x4, Pallas kernels: none -> 42 us  [the longest x2 18.6 us: weighted_sums(): pl.pallas_call(pass_kernel, grid=(lab_dev // TILE,), in_specs=[whole((tot...]
    dot_general x12 -> x2, matrix products: 36.2 us -> 2.1 us  [the longest x1 1.86 us: shards(): lax.dot_general(seed_counts.astype(BF16), inst_rows, (((0,), (0,)), ((),...]
    ppermute x0 -> x32, waiting for transfers between devices: none -> 32.7 us  [the longest x21 18.3 us: grp_shift(): return lax.ppermute(value, 'grp', [(i, (i + step) % n) for i in range(n)])]
    psum x2 -> x0, blocking collectives: 31.2 us -> none  [group_total(): return lax.psum(partial_value, 'grp')]
    all_to_all x1 -> x2, blocking collectives: 19.5 us -> 47.3 us  [to_all(): lax.all_to_all(blocks, 'wide', split_axis=0, concat_axis=0, tiled=True)]
    scatter x2 -> x0, local copies, waits for them, and re-layouts: 22.4 us -> none  [the longest x1 14.4 us: shards(): buffer = jnp.zeros((n_wide * host_slots * capacity, feature_width), jnp.b...]
  transfers between devices with their start and end apart: 6 -> 36, of which waited for: 4 -> 17; matrix products, arithmetic and copies ran while one was open for 7% -> 5% of each run, Pallas kernels for 0% -> 10%
where the time goes in v1:
time: 266 us; the launch traced here: 261 us
  starting transfers between devices  92.3 us (35%)
  waiting for transfers between devices  52.3 us (20%)
  blocking collectives  47.3 us (18%)
  Pallas kernels  42 us (16%)
  local copies, waits for them, and re-layouts  12.2 us (5%)
  other arithmetic  11.6 us (4%)
    all_to_all x2, blocking collectives, to_all(): lax.all_to_all(blocks, 'wide', split_axis=0, concat_axis=0, tiled=True)  47.3 us
    ppermute x21, starting transfers between devices, grp_shift(): return lax.ppermute(value, 'grp', [(i, (i + step) % n) for i in range(n)])  41.6 us
    all_to_all x4, starting transfers between devices, to_all(): lax.all_to_all(blocks, 'wide', split_axis=0, concat_axis=0, tiled=True)  31.4 us
    all_to_all x4, waiting for transfers between devices, to_all(): lax.all_to_all(blocks, 'wide', split_axis=0, concat_axis=0, tiled=True)  19.7 us
    ppermute x11, starting transfers between devices, shards(): pieces.append(lax.ppermute(gathered, 'wide', pairs))  19.3 us
    pallas_call x2, Pallas kernels, weighted_sums(): pl.pallas_call(pass_kernel, grid=(lab_dev // TILE,), in_specs=[whole((tot...  18.6 us
    ppermute x21, waiting for transfers between devices, grp_shift(): return lax.ppermute(value, 'grp', [(i, (i + step) % n) for i in range(n)])  18.3 us
    pallas_call x1, Pallas kernels, label_pass(): pl.pallas_call(label_kernel, grid=(lab_dev // TILE,), in_specs=[pl.BlockS...  15.2 us
  transfers between devices with their start and end apart: 36, of which 17 were waited for; matrix products, arithmetic and copies ran while one was open for 5% of the time, Pallas kernels for 10%

profile of v1, /device:TPU:6, one launch (start us, length us, event | category | flops | bytes accessed | tf_op | source)
XLA Modules:
  0.0 261.2 jit_solution(12520781150118215483)
XLA Ops:
  5.5 12.2 %all-to-all-start = ((f32[64,1,512]{2,1,0:T(1,128)}), f32[64,1,512]{2,1,0:T(1,128)S(1)}, u32[]{:S(2)}, u32[]{:S(2)}) async-start(f32[64,1,512]{2,1,0:T(1,128)} %all_to_all.26), calls=%async_computation | async-start | bytes 262144 | tf_op jit(solution)/shard_map/all_to_all | solution.py:159
  18.3 8.2 %all-to-all-done = f32[64,1,512]{2,1,0:T(1,128)S(1)} async-done(((f32[64,1,512]{2,1,0:T(1,128)}), f32[64,1,512]{2,1,0:T(1,128)S(1)}, u32[]{:S(2)}, u32[]{:S(2)}) %all-to-all-start) | async-done | bytes 131104 | tf_op jit(solution)/shard_map/all_to_all | solution.py:159
  28.5 2.9 %collective-permute-start.1 = (f32[384]{0:T(512)S(1)}, f32[384]{0:T(512)S(1)}, u32[]{:S(2)}, u32[]{:S(2)}) collective-permute-start(f32[384]{0:T(512)S(1)} %slice_reduce_fusion), channel_id=1, source_target_pairs={{0,2},{1,3},{2,0},{3,1},{4,6},{5,7},{6,4},{7,5},{8,10},{9,11},{10,... | collective-permute-start | bytes 4616 | tf_op jit(solution)/shard_map/ppermute | solution.py:168
  32.7 6.4 %all-to-all-start.1 = ((bf16[64,16,768]{2,1,0:T(8,128)(2,1)}), bf16[64,16,768]{2,1,0:T(8,128)(2,1)S(1)}, u32[]{:S(2)}, u32[]{:S(2)}) async-start(bf16[64,16,768]{2,1,0:T(8,128)(2,1)} %bitcast.13), calls=%async_computation.1 | async-start | bytes 3145728 | tf_op jit(solution)/shard_map/all_to_all | solution.py:159
  46.5 2.8 %collective-permute-start.7 = (f32[4,2,1,384]{3,2,1,0:T(1,128)S(1)}, f32[4,2,1,384]{3,2,1,0:T(1,128)S(1)}, u32[]{:S(2)}, u32[]{:S(2)}) collective-permute-start(f32[4,2,1,384]{3,2,1,0:T(1,128)S(1)} %constant_dynamic-slice_fusion.3), channel_id=1, source_target_pairs={{0,56},{4,60},{8,0},{12,4},{16,8},{20,12},{24,16},{28,20},{32,24},... | collective-permute-start | bytes 36872 | tf_op jit(solution)/shard_map/ppermute | solution.py:253
  52.6 8.2 %label_counts.1.counts_ref = bf16[2048,1024]{1,0:T(8,128)(2,1)} custom-call(s32[8,1024]{1,0:T(8,128)} %reshape.220.labels_ref), custom_call_target="tpu_custom_call" | custom-call | flops 50331648 | bytes 4194304 | tf_op jit(solution)/shard_map/label_counts/pallas_call | solution.py:44
  62.3 3.6 %collective-permute-start.10 = (f32[4,2,1,384]{3,2,1,0:T(1,128)S(1)}, f32[4,2,1,384]{3,2,1,0:T(1,128)S(1)}, u32[]{:S(2)}, u32[]{:S(2)}) collective-permute-start(f32[4,2,1,384]{3,2,1,0:T(1,128)S(1)} %constant_dynamic-slice_fusion.3), channel_id=1, source_target_pairs={{0,32},{4,36},{8,40},{12,44},{16,48},{20,52},{24,56},{28,60},{32,0... | collective-permute-start | bytes 36872 | tf_op jit(solution)/shard_map/ppermute | solution.py:253
  66.3 10.0 %collective-permute-done.7 = f32[4,2,1,384]{3,2,1,0:T(1,128)S(1)} collective-permute-done((f32[4,2,1,384]{3,2,1,0:T(1,128)S(1)}, f32[4,2,1,384]{3,2,1,0:T(1,128)S(1)}, u32[]{:S(2)}, u32[]{:S(2)}) %collective-permute-start.7) | collective-permute-done | bytes 12320 | tf_op jit(solution)/shard_map/ppermute | solution.py:253
  77.0 3.8 %collective-permute-start.13 = (f32[4,2,1,384]{3,2,1,0:T(1,128)S(1)}, f32[4,2,1,384]{3,2,1,0:T(1,128)S(1)}, u32[]{:S(2)}, u32[]{:S(2)}) collective-permute-start(f32[4,2,1,384]{3,2,1,0:T(1,128)S(1)} %constant_dynamic-slice_fusion.3), channel_id=1, source_target_pairs={{0,8},{4,12},{8,16},{12,20},{16,24},{20,28},{24,32},{28,36},{32,40... | collective-permute-start | bytes 36872 | tf_op jit(solution)/shard_map/ppermute | solution.py:253
  84.9 15.2 %label_pass.1 = (bf16[2048,768]{1,0:T(8,128)(2,1)}, f32[32,768]{1,0:T(8,128)}, bf16[512,768]{1,0:T(8,128)(2,1)}) custom-call(bf16[2048,1024]{1,0:T(8,128)(2,1)} %label_counts.1.counts_ref, bf16[1024,768]{1,0:T(8,128)(2,1)} %bitcast.127, bf16[32,768]{1,0:T(8,128)(2,1)} %multiply_convert_fusion.1.start_ref, s32[8,1,256]{2,1,0:T(1,128)} %bitcast.168, ...), custom_call_target="tpu_custom_call" | custom-call | tf_op jit(solution)/shard_map/label_pass/pallas_call | solution.py:95
  112.0 3.9 %collective-permute-done.14 = bf16[128,768]{1,0:T(8,128)(2,1)S(1)} collective-permute-done((bf16[128,768]{1,0:T(8,128)(2,1)S(1)}, bf16[128,768]{1,0:T(8,128)(2,1)S(1)}, u32[]{:S(2)}, u32[]{:S(2)}) %collective-permute-start.14) | collective-permute-done | bytes 196640 | tf_op jit(solution)/shard_map/ppermute | solution.py:168
  117.5 20.5 %all_to_all.42 = bf16[64,16,128]{2,1,0:T(8,128)(2,1)S(1)} all-to-all(bf16[64,16,128]{2,1,0:T(8,128)(2,1)S(1)} %maximum_maximum_fusion), channel_id=1, replica_groups=mesh['wide'=64,'grp'=4] {'wide'}, dimensions={0} | all-to-all | bytes 524288 | tf_op jit(solution)/shard_map/all_to_all | solution.py:159
  139.5 6.5 %all-to-all-start.3 = ((bf16[64,16,128]{2,1,0:T(8,128)(2,1)}), bf16[64,16,128]{2,1,0:T(8,128)(2,1)S(1)}, u32[]{:S(2)}, u32[]{:S(2)}) async-start(bf16[64,16,128]{2,1,0:T(8,128)(2,1)} %broadcast_in_dim.15), calls=%async_computation.3 | async-start | bytes 524288 | tf_op jit(solution)/shard_map/all_to_all | solution.py:159
  146.1 11.5 %all-to-all-done.3 = bf16[64,16,128]{2,1,0:T(8,128)(2,1)S(1)} async-done(((bf16[64,16,128]{2,1,0:T(8,128)(2,1)}), bf16[64,16,128]{2,1,0:T(8,128)(2,1)S(1)}, u32[]{:S(2)}, u32[]{:S(2)}) %all-to-all-start.3) | async-done | bytes 262176 | tf_op jit(solution)/shard_map/all_to_all | solution.py:159
  157.9 2.8 %collective-permute-start.20 = (bf16[128,768]{1,0:T(8,128)(2,1)S(1)}, bf16[128,768]{1,0:T(8,128)(2,1)S(1)}, u32[]{:S(2)}, u32[]{:S(2)}) collective-permute-start(bf16[128,768]{1,0:T(8,128)(2,1)S(1)} %reshape.230), channel_id=1, source_target_pairs={{0,3},{1,0},{2,1},{3,2},{4,7},{5,4},{6,5},{7,6},{8,11},{9,8},{10,9... | collective-permute-start | bytes 589832 | tf_op jit(solution)/shard_map/ppermute | solution.py:168
  160.7 9.7 %collective-permute-start.21 = (bf16[128,768]{1,0:T(8,128)(2,1)S(1)}, bf16[128,768]{1,0:T(8,128)(2,1)S(1)}, u32[]{:S(2)}, u32[]{:S(2)}) collective-permute-start(bf16[128,768]{1,0:T(8,128)(2,1)S(1)} %reshape.230), channel_id=1, source_target_pairs={{0,2},{1,3},{2,0},{3,1},{4,6},{5,7},{6,4},{7,5},{8,10},{9,11},{10,... | collective-permute-start | bytes 589832 | tf_op jit(solution)/shard_map/ppermute | solution.py:168
  172.0 7.1 %second_pass.1 = f32[32,768]{1,0:T(8,128)} custom-call(bf16[32,768]{1,0:T(8,128)(2,1)} %multiply_convert_fusion.cent_ref, bf16[2048,768]{1,0:T(8,128)(2,1)} %get-tuple-element.5.lv_ref, s32[8,1,256]{2,1,0:T(1,128)} %bitcast.158), custom_call_target="tpu_custom_call" | custom-call | flops 201326592 | bytes 3145728 | tf_op jit(solution)/shard_map/second_pass/pallas_call | solution.py:139
  181.7 2.6 %collective-permute-start.28 = (f32[32,768]{1,0:T(8,128)}, f32[32,768]{1,0:T(8,128)S(1)}, u32[]{:S(2)}, u32[]{:S(2)}) collective-permute-start(f32[32,768]{1,0:T(8,128)} %second_pass.1), channel_id=1, source_target_pairs={{0,3},{1,0},{2,1},{3,2},{4,7},{5,4},{6,5},{7,6},{8,11},{9,8},{10,9... | collective-permute-start | bytes 294920 | tf_op jit(solution)/shard_map/ppermute | solution.py:168
  189.1 6.4 %all-to-all-start.4 = ((f32[64,1,384]{2,1,0:T(1,128)}), f32[64,1,384]{2,1,0:T(1,128)S(1)}, u32[]{:S(2)}, u32[]{:S(2)}) async-start(f32[64,1,384]{2,1,0:T(1,128)} %all_to_all.35), calls=%async_computation.4 | async-start | bytes 196608 | tf_op jit(solution)/shard_map/all_to_all | solution.py:159
  196.6 11.5 %sub_pass.1 = bf16[512,768]{1,0:T(8,128)(2,1)} custom-call(bf16[512,768]{1,0:T(8,128)(2,1)} %bitcast.139, bf16[2048,768]{1,0:T(8,128)(2,1)} %get-tuple-element.5.lv_ref, s32[8,1,256]{2,1,0:T(1,128)} %bitcast.157), custom_call_target="tpu_custom_call" | custom-call | flops 3221225472 | bytes 3145728 | tf_op jit(solution)/shard_map/sub_pass/pallas_call | solution.py:139
  211.2 2.8 %collective-permute-start.24 = (bf16[128,768]{1,0:T(8,128)(2,1)S(1)}, bf16[128,768]{1,0:T(8,128)(2,1)S(1)}, u32[]{:S(2)}, u32[]{:S(2)}) collective-permute-start(bf16[128,768]{1,0:T(8,128)(2,1)S(1)} %get-tuple-element.21), channel_id=1, source_target_pairs={{0,2},{1,3},{2,0},{3,1},{4,6},{5,7},{6,4},{7,5},{8,10},{9,11},{10,... | collective-permute-start | bytes 589832 | tf_op jit(solution)/shard_map/ppermute | solution.py:168
  214.9 2.8 %collective-permute-done.23 = bf16[128,768]{1,0:T(8,128)(2,1)S(1)} collective-permute-done((bf16[128,768]{1,0:T(8,128)(2,1)S(1)}, bf16[128,768]{1,0:T(8,128)(2,1)S(1)}, u32[]{:S(2)}, u32[]{:S(2)}) %collective-permute-start.23) | collective-permute-done | bytes 196640 | tf_op jit(solution)/shard_map/ppermute | solution.py:168
  217.7 5.4 %collective-permute-done.24 = bf16[128,768]{1,0:T(8,128)(2,1)S(1)} collective-permute-done((bf16[128,768]{1,0:T(8,128)(2,1)S(1)}, bf16[128,768]{1,0:T(8,128)(2,1)S(1)}, u32[]{:S(2)}, u32[]{:S(2)}) %collective-permute-start.24) | collective-permute-done | bytes 196640 | tf_op jit(solution)/shard_map/ppermute | solution.py:168
  224.7 26.8 %all_to_all.43 = bf16[64,32,128]{2,1,0:T(8,128)(2,1)S(1)} all-to-all(bf16[64,32,128]{2,1,0:T(8,128)(2,1)S(1)} %pad_maximum_fusion), channel_id=1, replica_groups=mesh['wide'=64,'grp'=4] {'wide'}, dimensions={0} | all-to-all | bytes 1048576 | tf_op jit(solution)/shard_map/all_to_all | solution.py:159
  (176 shorter events, 66.4 us)
Async XLA Ops:
  5.5 21.0 %all-to-all-start = ((f32[64,1,512]{2,1,0:T(1,128)}), f32[64,1,512]{2,1,0:T(1,128)S(1)}, u32[]{:S(2)}, u32[]{:S(2)}) async-start(f32[64,1,512]{2,1,0:T(1,128)} %all_to_all.26), calls=%async_computation | async-start | bytes 262144 | tf_op jit(solution)/shard_map/all_to_all | solution.py:159
  26.8 12.3 %collective-permute-start = (f32[384]{0:T(512)S(1)}, f32[384]{0:T(512)S(1)}, u32[]{:S(2)}, u32[]{:S(2)}) collective-permute-start(f32[384]{0:T(512)S(1)} %slice_reduce_fusion), channel_id=1, source_target_pairs={{0,1},{1,2},{2,3},{3,0},{4,5},{5,6},{6,7},{7,4},{8,9},{9,10},{10,1... | collective-permute-start | bytes 4616 | tf_op jit(solution)/shard_map/ppermute | solution.py:168
  28.5 10.6 %collective-permute-start.1 = (f32[384]{0:T(512)S(1)}, f32[384]{0:T(512)S(1)}, u32[]{:S(2)}, u32[]{:S(2)}) collective-permute-start(f32[384]{0:T(512)S(1)} %slice_reduce_fusion), channel_id=1, source_target_pairs={{0,2},{1,3},{2,0},{3,1},{4,6},{5,7},{6,4},{7,5},{8,10},{9,11},{10,... | collective-permute-start | bytes 4616 | tf_op jit(solution)/shard_map/ppermute | solution.py:168
  31.4 7.8 %collective-permute-start.2 = (f32[384]{0:T(512)S(1)}, f32[384]{0:T(512)S(1)}, u32[]{:S(2)}, u32[]{:S(2)}) collective-permute-start(f32[384]{0:T(512)S(1)} %slice_reduce_fusion), channel_id=1, source_target_pairs={{0,3},{1,0},{2,1},{3,2},{4,7},{5,4},{6,5},{7,6},{8,11},{9,8},{10,9... | collective-permute-start | bytes 4616 | tf_op jit(solution)/shard_map/ppermute | solution.py:168
  32.7 51.0 %all-to-all-start.1 = ((bf16[64,16,768]{2,1,0:T(8,128)(2,1)}), bf16[64,16,768]{2,1,0:T(8,128)(2,1)S(1)}, u32[]{:S(2)}, u32[]{:S(2)}) async-start(bf16[64,16,768]{2,1,0:T(8,128)(2,1)} %bitcast.13), calls=%async_computation.1 | async-start | bytes 3145728 | tf_op jit(solution)/shard_map/all_to_all | solution.py:159
  46.5 29.8 %collective-permute-start.7 = (f32[4,2,1,384]{3,2,1,0:T(1,128)S(1)}, f32[4,2,1,384]{3,2,1,0:T(1,128)S(1)}, u32[]{:S(2)}, u32[]{:S(2)}) collective-permute-start(f32[4,2,1,384]{3,2,1,0:T(1,128)S(1)} %constant_dynamic-slice_fusion.3), channel_id=1, source_target_pairs={{0,56},{4,60},{8,0},{12,4},{16,8},{20,12},{24,16},{28,20},{32,24},... | collective-permute-start | bytes 36872 | tf_op jit(solution)/shard_map/ppermute | solution.py:253
  49.4 27.7 %collective-permute-start.8 = (f32[4,2,1,384]{3,2,1,0:T(1,128)S(1)}, f32[4,2,1,384]{3,2,1,0:T(1,128)S(1)}, u32[]{:S(2)}, u32[]{:S(2)}) collective-permute-start(f32[4,2,1,384]{3,2,1,0:T(1,128)S(1)} %constant_dynamic-slice_fusion.3), channel_id=1, source_target_pairs={{0,48},{4,52},{8,56},{12,60},{16,0},{20,4},{24,8},{28,12},{32,16},... | collective-permute-start | bytes 36872 | tf_op jit(solution)/shard_map/ppermute | solution.py:253
  60.8 20.0 %collective-permute-start.9 = (f32[4,2,1,384]{3,2,1,0:T(1,128)S(1)}, f32[4,2,1,384]{3,2,1,0:T(1,128)S(1)}, u32[]{:S(2)}, u32[]{:S(2)}) collective-permute-start(f32[4,2,1,384]{3,2,1,0:T(1,128)S(1)} %constant_dynamic-slice_fusion.3), channel_id=1, source_target_pairs={{0,40},{4,44},{8,48},{12,52},{16,56},{20,60},{24,0},{28,4},{32,8},... | collective-permute-start | bytes 36872 | tf_op jit(solution)/shard_map/ppermute | solution.py:253
  62.3 18.5 %collective-permute-start.10 = (f32[4,2,1,384]{3,2,1,0:T(1,128)S(1)}, f32[4,2,1,384]{3,2,1,0:T(1,128)S(1)}, u32[]{:S(2)}, u32[]{:S(2)}) collective-permute-start(f32[4,2,1,384]{3,2,1,0:T(1,128)S(1)} %constant_dynamic-slice_fusion.3), channel_id=1, source_target_pairs={{0,32},{4,36},{8,40},{12,44},{16,48},{20,52},{24,56},{28,60},{32,0... | collective-permute-start | bytes 36872 | tf_op jit(solution)/shard_map/ppermute | solution.py:253
  65.9 14.9 %collective-permute-start.11 = (f32[4,2,1,384]{3,2,1,0:T(1,128)S(1)}, f32[4,2,1,384]{3,2,1,0:T(1,128)S(1)}, u32[]{:S(2)}, u32[]{:S(2)}) collective-permute-start(f32[4,2,1,384]{3,2,1,0:T(1,128)S(1)} %constant_dynamic-slice_fusion.3), channel_id=1, source_target_pairs={{0,24},{4,28},{8,32},{12,36},{16,40},{20,44},{24,48},{28,52},{32,5... | collective-permute-start | bytes 36872 | tf_op jit(solution)/shard_map/ppermute | solution.py:253
  101.7 9.3 %collective-permute-start.18 = (bf16[32,768]{1,0:T(8,128)(2,1)S(1)}, bf16[32,768]{1,0:T(8,128)(2,1)S(1)}, u32[]{:S(2)}, u32[]{:S(2)}) collective-permute-start(bf16[32,768]{1,0:T(8,128)(2,1)S(1)} %convert_element_type.156), channel_id=1, source_target_pairs={{0,2},{1,3},{2,0},{3,1},{4,6},{5,7},{6,4},{7,5},{8,10},{9,11},{10,... | collective-permute-start | bytes 147464 | tf_op jit(solution)/shard_map/ppermute | solution.py:168
  102.4 8.6 %collective-permute-start.19 = (bf16[32,768]{1,0:T(8,128)(2,1)S(1)}, bf16[32,768]{1,0:T(8,128)(2,1)S(1)}, u32[]{:S(2)}, u32[]{:S(2)}) collective-permute-start(bf16[32,768]{1,0:T(8,128)(2,1)S(1)} %convert_element_type.156), channel_id=1, source_target_pairs={{0,3},{1,0},{2,1},{3,2},{4,7},{5,4},{6,5},{7,6},{8,11},{9,8},{10,9... | collective-permute-start | bytes 147464 | tf_op jit(solution)/shard_map/ppermute | solution.py:168
  105.6 10.3 %collective-permute-start.14 = (bf16[128,768]{1,0:T(8,128)(2,1)S(1)}, bf16[128,768]{1,0:T(8,128)(2,1)S(1)}, u32[]{:S(2)}, u32[]{:S(2)}) collective-permute-start(bf16[128,768]{1,0:T(8,128)(2,1)S(1)} %get-tuple-element.22), channel_id=1, source_target_pairs={{0,1},{1,2},{2,3},{3,0},{4,5},{5,6},{6,7},{7,4},{8,9},{9,10},{10,1... | collective-permute-start | bytes 589832 | tf_op jit(solution)/shard_map/ppermute | solution.py:168
  106.3 9.6 %collective-permute-start.15 = (bf16[128,768]{1,0:T(8,128)(2,1)S(1)}, bf16[128,768]{1,0:T(8,128)(2,1)S(1)}, u32[]{:S(2)}, u32[]{:S(2)}) collective-permute-start(bf16[128,768]{1,0:T(8,128)(2,1)S(1)} %get-tuple-element.24), channel_id=1, source_target_pairs={{0,2},{1,3},{2,0},{3,1},{4,6},{5,7},{6,4},{7,5},{8,10},{9,11},{10,... | collective-permute-start | bytes 589832 | tf_op jit(solution)/shard_map/ppermute | solution.py:168
  108.5 7.6 %collective-permute-start.16 = (bf16[128,768]{1,0:T(8,128)(2,1)S(1)}, bf16[128,768]{1,0:T(8,128)(2,1)S(1)}, u32[]{:S(2)}, u32[]{:S(2)}) collective-permute-start(bf16[128,768]{1,0:T(8,128)(2,1)S(1)} %get-tuple-element.23), channel_id=1, source_target_pairs={{0,3},{1,0},{2,1},{3,2},{4,7},{5,4},{6,5},{7,6},{8,11},{9,8},{10,9... | collective-permute-start | bytes 589832 | tf_op jit(solution)/shard_map/ppermute | solution.py:168
  139.5 18.0 %all-to-all-start.3 = ((bf16[64,16,128]{2,1,0:T(8,128)(2,1)}), bf16[64,16,128]{2,1,0:T(8,128)(2,1)S(1)}, u32[]{:S(2)}, u32[]{:S(2)}) async-start(bf16[64,16,128]{2,1,0:T(8,128)(2,1)} %broadcast_in_dim.15), calls=%async_computation.3 | async-start | bytes 524288 | tf_op jit(solution)/shard_map/all_to_all | solution.py:159
  157.9 37.6 %collective-permute-start.20 = (bf16[128,768]{1,0:T(8,128)(2,1)S(1)}, bf16[128,768]{1,0:T(8,128)(2,1)S(1)}, u32[]{:S(2)}, u32[]{:S(2)}) collective-permute-start(bf16[128,768]{1,0:T(8,128)(2,1)S(1)} %reshape.230), channel_id=1, source_target_pairs={{0,3},{1,0},{2,1},{3,2},{4,7},{5,4},{6,5},{7,6},{8,11},{9,8},{10,9... | collective-permute-start | bytes 589832 | tf_op jit(solution)/shard_map/ppermute | solution.py:168
  160.7 34.8 %collective-permute-start.21 = (bf16[128,768]{1,0:T(8,128)(2,1)S(1)}, bf16[128,768]{1,0:T(8,128)(2,1)S(1)}, u32[]{:S(2)}, u32[]{:S(2)}) collective-permute-start(bf16[128,768]{1,0:T(8,128)(2,1)S(1)} %reshape.230), channel_id=1, source_target_pairs={{0,2},{1,3},{2,0},{3,1},{4,6},{5,7},{6,4},{7,5},{8,10},{9,11},{10,... | collective-permute-start | bytes 589832 | tf_op jit(solution)/shard_map/ppermute | solution.py:168
  179.4 7.8 %collective-permute-start.27 = (f32[32,768]{1,0:T(8,128)}, f32[32,768]{1,0:T(8,128)S(1)}, u32[]{:S(2)}, u32[]{:S(2)}) collective-permute-start(f32[32,768]{1,0:T(8,128)} %second_pass.1), channel_id=1, source_target_pairs={{0,2},{1,3},{2,0},{3,1},{4,6},{5,7},{6,4},{7,5},{8,10},{9,11},{10,... | collective-permute-start | bytes 294920 | tf_op jit(solution)/shard_map/ppermute | solution.py:168
  186.5 9.0 %collective-permute-start.22 = (bf16[128,768]{1,0:T(8,128)(2,1)S(1)}, bf16[128,768]{1,0:T(8,128)(2,1)S(1)}, u32[]{:S(2)}, u32[]{:S(2)}) collective-permute-start(bf16[128,768]{1,0:T(8,128)(2,1)S(1)} %reshape.230), channel_id=1, source_target_pairs={{0,1},{1,2},{2,3},{3,0},{4,5},{5,6},{6,7},{7,4},{8,9},{9,10},{10,1... | collective-permute-start | bytes 589832 | tf_op jit(solution)/shard_map/ppermute | solution.py:168
  189.1 25.6 %all-to-all-start.4 = ((f32[64,1,384]{2,1,0:T(1,128)}), f32[64,1,384]{2,1,0:T(1,128)S(1)}, u32[]{:S(2)}, u32[]{:S(2)}) async-start(f32[64,1,384]{2,1,0:T(1,128)} %all_to_all.35), calls=%async_computation.4 | async-start | bytes 196608 | tf_op jit(solution)/shard_map/all_to_all | solution.py:159
  209.4 8.4 %collective-permute-start.23 = (bf16[128,768]{1,0:T(8,128)(2,1)S(1)}, bf16[128,768]{1,0:T(8,128)(2,1)S(1)}, u32[]{:S(2)}, u32[]{:S(2)}) collective-permute-start(bf16[128,768]{1,0:T(8,128)(2,1)S(1)} %get-tuple-element.19), channel_id=1, source_target_pairs={{0,1},{1,2},{2,3},{3,0},{4,5},{5,6},{6,7},{7,4},{8,9},{9,10},{10,1... | collective-permute-start | bytes 589832 | tf_op jit(solution)/shard_map/ppermute | solution.py:168
  211.2 11.9 %collective-permute-start.24 = (bf16[128,768]{1,0:T(8,128)(2,1)S(1)}, bf16[128,768]{1,0:T(8,128)(2,1)S(1)}, u32[]{:S(2)}, u32[]{:S(2)}) collective-permute-start(bf16[128,768]{1,0:T(8,128)(2,1)S(1)} %get-tuple-element.21), channel_id=1, source_target_pairs={{0,2},{1,3},{2,0},{3,1},{4,6},{5,7},{6,4},{7,5},{8,10},{9,11},{10,... | collective-permute-start | bytes 589832 | tf_op jit(solution)/shard_map/ppermute | solution.py:168
  214.0 9.1 %collective-permute-start.25 = (bf16[128,768]{1,0:T(8,128)(2,1)S(1)}, bf16[128,768]{1,0:T(8,128)(2,1)S(1)}, u32[]{:S(2)}, u32[]{:S(2)}) collective-permute-start(bf16[128,768]{1,0:T(8,128)(2,1)S(1)} %get-tuple-element.20), channel_id=1, source_target_pairs={{0,3},{1,0},{2,1},{3,2},{4,7},{5,4},{6,5},{7,6},{8,11},{9,8},{10,9... | collective-permute-start | bytes 589832 | tf_op jit(solution)/shard_map/ppermute | solution.py:168
  (16 other events, 110.0 us)

commit v2 on v1

v2 whole, which is shorter than its diff:
```python
import functools

import jax
import jax.numpy as jnp
from jax import lax
from jax.experimental import pallas as pl
from jax.experimental.pallas import tpu as pltpu
from jax.sharding import PartitionSpec as P

SUB = 16
EPSILON = 1e-06
CONCENTRATION = 16.0
TILE = 256
VMEM_LIMIT = 56 * 1024 * 1024

F32 = jnp.float32
BF16 = jnp.bfloat16


def rms_rows(matrix):
    return matrix * lax.rsqrt(jnp.mean(matrix * matrix, axis=-1, keepdims=True) + EPSILON)


def params():
    return pltpu.CompilerParams(
        dimension_semantics=("arbitrary",), vmem_limit_bytes=VMEM_LIMIT
    )


def whole(shape):
    return pl.BlockSpec(shape, lambda i: (0,) * len(shape))


def counts_kernel(labels_ref, out_ref):
    tile = pl.program_id(0)
    shape = out_ref.shape
    label = tile * shape[0] + lax.broadcasted_iota(jnp.int32, shape, 0)
    total = jnp.zeros(shape, F32)
    for slot in range(labels_ref.shape[0]):
        total = total + jnp.where(labels_ref[slot : slot + 1, :] == label, 1.0, 0.0)
    out_ref[...] = total.astype(BF16)


def label_counts(labels_by_slot, lab_dev):
    slots, rows = labels_by_slot.shape
    return pl.pallas_call(
        counts_kernel,
        grid=(lab_dev // TILE,),
        in_specs=[whole((slots, rows))],
        out_specs=pl.BlockSpec((TILE, rows), lambda i: (i, 0)),
        out_shape=jax.ShapeDtypeStruct((lab_dev, rows), BF16),
        compiler_params=params(),
        cost_estimate=pl.CostEstimate(
            flops=3 * slots * rows * lab_dev, bytes_accessed=2 * rows * lab_dev, transcendentals=0
        ),
        name="label_counts",
    )(labels_by_slot)


def weight_rows(centroids, vectors, ids_row):
    scores = lax.dot_general(
        centroids, vectors, (((1,), (1,)), ((), ())), preferred_element_type=F32
    )
    member = ids_row == lax.broadcasted_iota(jnp.int32, scores.shape, 0)
    cosine = jnp.sum(jnp.where(member, scores, 0.0), axis=0, keepdims=True) / vectors.shape[1]
    weight = jnp.exp(CONCENTRATION * cosine)
    return jnp.where(member, weight, 0.0).astype(BF16)


def label_kernel(counts_ref, rows_ref, sub_ref, lv_ref, *rest):
    blocks, (acc, before) = rest[:-2], rest[-2:]
    step = pl.program_id(0)
    sub_total, width = acc.shape
    quarter = sub_total // len(blocks)

    @pl.when(step == 0)
    def _():
        acc[...] = jnp.zeros_like(acc)
        before[...] = jnp.zeros_like(before)

    vectors = before[...]
    member = sub_ref[0] == lax.broadcasted_iota(jnp.int32, (sub_total, vectors.shape[0]), 0)
    sums = jnp.dot(counts_ref[...], rows_ref[:, :width], preferred_element_type=F32)
    acc[...] += jnp.dot(
        jnp.where(member, 1.0, 0.0).astype(BF16), vectors, preferred_element_type=F32
    )
    fresh = rms_rows(sums).astype(BF16)
    lv_ref[...] = fresh
    before[...] = fresh

    @pl.when(step == pl.num_programs(0) - 1)
    def _():
        for index, block in enumerate(blocks):
            block[...] = acc[index * quarter : (index + 1) * quarter].astype(BF16)


def label_pass(counts, rows, sub, width, sub_total, blocks):
    lab_dev, row_total = counts.shape
    tile = 512
    tiles = lab_dev // tile
    each = sub_total // blocks

    def now(i):
        return (jnp.minimum(i, tiles - 1), 0)

    return pl.pallas_call(
        label_kernel,
        grid=(tiles + 1,),
        in_specs=[
            pl.BlockSpec((tile, row_total), now),
            whole(rows.shape),
            pl.BlockSpec((1, 1, tile), lambda i: (jnp.maximum(i - 1, 0), 0, 0)),
        ],
        out_specs=[pl.BlockSpec((tile, width), now)] + [whole((each, width))] * blocks,
        out_shape=[jax.ShapeDtypeStruct((lab_dev, width), BF16)]
        + [jax.ShapeDtypeStruct((each, width), BF16)] * blocks,
        scratch_shapes=[
            pltpu.VMEM((sub_total, width), F32),
            pltpu.VMEM((tile, width), BF16),
        ],
        compiler_params=params(),
        cost_estimate=pl.CostEstimate(
            flops=2 * lab_dev * width * (row_total + sub_total),
            bytes_accessed=2 * lab_dev * (row_total + width),
            transcendentals=0,
        ),
        name="label_pass",
    )(counts, rows, sub.reshape(tiles, 1, tile))


def pass_kernel(cent_total, lv_ref, ids_ref, *rest):
    cents, outs, acc = rest[:cent_total], rest[cent_total:-1], rest[-1]
    step = pl.program_id(0)

    @pl.when(step == 0)
    def _():
        acc[...] = jnp.zeros_like(acc)

    vectors = lv_ref[...]
    centroids = jnp.concatenate([cent[...] for cent in cents], axis=0)
    acc[...] += jnp.dot(
        weight_rows(centroids, vectors, ids_ref[0]), vectors, preferred_element_type=F32
    )

    @pl.when(step == pl.num_programs(0) - 1)
    def _():
        each = acc.shape[0] // len(outs)
        for index, out in enumerate(outs):
            out[...] = acc[index * each : (index + 1) * each].astype(out.dtype)


def weighted_sums(centroids, vectors, ids, outs, kind, name):
    lab_dev, width = vectors.shape
    each = centroids[0].shape[0]
    total = each * len(centroids)
    share = total // outs
    tile = 1024
    tiles = lab_dev // tile
    return pl.pallas_call(
        functools.partial(pass_kernel, len(centroids)),
        grid=(tiles,),
        in_specs=[
            pl.BlockSpec((tile, width), lambda i: (i, 0)),
            pl.BlockSpec((1, 1, tile), lambda i: (i, 0, 0)),
        ]
        + [whole((each, width))] * len(centroids),
        out_specs=[whole((share, width))] * outs,
        out_shape=[jax.ShapeDtypeStruct((share, width), kind)] * outs,
        scratch_shapes=[pltpu.VMEM((total, width), F32)],
        compiler_params=params(),
        cost_estimate=pl.CostEstimate(
            flops=4 * total * lab_dev * width, bytes_accessed=2 * lab_dev * width, transcendentals=0
        ),
        name=name,
    )(vectors, ids.reshape(tiles, 1, tile), *centroids)


def to_all(blocks):
    return lax.all_to_all(blocks, "wide", split_axis=0, concat_axis=0, tiled=True)


def to_chips(blocks):
    n = lax.axis_size("wide")
    groups = [list(range(core, n, 2)) for core in range(2)]
    return lax.all_to_all(
        blocks, "wide", split_axis=0, concat_axis=0, axis_index_groups=groups, tiled=True
    )


def core_swap(value):
    n = lax.axis_size("wide")
    return lax.ppermute(value, "wide", [(i, i ^ 1) for i in range(n)])


def spread(piece, n_wide):
    return jnp.broadcast_to(piece[None], (n_wide,) + piece.shape)


def grp_shift(value, step):
    n = lax.axis_size("grp")
    return lax.ppermute(value, "grp", [(i, (i + step) % n) for i in range(n)])


def grp_sum(value):
    others = [grp_shift(value, step) for step in range(1, lax.axis_size("grp"))]
    total = value.astype(F32)
    for other in others:
        total = total + other.astype(F32)
    return total


def grp_gather(value):
    n = lax.axis_size("grp")
    return [value] + [grp_shift(value, n - step) for step in range(1, n)]


def grp_scatter(blocks):
    total = blocks[0].astype(F32)
    for step in range(1, len(blocks)):
        total = total + grp_shift(blocks[step], step).astype(F32)
    return total


def halves(value):
    high = lax.reduce_precision(value, 8, 7)
    return high.astype(BF16), (value - high).astype(BF16)


def shards(inst_rows, inst_labels, seed_labels, coarse_first, coarse_second, sub_assign, group_map):
    n_wide = lax.axis_size("wide")
    n_grp = lax.axis_size("grp")
    lab_dev = coarse_first.shape[0]
    row_total, width = inst_rows.shape
    slots = inst_labels.shape[1]
    coarse = group_map.shape[0]
    per_dest = row_total // n_wide
    piece = coarse * width // n_wide
    me_grp = lax.axis_index("grp")
    lanes = 128

    block_base = (jnp.arange(row_total, dtype=jnp.int32) // per_dest * n_grp + me_grp) * lab_dev
    wanted = seed_labels[None, :] - block_base[:, None]
    seed_counts = jnp.zeros((row_total, coarse), F32)
    for slot in range(slots):
        seed_counts = seed_counts + (inst_labels[:, slot][:, None] == wanted)
    seed_part = lax.dot_general(
        seed_counts.astype(BF16), inst_rows, (((0,), (0,)), ((), ())), preferred_element_type=F32
    )
    by_slot = inst_labels.reshape(n_wide, per_dest, slots).transpose(0, 2, 1)
    sent = jnp.concatenate(
        [
            seed_part.reshape(n_wide, piece),
            by_slot.reshape(n_wide, slots * per_dest).astype(F32),
        ],
        axis=1,
    )
    early = to_all(sent)
    labels_by_slot = (
        early[:, piece:]
        .astype(jnp.int32)
        .reshape(n_wide, slots, per_dest)
        .transpose(1, 0, 2)
        .reshape(slots, row_total)
    )
    counts = label_counts(labels_by_slot, lab_dev)

    chunk_m = piece // lanes
    high, low = halves(jnp.sum(early[:, :piece], axis=0).reshape(chunk_m, lanes))
    beside = jnp.concatenate(
        [high, low, jnp.zeros((per_dest - 2 * chunk_m, lanes), BF16)], axis=0
    )
    sent = jnp.concatenate(
        [inst_rows.reshape(n_wide, per_dest, width), spread(beside, n_wide)], axis=2
    )
    received = to_all(sent)
    seed_sums = received[:, : 2 * chunk_m, width:].astype(F32)
    seed_sums = (seed_sums[:, :chunk_m] + seed_sums[:, chunk_m:]).reshape(coarse, width)
    seed_rows = grp_sum(lax.reduce_precision(rms_rows(seed_sums), 8, 7).astype(BF16))
    start = rms_rows(seed_rows).astype(BF16)
    received = received.reshape(row_total, width + lanes)

    me_core = lax.rem(lax.axis_index("wide"), 2)
    second = coarse_second.reshape(lab_dev)
    sub_total = coarse * SUB
    share = SUB // 2 // n_grp
    each = coarse * share
    core_turn = (sub_assign // (SUB // 2)) ^ me_core
    grp_turn = lax.rem(sub_assign // share + (n_grp - me_grp), n_grp)
    sub_ids = (core_turn * n_grp + grp_turn) * each + second * share + sub_assign % share
    label_vectors, own_half, other_half = label_pass(
        counts, received, sub_ids, width, sub_total, 2
    )

    def reduced(own, other):
        half = own.astype(F32) + core_swap(other).astype(F32)
        half = half.astype(BF16)
        return grp_scatter([half[i * each : (i + 1) * each] for i in range(n_grp)]).astype(BF16)

    (m_one,) = weighted_sums([start], label_vectors, coarse_first, 1, BF16, "first_pass")
    sub_mine = reduced(own_half, other_half)
    m_one = grp_sum(m_one).astype(BF16)
    chips = n_wide // 2
    chunk_s, chunk_r = share * width // lanes, width // lanes
    pad = (-(chunk_s + chunk_r)) % 8
    sent = jnp.concatenate(
        [
            sub_mine.reshape(chips, chunk_s, lanes),
            m_one.reshape(chips, chunk_r, lanes),
            jnp.zeros((chips, pad, lanes), BF16),
        ],
        axis=1,
    )
    got = jnp.sum(to_chips(sent).astype(F32), axis=0)

    sub_rows = rms_rows(got[:chunk_s].reshape(share, width)).astype(BF16)
    sent = jnp.concatenate(
        [
            sub_rows.reshape(chunk_s, lanes),
            got[chunk_s : chunk_s + chunk_r].astype(BF16),
            jnp.zeros((pad, lanes), BF16),
        ],
        axis=0,
    )
    got = to_chips(spread(sent, chips))
    first = got[:, chunk_s : chunk_s + chunk_r].reshape(coarse, width)
    first = rms_rows(first.astype(F32) + core_swap(first).astype(F32)).astype(BF16)
    sub_own = got[:, :chunk_s].reshape(each, width)

    (m_two,) = weighted_sums([first], label_vectors, second, 1, F32, "second_pass")
    sub_own, m_two = lax.optimization_barrier((sub_own, m_two))
    m_two = grp_sum(m_two)
    two_piece = jnp.sum(to_all(m_two.reshape(n_wide, piece)), axis=0)

    sub_start = grp_gather(sub_own)
    sub_start = sub_start + [core_swap(block) for block in sub_start]
    w_own, w_other = weighted_sums(sub_start, label_vectors, sub_ids, 2, BF16, "sub_pass")
    w_mine = reduced(w_own, w_other)
    host = (
        group_map[None, :] == lax.broadcasted_iota(jnp.int32, (n_wide, coarse), 0)
    ).astype(BF16)
    to_hosts = jnp.dot(
        host, w_mine.reshape(coarse, share * width), preferred_element_type=F32
    ).astype(BF16)
    high, low = halves(two_piece.reshape(chunk_m, lanes))
    pad = (-(2 * chunk_m + chunk_s)) % 8
    sent = jnp.concatenate(
        [
            to_hosts.reshape(n_wide, chunk_s, lanes),
            spread(jnp.concatenate([high, low, jnp.zeros((pad, lanes), BF16)]), n_wide),
        ],
        axis=1,
    )
    got = to_all(sent)
    hosted = jnp.sum(got[:, :chunk_s].astype(F32).reshape(chips, 2, chunk_s, lanes), axis=0)
    hosted = rms_rows(hosted.reshape(2 * share, width))
    last = got[:, chunk_s : chunk_s + 2 * chunk_m].astype(F32)
    coarse_centroids = rms_rows(
        (last[:, :chunk_m] + last[:, chunk_m:]).reshape(coarse, width)
    )
    pieces = grp_gather(hosted)
    ordered = []
    for position in range(n_grp):
        turn = lax.rem(position + (n_grp - me_grp), n_grp)
        value = pieces[0]
        for index in range(1, n_grp):
            value = jnp.where(turn == index, pieces[index], value)
        ordered.append(value.reshape(2, 1, share, width))
    sub_centroids = jnp.concatenate(ordered, axis=1).reshape(1, SUB, width)
    return label_vectors, coarse_centroids, sub_centroids


def solution(mesh):
    in_specs = (
        P(("wide", "grp"), None),
        P(("wide", "grp"), None),
        P(),
        P(("wide", "grp")),
        P(("wide", "grp"), None),
        P(("wide", "grp")),
        P(),
    )
    out_specs = (P(("wide", "grp"), None), P(), P("wide", None, None))
    return jax.shard_map(shards, mesh=mesh, in_specs=in_specs, out_specs=out_specs, check_vma=False)
```

time: 266 us -> 230 us (0.86); the launches traced: 261 us -> 229 us
  starting transfers between devices: 92.3 us -> 73.2 us
  waiting for transfers between devices: 52.3 us -> 70.1 us
  blocking collectives: 47.3 us -> 30 us
  Pallas kernels: 42 us -> 33.5 us
  local copies, waits for them, and re-layouts: 12.2 us -> 6.84 us
    all_to_all x4, waiting for transfers between devices: 19.7 us -> 56.5 us  [to_all(): lax.all_to_all(blocks, 'wide', split_axis=0, concat_axis=0, tiled=True)]
    all_to_all x2, blocking collectives: 47.3 us -> 30 us  [to_chips(): lax.all_to_all(blocks, 'wide', split_axis=0, concat_axis=0, axis_index_gr...]
    ppermute x11 -> x7, starting transfers between devices: 19.3 us -> 2.26 us  [core_swap(): return lax.ppermute(value, 'wide', [(i, i ^ 1) for i in range(n)])]
    ppermute x11 -> x7, waiting for transfers between devices: 14.3 us -> 2.4 us  [core_swap(): return lax.ppermute(value, 'wide', [(i, i ^ 1) for i in range(n)])]
    pallas_call x3 -> x4, Pallas kernels: 33.8 us -> 25.3 us  [the longest x3 14.8 us: weighted_sums(): pl.pallas_call(functools.partial(pass_kernel, len(centroids)), grid=(tile...]
    ppermute x21, waiting for transfers between devices: 18.3 us -> 11.3 us  [grp_shift(): return lax.ppermute(value, 'grp', [(i, (i + step) % n) for i in range(n)])]
    ppermute x21, starting transfers between devices: 41.6 us -> 35.3 us  [grp_shift(): return lax.ppermute(value, 'grp', [(i, (i + step) % n) for i in range(n)])]
    all_to_all x4, starting transfers between devices: 31.4 us -> 35.6 us  [to_all(): lax.all_to_all(blocks, 'wide', split_axis=0, concat_axis=0, tiled=True)]
  transfers between devices with their start and end apart: 36 -> 32, of which waited for: 17 -> 14; matrix products, arithmetic and copies ran while one was open for 5% -> 3% of each run, Pallas kernels for 10% -> 13%
where the time goes in v2:
time: 230 us; the launch traced here: 229 us
  starting transfers between devices  73.2 us (32%)
  waiting for transfers between devices  70.1 us (30%)
  Pallas kernels  33.5 us (15%)
  blocking collectives  30 us (13%)
  other arithmetic  12 us (5%)
  local copies, waits for them, and re-layouts  6.84 us (3%)
    all_to_all x4, waiting for transfers between devices, to_all(): lax.all_to_all(blocks, 'wide', split_axis=0, concat_axis=0, tiled=True)  56.5 us
    all_to_all x4, starting transfers between devices, to_all(): lax.all_to_all(blocks, 'wide', split_axis=0, concat_axis=0, tiled=True)  35.6 us
    ppermute x21, starting transfers between devices, grp_shift(): return lax.ppermute(value, 'grp', [(i, (i + step) % n) for i in range(n)])  35.3 us
    all_to_all x2, blocking collectives, to_chips(): lax.all_to_all(blocks, 'wide', split_axis=0, concat_axis=0, axis_index_gr...  30 us
    pallas_call x3, Pallas kernels, weighted_sums(): pl.pallas_call(functools.partial(pass_kernel, len(centroids)), grid=(tile...  14.8 us
    ppermute x21, waiting for transfers between devices, grp_shift(): return lax.ppermute(value, 'grp', [(i, (i + step) % n) for i in range(n)])  11.3 us
    pallas_call x1, Pallas kernels, label_pass(): pl.pallas_call(label_kernel, grid=(tiles + 1,), in_specs=[pl.BlockSpec((t...  10.5 us
    pallas_call x1, Pallas kernels, label_counts(): pl.pallas_call(counts_kernel, grid=(lab_dev // TILE,), in_specs=[whole((s...  8.24 us
  transfers between devices with their start and end apart: 32, of which 14 were waited for; matrix products, arithmetic and copies ran while one was open for 3% of the time, Pallas kernels for 13%

profile of v2, /device:TPU:6, one launch (start us, length us, event | category | flops | bytes accessed | tf_op | source)
XLA Modules:
  0.0 229.0 jit_solution(14871688709752188545)
XLA Ops:
  5.6 12.2 %all-to-all-start = ((f32[64,1,512]{2,1,0:T(1,128)}), f32[64,1,512]{2,1,0:T(1,128)S(1)}, u32[]{:S(2)}, u32[]{:S(2)}) async-start(f32[64,1,512]{2,1,0:T(1,128)} %all_to_all.26), calls=%async_computation | async-start | bytes 262144 | tf_op jit(solution)/shard_map/all_to_all | solution.py:179
  17.9 8.8 %all-to-all-done = f32[64,1,512]{2,1,0:T(1,128)S(1)} async-done(((f32[64,1,512]{2,1,0:T(1,128)}), f32[64,1,512]{2,1,0:T(1,128)S(1)}, u32[]{:S(2)}, u32[]{:S(2)}) %all-to-all-start) | async-done | bytes 131104 | tf_op jit(solution)/shard_map/all_to_all | solution.py:179
  28.4 6.5 %all-to-all-start.1 = ((bf16[64,16,896]{2,1,0:T(8,128)(2,1)}), bf16[64,16,896]{2,1,0:T(8,128)(2,1)S(1)}, u32[]{:S(2)}, u32[]{:S(2)}) async-start(bf16[64,16,896]{2,1,0:T(8,128)(2,1)} %pad_maximum_fusion), calls=%async_computation.1 | async-start | bytes 3670016 | tf_op jit(solution)/shard_map/all_to_all | solution.py:179
  36.6 8.2 %label_counts.1.counts_ref = bf16[2048,1024]{1,0:T(8,128)(2,1)} custom-call(s32[8,1024]{1,0:T(8,128)} %reshape.175.labels_ref), custom_call_target="tpu_custom_call" | custom-call | flops 50331648 | bytes 4194304 | tf_op jit(solution)/shard_map/label_counts/pallas_call | solution.py:46
  44.9 33.2 %all-to-all-done.1 = bf16[64,16,896]{2,1,0:T(8,128)(2,1)S(1)} async-done(((bf16[64,16,896]{2,1,0:T(8,128)(2,1)}), bf16[64,16,896]{2,1,0:T(8,128)(2,1)S(1)}, u32[]{:S(2)}, u32[]{:S(2)}) %all-to-all-start.1) | async-done | bytes 1835040 | tf_op jit(solution)/shard_map/all_to_all | solution.py:179
  80.6 2.9 %collective-permute-start.5 = (bf16[32,768]{1,0:T(8,128)(2,1)S(1)}, bf16[32,768]{1,0:T(8,128)(2,1)S(1)}, u32[]{:S(2)}, u32[]{:S(2)}) collective-permute-start(bf16[32,768]{1,0:T(8,128)(2,1)S(1)} %reduce-precision_convert_fusion), channel_id=1, source_target_pairs={{0,2},{1,3},{2,0},{3,1},{4,6},{5,7},{6,4},{7,5},{8,10},{9,11},{10,... | collective-permute-start | bytes 147464 | tf_op jit(solution)/shard_map/ppermute | solution.py:201
  84.9 10.5 %label_pass.1 = (bf16[2048,768]{1,0:T(8,128)(2,1)}, bf16[256,768]{1,0:T(8,128)(2,1)}, bf16[256,768]{1,0:T(8,128)(2,1)}) custom-call(bf16[2048,1024]{1,0:T(8,128)(2,1)} %label_counts.1.counts_ref, bf16[1024,896]{1,0:T(8,128)(2,1)} %bitcast.42, s32[4,1,512]{2,1,0:T(1,128)} %bitcast.64), custom_call_target="tpu_custom_call" | custom-call | flops 4831838208 | bytes 7340032 | tf_op jit(solution)/shard_map/label_pass/pallas_call | solution.py:106
  97.8 3.9 %first_pass.1 = bf16[32,768]{1,0:T(8,128)(2,1)} custom-call(bf16[2048,768]{1,0:T(8,128)(2,1)} %get-tuple-element.7.lv_ref, s32[2,1,1024]{2,1,0:T(1,128)} %bitcast.63, bf16[32,768]{1,0:T(8,128)(2,1)} %multiply_convert_fusion.1.rest_0_), custom_call_target="tpu_custom_call" | custom-call | flops 201326592 | bytes 3145728 | tf_op jit(solution)/shard_map/first_pass/pallas_call | solution.py:159
  106.2 2.2 collective-permute-start.2
  108.4 2.5 %collective-permute-start.3 = (bf16[64,768]{1,0:T(8,128)(2,1)S(1)}, bf16[64,768]{1,0:T(8,128)(2,1)S(1)}, u32[]{:S(2)}, u32[]{:S(2)}) collective-permute-start(bf16[64,768]{1,0:T(8,128)(2,1)S(1)} %get-tuple-element.25), channel_id=1, source_target_pairs={{0,3},{1,0},{2,1},{3,2},{4,7},{5,4},{6,5},{7,6},{8,11},{9,8},{10,9... | collective-permute-start | bytes 294920 | tf_op jit(solution)/shard_map/ppermute | solution.py:201
  113.8 15.6 %all_to_all.42 = bf16[32,24,128]{2,1,0:T(8,128)(2,1)S(1)} all-to-all(bf16[32,24,128]{2,1,0:T(8,128)(2,1)S(1)} %maximum_maximum_fusion), channel_id=1, replica_groups={{0,8,16,24,32,40,48,56,64,72,80,88,96,104,112,120,128,136,144,152,160,1..., dimensions={0} | all-to-all | bytes 393216 | tf_op jit(solution)/shard_map/all_to_all | solution.py:185
  130.0 14.4 %all_to_all.43 = bf16[32,24,128]{2,1,0:T(8,128)(2,1)S(1)} all-to-all(bf16[32,24,128]{2,1,0:T(8,128)(2,1)S(1)} %broadcast_in_dim.13), channel_id=1, replica_groups={{0,8,16,24,32,40,48,56,64,72,80,88,96,104,112,120,128,136,144,152,160,1..., dimensions={0} | all-to-all | bytes 393216 | tf_op jit(solution)/shard_map/all_to_all | solution.py:185
  146.7 4.0 %second_pass.1 = f32[32,768]{1,0:T(8,128)} custom-call(bf16[2048,768]{1,0:T(8,128)(2,1)} %get-tuple-element.7.lv_ref, s32[2,1,1024]{2,1,0:T(1,128)} %bitcast.53, bf16[32,768]{1,0:T(8,128)(2,1)} %multiply_convert_fusion.rest_0_), custom_call_target="tpu_custom_call" | custom-call | flops 201326592 | bytes 3145728 | tf_op jit(solution)/shard_map/second_pass/pallas_call | solution.py:159
  150.6 3.1 %collective-permute-start.11 = (bf16[64,768]{1,0:T(8,128)(2,1)S(1)}, bf16[64,768]{1,0:T(8,128)(2,1)S(1)}, u32[]{:S(2)}, u32[]{:S(2)}) collective-permute-start(bf16[64,768]{1,0:T(8,128)(2,1)S(1)} %reshape.185.rest_0_), channel_id=1, source_target_pairs={{0,3},{1,0},{2,1},{3,2},{4,7},{5,4},{6,5},{7,6},{8,11},{9,8},{10,9... | collective-permute-start | bytes 294920 | tf_op jit(solution)/shard_map/ppermute | solution.py:201
  154.8 2.3 %collective-permute-start.22 = (f32[32,768]{1,0:T(8,128)}, f32[32,768]{1,0:T(8,128)S(1)}, u32[]{:S(2)}, u32[]{:S(2)}) collective-permute-start(f32[32,768]{1,0:T(8,128)} %second_pass.1), channel_id=1, source_target_pairs={{0,1},{1,2},{2,3},{3,0},{4,5},{5,6},{6,7},{7,4},{8,9},{9,10},{10,1... | collective-permute-start | bytes 294920 | tf_op jit(solution)/shard_map/ppermute | solution.py:201
  157.2 2.4 %collective-permute-start.23 = (f32[32,768]{1,0:T(8,128)}, f32[32,768]{1,0:T(8,128)S(1)}, u32[]{:S(2)}, u32[]{:S(2)}) collective-permute-start(f32[32,768]{1,0:T(8,128)} %second_pass.1), channel_id=1, source_target_pairs={{0,2},{1,3},{2,0},{3,1},{4,6},{5,7},{6,4},{7,5},{8,10},{9,11},{10,... | collective-permute-start | bytes 294920 | tf_op jit(solution)/shard_map/ppermute | solution.py:201
  159.5 3.4 %collective-permute-start.24 = (f32[32,768]{1,0:T(8,128)}, f32[32,768]{1,0:T(8,128)S(1)}, u32[]{:S(2)}, u32[]{:S(2)}) collective-permute-start(f32[32,768]{1,0:T(8,128)} %second_pass.1), channel_id=1, source_target_pairs={{0,3},{1,0},{2,1},{3,2},{4,7},{5,4},{6,5},{7,6},{8,11},{9,8},{10,9... | collective-permute-start | bytes 294920 | tf_op jit(solution)/shard_map/ppermute | solution.py:201
  167.8 6.6 %all-to-all-start.4 = ((f32[64,1,384]{2,1,0:T(1,128)}), f32[64,1,384]{2,1,0:T(1,128)S(1)}, u32[]{:S(2)}, u32[]{:S(2)}) async-start(f32[64,1,384]{2,1,0:T(1,128)} %all_to_all.35), calls=%async_computation.4 | async-start | bytes 196608 | tf_op jit(solution)/shard_map/all_to_all | solution.py:179
  175.2 6.9 %sub_pass.1 = (bf16[256,768]{1,0:T(8,128)(2,1)}, bf16[256,768]{1,0:T(8,128)(2,1)}) custom-call(bf16[2048,768]{1,0:T(8,128)(2,1)} %get-tuple-element.7.lv_ref, s32[2,1,1024]{2,1,0:T(1,128)} %bitcast.65, bf16[64,768]{1,0:T(8,128)(2,1)} %copy-done.3, bf16[64,768]{1,0:T(8,128)(2,1)} %copy-done.7, bf16[64,768]{1,0:T(8,128)(2,1)} %copy-done.8, ...), custom_call_target="tpu_custom_call" | custom-call | flops 3221225472 | bytes 3145728 | tf_op jit(solution)/shard_map/sub_pass/pallas_call | solution.py:159
  185.2 4.2 %collective-permute-start.20 = (bf16[64,768]{1,0:T(8,128)(2,1)S(1)}, bf16[64,768]{1,0:T(8,128)(2,1)S(1)}, u32[]{:S(2)}, u32[]{:S(2)}) collective-permute-start(bf16[64,768]{1,0:T(8,128)(2,1)S(1)} %get-tuple-element.23), channel_id=1, source_target_pairs={{0,2},{1,3},{2,0},{3,1},{4,6},{5,7},{6,4},{7,5},{8,10},{9,11},{10,... | collective-permute-start | bytes 294920 | tf_op jit(solution)/shard_map/ppermute | solution.py:201
  191.3 3.1 %collective-permute-done.20 = bf16[64,768]{1,0:T(8,128)(2,1)S(1)} collective-permute-done((bf16[64,768]{1,0:T(8,128)(2,1)S(1)}, bf16[64,768]{1,0:T(8,128)(2,1)S(1)}, u32[]{:S(2)}, u32[]{:S(2)}) %collective-permute-start.20) | collective-permute-done | bytes 98336 | tf_op jit(solution)/shard_map/ppermute | solution.py:201
  195.8 10.3 %all-to-all-start.5 = ((bf16[64,24,128]{2,1,0:T(8,128)(2,1)}), bf16[64,24,128]{2,1,0:T(8,128)(2,1)S(1)}, u32[]{:S(2)}, u32[]{:S(2)}) async-start(bf16[64,24,128]{2,1,0:T(8,128)(2,1)} %pad_maximum_fusion.1), calls=%async_computation.5 | async-start | bytes 786432 | tf_op jit(solution)/shard_map/all_to_all | solution.py:179
  206.1 14.1 %all-to-all-done.5 = bf16[64,24,128]{2,1,0:T(8,128)(2,1)S(1)} async-done(((bf16[64,24,128]{2,1,0:T(8,128)(2,1)}), bf16[64,24,128]{2,1,0:T(8,128)(2,1)S(1)}, u32[]{:S(2)}, u32[]{:S(2)}) %all-to-all-start.5) | async-done | bytes 393248 | tf_op jit(solution)/shard_map/all_to_all | solution.py:179
  221.0 3.5 %collective-permute-start.26 = (f32[4,768]{1,0:T(4,128)S(1)}, f32[4,768]{1,0:T(4,128)S(1)}, u32[]{:S(2)}, u32[]{:S(2)}) collective-permute-start(f32[4,768]{1,0:T(4,128)S(1)} %broadcast_multiply_fusion.1), channel_id=1, source_target_pairs={{0,2},{1,3},{2,0},{3,1},{4,6},{5,7},{6,4},{7,5},{8,10},{9,11},{10,... | collective-permute-start | bytes 36872 | tf_op jit(solution)/shard_map/ppermute | solution.py:201
  (172 shorter events, 43.1 us)
Async XLA Ops:
  5.6 21.0 %all-to-all-start = ((f32[64,1,512]{2,1,0:T(1,128)}), f32[64,1,512]{2,1,0:T(1,128)S(1)}, u32[]{:S(2)}, u32[]{:S(2)}) async-start(f32[64,1,512]{2,1,0:T(1,128)} %all_to_all.26), calls=%async_computation | async-start | bytes 262144 | tf_op jit(solution)/shard_map/all_to_all | solution.py:179
  28.4 49.6 %all-to-all-start.1 = ((bf16[64,16,896]{2,1,0:T(8,128)(2,1)}), bf16[64,16,896]{2,1,0:T(8,128)(2,1)S(1)}, u32[]{:S(2)}, u32[]{:S(2)}) async-start(bf16[64,16,896]{2,1,0:T(8,128)(2,1)} %pad_maximum_fusion), calls=%async_computation.1 | async-start | bytes 3670016 | tf_op jit(solution)/shard_map/all_to_all | solution.py:179
  79.0 17.8 %collective-permute-start.4 = (bf16[32,768]{1,0:T(8,128)(2,1)S(1)}, bf16[32,768]{1,0:T(8,128)(2,1)S(1)}, u32[]{:S(2)}, u32[]{:S(2)}) collective-permute-start(bf16[32,768]{1,0:T(8,128)(2,1)S(1)} %reduce-precision_convert_fusion), channel_id=1, source_target_pairs={{0,1},{1,2},{2,3},{3,0},{4,5},{5,6},{6,7},{7,4},{8,9},{9,10},{10,1... | collective-permute-start | bytes 147464 | tf_op jit(solution)/shard_map/ppermute | solution.py:201
  80.6 16.2 %collective-permute-start.5 = (bf16[32,768]{1,0:T(8,128)(2,1)S(1)}, bf16[32,768]{1,0:T(8,128)(2,1)S(1)}, u32[]{:S(2)}, u32[]{:S(2)}) collective-permute-start(bf16[32,768]{1,0:T(8,128)(2,1)S(1)} %reduce-precision_convert_fusion), channel_id=1, source_target_pairs={{0,2},{1,3},{2,0},{3,1},{4,6},{5,7},{6,4},{7,5},{8,10},{9,11},{10,... | collective-permute-start | bytes 147464 | tf_op jit(solution)/shard_map/ppermute | solution.py:201
  83.5 13.3 %collective-permute-start.6 = (bf16[32,768]{1,0:T(8,128)(2,1)S(1)}, bf16[32,768]{1,0:T(8,128)(2,1)S(1)}, u32[]{:S(2)}, u32[]{:S(2)}) collective-permute-start(bf16[32,768]{1,0:T(8,128)(2,1)S(1)} %reduce-precision_convert_fusion), channel_id=1, source_target_pairs={{0,3},{1,0},{2,1},{3,2},{4,7},{5,4},{6,5},{7,6},{8,11},{9,8},{10,9... | collective-permute-start | bytes 147464 | tf_op jit(solution)/shard_map/ppermute | solution.py:201
  95.3 9.7 %collective-permute-start = (bf16[256,768]{1,0:T(8,128)(2,1)}, bf16[256,768]{1,0:T(8,128)(2,1)S(1)}, u32[]{:S(2)}, u32[]{:S(2)}) collective-permute-start(bf16[256,768]{1,0:T(8,128)(2,1)} %get-tuple-element.12), channel_id=1, source_target_pairs={{0,4},{4,0},{8,12},{12,8},{16,20},{20,16},{24,28},{28,24},{32,36},... | collective-permute-start | bytes 1179656 | tf_op jit(solution)/shard_map/ppermute | solution.py:192
  101.7 6.7 %collective-permute-start.7 = (bf16[32,768]{1,0:T(8,128)(2,1)}, bf16[32,768]{1,0:T(8,128)(2,1)S(1)}, u32[]{:S(2)}, u32[]{:S(2)}) collective-permute-start(bf16[32,768]{1,0:T(8,128)(2,1)} %first_pass.1), channel_id=1, source_target_pairs={{0,1},{1,2},{2,3},{3,0},{4,5},{5,6},{6,7},{7,4},{8,9},{9,10},{10,1... | collective-permute-start | bytes 147464 | tf_op jit(solution)/shard_map/ppermute | solution.py:201
  102.4 8.5 %collective-permute-start.8 = (bf16[32,768]{1,0:T(8,128)(2,1)}, bf16[32,768]{1,0:T(8,128)(2,1)S(1)}, u32[]{:S(2)}, u32[]{:S(2)}) collective-permute-start(bf16[32,768]{1,0:T(8,128)(2,1)} %first_pass.1), channel_id=1, source_target_pairs={{0,2},{1,3},{2,0},{3,1},{4,6},{5,7},{6,4},{7,5},{8,10},{9,11},{10,... | collective-permute-start | bytes 147464 | tf_op jit(solution)/shard_map/ppermute | solution.py:201
  103.5 7.4 %collective-permute-start.9 = (bf16[32,768]{1,0:T(8,128)(2,1)}, bf16[32,768]{1,0:T(8,128)(2,1)S(1)}, u32[]{:S(2)}, u32[]{:S(2)}) collective-permute-start(bf16[32,768]{1,0:T(8,128)(2,1)} %first_pass.1), channel_id=1, source_target_pairs={{0,3},{1,0},{2,1},{3,2},{4,7},{5,4},{6,5},{7,6},{8,11},{9,8},{10,9... | collective-permute-start | bytes 147464 | tf_op jit(solution)/shard_map/ppermute | solution.py:201
  105.2 7.7 %collective-permute-start.1 = (bf16[64,768]{1,0:T(8,128)(2,1)S(1)}, bf16[64,768]{1,0:T(8,128)(2,1)S(1)}, u32[]{:S(2)}, u32[]{:S(2)}) collective-permute-start(bf16[64,768]{1,0:T(8,128)(2,1)S(1)} %get-tuple-element.24), channel_id=1, source_target_pairs={{0,1},{1,2},{2,3},{3,0},{4,5},{5,6},{6,7},{7,4},{8,9},{9,10},{10,1... | collective-permute-start | bytes 294920 | tf_op jit(solution)/shard_map/ppermute | solution.py:201
  106.2 6.7 %collective-permute-start.2 = (bf16[64,768]{1,0:T(8,128)(2,1)S(1)}, bf16[64,768]{1,0:T(8,128)(2,1)S(1)}, u32[]{:S(2)}, u32[]{:S(2)}) collective-permute-start(bf16[64,768]{1,0:T(8,128)(2,1)S(1)} %get-tuple-element.26), channel_id=1, source_target_pairs={{0,2},{1,3},{2,0},{3,1},{4,6},{5,7},{6,4},{7,5},{8,10},{9,11},{10,... | collective-permute-start | bytes 294920 | tf_op jit(solution)/shard_map/ppermute | solution.py:201
  150.6 8.9 %collective-permute-start.11 = (bf16[64,768]{1,0:T(8,128)(2,1)S(1)}, bf16[64,768]{1,0:T(8,128)(2,1)S(1)}, u32[]{:S(2)}, u32[]{:S(2)}) collective-permute-start(bf16[64,768]{1,0:T(8,128)(2,1)S(1)} %reshape.185.rest_0_), channel_id=1, source_target_pairs={{0,3},{1,0},{2,1},{3,2},{4,7},{5,4},{6,5},{7,6},{8,11},{9,8},{10,9... | collective-permute-start | bytes 294920 | tf_op jit(solution)/shard_map/ppermute | solution.py:201
  153.7 9.2 %collective-permute-start.12 = (bf16[64,768]{1,0:T(8,128)(2,1)S(1)}, bf16[64,768]{1,0:T(8,128)(2,1)S(1)}, u32[]{:S(2)}, u32[]{:S(2)}) collective-permute-start(bf16[64,768]{1,0:T(8,128)(2,1)S(1)} %reshape.185.rest_0_), channel_id=1, source_target_pairs={{0,2},{1,3},{2,0},{3,1},{4,6},{5,7},{6,4},{7,5},{8,10},{9,11},{10,... | collective-permute-start | bytes 294920 | tf_op jit(solution)/shard_map/ppermute | solution.py:201
  154.8 8.1 %collective-permute-start.13 = (bf16[64,768]{1,0:T(8,128)(2,1)S(1)}, bf16[64,768]{1,0:T(8,128)(2,1)S(1)}, u32[]{:S(2)}, u32[]{:S(2)}) collective-permute-start(bf16[64,768]{1,0:T(8,128)(2,1)S(1)} %reshape.185.rest_0_), channel_id=1, source_target_pairs={{0,1},{1,2},{2,3},{3,0},{4,5},{5,6},{6,7},{7,4},{8,9},{9,10},{10,1... | collective-permute-start | bytes 294920 | tf_op jit(solution)/shard_map/ppermute | solution.py:201
  154.8 10.2 %collective-permute-start.22 = (f32[32,768]{1,0:T(8,128)}, f32[32,768]{1,0:T(8,128)S(1)}, u32[]{:S(2)}, u32[]{:S(2)}) collective-permute-start(f32[32,768]{1,0:T(8,128)} %second_pass.1), channel_id=1, source_target_pairs={{0,1},{1,2},{2,3},{3,0},{4,5},{5,6},{6,7},{7,4},{8,9},{9,10},{10,1... | collective-permute-start | bytes 294920 | tf_op jit(solution)/shard_map/ppermute | solution.py:201
  157.2 8.9 %collective-permute-start.23 = (f32[32,768]{1,0:T(8,128)}, f32[32,768]{1,0:T(8,128)S(1)}, u32[]{:S(2)}, u32[]{:S(2)}) collective-permute-start(f32[32,768]{1,0:T(8,128)} %second_pass.1), channel_id=1, source_target_pairs={{0,2},{1,3},{2,0},{3,1},{4,6},{5,7},{6,4},{7,5},{8,10},{9,11},{10,... | collective-permute-start | bytes 294920 | tf_op jit(solution)/shard_map/ppermute | solution.py:201
  159.5 6.5 %collective-permute-start.24 = (f32[32,768]{1,0:T(8,128)}, f32[32,768]{1,0:T(8,128)S(1)}, u32[]{:S(2)}, u32[]{:S(2)}) collective-permute-start(f32[32,768]{1,0:T(8,128)} %second_pass.1), channel_id=1, source_target_pairs={{0,3},{1,0},{2,1},{3,2},{4,7},{5,4},{6,5},{7,6},{8,11},{9,8},{10,9... | collective-permute-start | bytes 294920 | tf_op jit(solution)/shard_map/ppermute | solution.py:201
  162.9 11.5 %collective-permute-start.14 = (bf16[64,768]{1,0:T(8,128)(2,1)S(1)}, bf16[64,768]{1,0:T(8,128)(2,1)S(1)}, u32[]{:S(2)}, u32[]{:S(2)}) collective-permute-start(bf16[64,768]{1,0:T(8,128)(2,1)S(1)} %reshape.185.rest_0_), channel_id=1, source_target_pairs={{0,4},{4,0},{8,12},{12,8},{16,20},{20,16},{24,28},{28,24},{32,36},... | collective-permute-start | bytes 294920 | tf_op jit(solution)/shard_map/ppermute | solution.py:192
  162.9 11.5 %collective-permute-start.15 = (bf16[64,768]{1,0:T(8,128)(2,1)S(1)}, bf16[64,768]{1,0:T(8,128)(2,1)S(1)}, u32[]{:S(2)}, u32[]{:S(2)}) collective-permute-start(bf16[64,768]{1,0:T(8,128)(2,1)S(1)} %collective-permute-done.11.rest_1_), channel_id=1, source_target_pairs={{0,4},{4,0},{8,12},{12,8},{16,20},{20,16},{24,28},{28,24},{32,36},... | collective-permute-start | bytes 294920 | tf_op jit(solution)/shard_map/ppermute | solution.py:192
  165.0 9.4 %collective-permute-start.16 = (bf16[64,768]{1,0:T(8,128)(2,1)S(1)}, bf16[64,768]{1,0:T(8,128)(2,1)S(1)}, u32[]{:S(2)}, u32[]{:S(2)}) collective-permute-start(bf16[64,768]{1,0:T(8,128)(2,1)S(1)} %collective-permute-done.12.rest_2_), channel_id=1, source_target_pairs={{0,4},{4,0},{8,12},{12,8},{16,20},{20,16},{24,28},{28,24},{32,36},... | collective-permute-start | bytes 294920 | tf_op jit(solution)/shard_map/ppermute | solution.py:192
  166.1 8.4 %collective-permute-start.17 = (bf16[64,768]{1,0:T(8,128)(2,1)S(1)}, bf16[64,768]{1,0:T(8,128)(2,1)S(1)}, u32[]{:S(2)}, u32[]{:S(2)}) collective-permute-start(bf16[64,768]{1,0:T(8,128)(2,1)S(1)} %collective-permute-done.13.rest_3_), channel_id=1, source_target_pairs={{0,4},{4,0},{8,12},{12,8},{16,20},{20,16},{24,28},{28,24},{32,36},... | collective-permute-start | bytes 294920 | tf_op jit(solution)/shard_map/ppermute | solution.py:192
  167.8 14.8 %all-to-all-start.4 = ((f32[64,1,384]{2,1,0:T(1,128)}), f32[64,1,384]{2,1,0:T(1,128)S(1)}, u32[]{:S(2)}, u32[]{:S(2)}) async-start(f32[64,1,384]{2,1,0:T(1,128)} %all_to_all.35), calls=%async_computation.4 | async-start | bytes 196608 | tf_op jit(solution)/shard_map/all_to_all | solution.py:179
  185.2 9.1 %collective-permute-start.20 = (bf16[64,768]{1,0:T(8,128)(2,1)S(1)}, bf16[64,768]{1,0:T(8,128)(2,1)S(1)}, u32[]{:S(2)}, u32[]{:S(2)}) collective-permute-start(bf16[64,768]{1,0:T(8,128)(2,1)S(1)} %get-tuple-element.23), channel_id=1, source_target_pairs={{0,2},{1,3},{2,0},{3,1},{4,6},{5,7},{6,4},{7,5},{8,10},{9,11},{10,... | collective-permute-start | bytes 294920 | tf_op jit(solution)/shard_map/ppermute | solution.py:201
  195.8 24.5 %all-to-all-start.5 = ((bf16[64,24,128]{2,1,0:T(8,128)(2,1)}), bf16[64,24,128]{2,1,0:T(8,128)(2,1)S(1)}, u32[]{:S(2)}, u32[]{:S(2)}) async-start(bf16[64,24,128]{2,1,0:T(8,128)(2,1)} %pad_maximum_fusion.1), calls=%async_computation.5 | async-start | bytes 786432 | tf_op jit(solution)/shard_map/all_to_all | solution.py:179
  (22 other events, 162.1 us)

commit v3 on v2

--- a/solution.py
+++ b/solution.py
@@ -10,7 +10,9 @@
 SUB = 16
 EPSILON = 1e-06
 CONCENTRATION = 16.0
-TILE = 256
+TILE = 512
+LANES = 128
+PIECE = 96
 VMEM_LIMIT = 56 * 1024 * 1024
 
 F32 = jnp.float32
@@ -31,30 +33,95 @@
     return pl.BlockSpec(shape, lambda i: (0,) * len(shape))
 
 
-def counts_kernel(labels_ref, out_ref):
-    tile = pl.program_id(0)
+def sender_kernel(per_dest, span, labels_ref, rows_ref, seeds_ref, out_ref):
+    slots, row_total = labels_ref.shape
+    width = rows_ref.shape[1]
+    coarse = seeds_ref.shape[0]
+    labels = labels_ref[...]
+    block = lax.broadcasted_iota(jnp.int32, (coarse, row_total), 1) // per_dest
+    wanted = seeds_ref[...] - block * span
+    counts = jnp.zeros((coarse, row_total), F32)
+    for slot in range(slots):
+        counts = counts + jnp.where(labels[slot : slot + 1, :] == wanted, 1.0, 0.0)
+    part = jnp.dot(counts.astype(BF16), rows_ref[...], preferred_element_type=F32)
+    high = part.astype(BF16)
+    low = (part - high.astype(F32)).astype(BF16)
+    filler = jnp.zeros((coarse, LANES - PIECE), BF16)
+    pieces = width // PIECE
+    table = []
+    for value in (high, low):
+        for index in range(pieces):
+            chunk = value[:, index * PIECE : (index + 1) * PIECE]
+            table.append(jnp.concatenate([chunk, filler], axis=1))
+    table = jnp.concatenate(table, axis=0)
+    row = lax.broadcasted_iota(jnp.int32, (row_total, 1), 0)
+    dest, place = row // per_dest, row % per_dest
+    each = pieces // 2
+    index = (place // each * pieces + dest % 2 * each + place % each) * coarse + dest // 2
+    index = jnp.where(place < 2 * each, index, -1)
+    picked = lax.broadcasted_iota(jnp.int32, (row_total, table.shape[0]), 1) == index
+    beside = jnp.dot(
+        jnp.where(picked, 1.0, 0.0).astype(BF16), table, preferred_element_type=F32
+    )
+    digits = jnp.concatenate([labels // 256, labels % 256], axis=0).astype(F32)
+    digits = digits.T.astype(BF16)
+    shift = lax.broadcasted_iota(jnp.int32, (2 * slots, LANES), 0) + PIECE
+    shift = shift == lax.broadcasted_iota(jnp.int32, (2 * slots, LANES), 1)
+    beside = beside + jnp.dot(
+        digits, jnp.where(shift, 1.0, 0.0).astype(BF16), preferred_element_type=F32
+    )
+    out_ref[:, :width] = rows_ref[...]
+    out_ref[:, width:] = beside.astype(BF16)
+
+
+def sender(labels, rows, seeds, per_dest, span):
+    row_total, width = rows.shape
+    return pl.pallas_call(
+        functools.partial(sender_kernel, per_dest, span),
+        grid=(1,),
+        in_specs=[whole(labels.shape), whole(rows.shape), whole(seeds.shape)],
+        out_specs=whole((row_total, width + LANES)),
+        out_shape=jax.ShapeDtypeStruct((row_total, width + LANES), BF16),
+        compiler_params=params(),
+        name="sender",
+    )(labels, rows, seeds)
+
+
+def counts_kernel(beside_ref, out_ref, labels_ref):
     shape = out_ref.shape
-    label = tile * shape[0] + lax.broadcasted_iota(jnp.int32, shape, 0)
-    total = jnp.zeros(shape, F32)
-    for slot in range(labels_ref.shape[0]):
-        total = total + jnp.where(labels_ref[slot : slot + 1, :] == label, 1.0, 0.0)
-    out_ref[...] = total.astype(BF16)
-
-
-def label_counts(labels_by_slot, lab_dev):
-    slots, rows = labels_by_slot.shape
+    slots = labels_ref.shape[0]
+
+    @pl.when(pl.program_id(0) == 0)
+    def _():
+        turned = beside_ref[...].astype(F32).T
+        labels = turned[PIECE : PIECE + slots] * 256.0 + turned[PIECE + slots : PIECE + 2 * slots]
+        labels_ref[...] = labels.astype(jnp.int32)
+
+    labels = (labels_ref[...] - pl.program_id(0) * shape[0]).astype(jnp.int16)
+    label = lax.broadcasted_iota(jnp.int32, shape, 0).astype(jnp.int16)
+    one, zero = jnp.ones((), BF16), jnp.zeros((), BF16)
+    total = jnp.zeros(shape, BF16)
+    for slot in range(slots):
+        named = jnp.broadcast_to(labels[slot : slot + 1, :], shape)
+        total = total + jnp.where(named == label, one, zero)
+    out_ref[...] = total
+
+
+def label_counts(received, slots, lab_dev):
+    rows, full = received.shape
     return pl.pallas_call(
         counts_kernel,
         grid=(lab_dev // TILE,),
-        in_specs=[whole((slots, rows))],
+        in_specs=[pl.BlockSpec((rows, LANES), lambda i: (0, full // LANES - 1))],
         out_specs=pl.BlockSpec((TILE, rows), lambda i: (i, 0)),
         out_shape=jax.ShapeDtypeStruct((lab_dev, rows), BF16),
+        scratch_shapes=[pltpu.VMEM((slots, rows), jnp.int32)],
         compiler_params=params(),
         cost_estimate=pl.CostEstimate(
             flops=3 * slots * rows * lab_dev, bytes_accessed=2 * rows * lab_dev, transcendentals=0
         ),
         name="label_counts",
-    )(labels_by_slot)
+    )(received)
 
 
 def weight_rows(centroids, vectors, ids_row):
@@ -146,10 +213,16 @@
     def _():
         each = acc.shape[0] // len(outs)
         for index, out in enumerate(outs):
-            out[...] = acc[index * each : (index + 1) * each].astype(out.dtype)
-
-
-def weighted_sums(centroids, vectors, ids, outs, kind, name):
+            if len(out.shape) == 2:
+                out[...] = acc[index * each : (index + 1) * each].astype(out.dtype)
+            else:
+                per_row = acc.shape[1] // out.shape[2]
+                for place in range(out.shape[0]):
+                    row, start = place // per_row, place % per_row * out.shape[2]
+                    out[place] = acc[row : row + 1, start : start + out.shape[2]]
+
+
+def weighted_sums(centroids, vectors, ids, outs, kind, name, shape=None):
     lab_dev, width = vectors.shape
     each = centroids[0].shape[0]
     total = each * len(centroids)
@@ -164,8 +237,8 @@
             pl.BlockSpec((1, 1, tile), lambda i: (i, 0, 0)),
         ]
         + [whole((each, width))] * len(centroids),
-        out_specs=[whole((share, width))] * outs,
-        out_shape=[jax.ShapeDtypeStruct((share, width), kind)] * outs,
+        out_specs=[whole(shape or (share, width))] * outs,
+        out_shape=[jax.ShapeDtypeStruct(shape or (share, width), kind)] * outs,
         scratch_shapes=[pltpu.VMEM((total, width), F32)],
         compiler_params=params(),
         cost_estimate=pl.CostEstimate(
@@ -236,48 +309,23 @@
     per_dest = row_total // n_wide
     piece = coarse * width // n_wide
     me_grp = lax.axis_index("grp")
-    lanes = 128
-
-    block_base = (jnp.arange(row_total, dtype=jnp.int32) // per_dest * n_grp + me_grp) * lab_dev
-    wanted = seed_labels[None, :] - block_base[:, None]
-    seed_counts = jnp.zeros((row_total, coarse), F32)
-    for slot in range(slots):
-        seed_counts = seed_counts + (inst_labels[:, slot][:, None] == wanted)
-    seed_part = lax.dot_general(
-        seed_counts.astype(BF16), inst_rows, (((0,), (0,)), ((), ())), preferred_element_type=F32
-    )
-    by_slot = inst_labels.reshape(n_wide, per_dest, slots).transpose(0, 2, 1)
-    sent = jnp.concatenate(
-        [
-            seed_part.reshape(n_wide, piece),
-            by_slot.reshape(n_wide, slots * per_dest).astype(F32),
-        ],
-        axis=1,
-    )
-    early = to_all(sent)
-    labels_by_slot = (
-        early[:, piece:]
-        .astype(jnp.int32)
-        .reshape(n_wide, slots, per_dest)
-        .transpose(1, 0, 2)
-        .reshape(slots, row_total)
-    )
-    counts = label_counts(labels_by_slot, lab_dev)
-
+    lanes = LANES
     chunk_m = piece // lanes
-    high, low = halves(jnp.sum(early[:, :piece], axis=0).reshape(chunk_m, lanes))
-    beside = jnp.concatenate(
-        [high, low, jnp.zeros((per_dest - 2 * chunk_m, lanes), BF16)], axis=0
-    )
-    sent = jnp.concatenate(
-        [inst_rows.reshape(n_wide, per_dest, width), spread(beside, n_wide)], axis=2
-    )
-    received = to_all(sent)
-    seed_sums = received[:, : 2 * chunk_m, width:].astype(F32)
-    seed_sums = (seed_sums[:, :chunk_m] + seed_sums[:, chunk_m:]).reshape(coarse, width)
-    seed_rows = grp_sum(lax.reduce_precision(rms_rows(seed_sums), 8, 7).astype(BF16))
-    start = rms_rows(seed_rows).astype(BF16)
+
+    sent = sender(
+        inst_labels.T, inst_rows, (seed_labels - me_grp * lab_dev)[:, None], per_dest,
+        n_grp * lab_dev,
+    )
+    received = to_all(sent.reshape(n_wide, per_dest, width + lanes))
+    beside = received[:, :, width:].astype(F32)
     received = received.reshape(row_total, width + lanes)
+    seed_piece = jnp.sum(beside, axis=0)[:, :PIECE]
+    each = piece // PIECE
+    seed_piece = (seed_piece[:each] + seed_piece[each : 2 * each]).reshape(1, piece)
+    seed_piece = grp_sum(seed_piece)
+    counts = label_counts(received, slots, lab_dev)
+    seed_sums = to_all(spread(seed_piece, n_wide)).reshape(coarse, width)
+    start = rms_rows(lax.reduce_precision(rms_rows(seed_sums), 8, 7)).astype(BF16)
 
     me_core = lax.rem(lax.axis_index("wide"), 2)
     second = coarse_second.reshape(lab_dev)
@@ -291,72 +339,56 @@
         counts, received, sub_ids, width, sub_total, 2
     )
 
-    def reduced(own, other):
-        half = own.astype(F32) + core_swap(other).astype(F32)
-        half = half.astype(BF16)
-        return grp_scatter([half[i * each : (i + 1) * each] for i in range(n_grp)]).astype(BF16)
+    def reduced(own, other, *more):
+        half = (own.astype(F32) + core_swap(other).astype(F32)).astype(BF16)
+        return grp_scatter(
+            [jnp.concatenate([half[i * each : (i + 1) * each], *more]) for i in range(n_grp)]
+        )
 
     (m_one,) = weighted_sums([start], label_vectors, coarse_first, 1, BF16, "first_pass")
-    sub_mine = reduced(own_half, other_half)
+    sub_mine = reduced(own_half, other_half).astype(BF16)
     m_one = grp_sum(m_one).astype(BF16)
     chips = n_wide // 2
-    chunk_s, chunk_r = share * width // lanes, width // lanes
-    pad = (-(chunk_s + chunk_r)) % 8
     sent = jnp.concatenate(
-        [
-            sub_mine.reshape(chips, chunk_s, lanes),
-            m_one.reshape(chips, chunk_r, lanes),
-            jnp.zeros((chips, pad, lanes), BF16),
-        ],
-        axis=1,
+        [sub_mine.reshape(chips, share, width), m_one.reshape(chips, share, piece)], axis=2
     )
     got = jnp.sum(to_chips(sent).astype(F32), axis=0)
 
-    sub_rows = rms_rows(got[:chunk_s].reshape(share, width)).astype(BF16)
-    sent = jnp.concatenate(
-        [
-            sub_rows.reshape(chunk_s, lanes),
-            got[chunk_s : chunk_s + chunk_r].astype(BF16),
-            jnp.zeros((pad, lanes), BF16),
-        ],
-        axis=0,
-    )
+    sent = jnp.concatenate([rms_rows(got[:, :width]), got[:, width:]], axis=1).astype(BF16)
     got = to_chips(spread(sent, chips))
-    first = got[:, chunk_s : chunk_s + chunk_r].reshape(coarse, width)
+    first = got[:, :, width:].reshape(coarse, width)
     first = rms_rows(first.astype(F32) + core_swap(first).astype(F32)).astype(BF16)
-    sub_own = got[:, :chunk_s].reshape(each, width)
-
-    (m_two,) = weighted_sums([first], label_vectors, second, 1, F32, "second_pass")
-    sub_own, m_two = lax.optimization_barrier((sub_own, m_two))
-    m_two = grp_sum(m_two)
-    two_piece = jnp.sum(to_all(m_two.reshape(n_wide, piece)), axis=0)
+    sub_own = got[:, :, :width].reshape(each, width)
+
+    (m_two,) = weighted_sums(
+        [first], label_vectors, second, 1, F32, "second_pass", (n_wide, 1, piece)
+    )
+    two_parts = to_all(m_two).reshape(n_wide, piece)
 
     sub_start = grp_gather(sub_own)
+    _, *sub_start = lax.optimization_barrier((m_two, *sub_start))
     sub_start = sub_start + [core_swap(block) for block in sub_start]
     w_own, w_other = weighted_sums(sub_start, label_vectors, sub_ids, 2, BF16, "sub_pass")
-    w_mine = reduced(w_own, w_other)
+    high, low = halves(jnp.sum(two_parts, axis=0))
+    two_row = jnp.concatenate([high, low])[None]
+    w_mine = reduced(w_own, w_other, jnp.pad(two_row, ((0, 7), (0, 0))))
+    two_piece = w_mine[each, :piece] + w_mine[each, piece:]
+    w_mine = w_mine[:each].astype(BF16)
     host = (
         group_map[None, :] == lax.broadcasted_iota(jnp.int32, (n_wide, coarse), 0)
     ).astype(BF16)
     to_hosts = jnp.dot(
         host, w_mine.reshape(coarse, share * width), preferred_element_type=F32
     ).astype(BF16)
-    high, low = halves(two_piece.reshape(chunk_m, lanes))
-    pad = (-(2 * chunk_m + chunk_s)) % 8
+    two_piece = jnp.stack(halves(two_piece))
     sent = jnp.concatenate(
-        [
-            to_hosts.reshape(n_wide, chunk_s, lanes),
-            spread(jnp.concatenate([high, low, jnp.zeros((pad, lanes), BF16)]), n_wide),
-        ],
-        axis=1,
-    )
-    got = to_all(sent)
-    hosted = jnp.sum(got[:, :chunk_s].astype(F32).reshape(chips, 2, chunk_s, lanes), axis=0)
+        [to_hosts.reshape(n_wide, share, width), spread(two_piece, n_wide)], axis=2
+    )
+    got = to_all(sent).astype(F32)
+    hosted = jnp.sum(got[:, :, :width].reshape(chips, 2, share, width), axis=0)
     hosted = rms_rows(hosted.reshape(2 * share, width))
-    last = got[:, chunk_s : chunk_s + 2 * chunk_m].astype(F32)
-    coarse_centroids = rms_rows(
-        (last[:, :chunk_m] + last[:, chunk_m:]).reshape(coarse, width)
-    )
+    last = got[:, 0, width:] + got[:, 1, width:]
+    coarse_centroids = rms_rows(last.reshape(coarse, width))
     pieces = grp_gather(hosted)
     ordered = []
     for position in range(n_grp):

time: 230 us -> 217 us (0.943)
  starting transfers between devices: 73.2 us -> 65.2 us
  local copies, waits for them, and re-layouts: 6.84 us -> 4.19 us
    ppermute x21 -> x18, starting transfers between devices: 35.3 us -> 26.3 us  [grp_shift(): return lax.ppermute(value, 'grp', [(i, (i + step) % n) for i in range(n)])]
    ppermute x21 -> x18, waiting for transfers between devices: 11.3 us -> 12.6 us  [grp_shift(): return lax.ppermute(value, 'grp', [(i, (i + step) % n) for i in range(n)])]
    pallas_call x1 -> x2, Pallas kernels: 8.24 us -> 9.43 us  [the longest x1 5.8 us: label_counts(): pl.pallas_call(counts_kernel, grid=(lab_dev // TILE,), in_specs=[pl.Block...]
  transfers between devices with their start and end apart: 32 -> 29, of which waited for: 14 -> 11; matrix products, arithmetic and copies ran while one was open for 3% -> 3% of each run, Pallas kernels for 13% -> 14%
where the time goes in v3:
time: 217 us; the launch traced here: 216 us
  waiting for transfers between devices  68.9 us (32%)
  starting transfers between devices  65.2 us (30%)
  Pallas kernels  34.7 us (16%)
  blocking collectives  32.1 us (15%)
  other arithmetic  9.74 us (4%)
  local copies, waits for them, and re-layouts  4.19 us (2%)
    all_to_all x4, waiting for transfers between devices, to_all(): lax.all_to_all(blocks, 'wide', split_axis=0, concat_axis=0, tiled=True)  55 us
    all_to_all x4, starting transfers between devices, to_all(): lax.all_to_all(blocks, 'wide', split_axis=0, concat_axis=0, tiled=True)  37.5 us
    all_to_all x2, blocking collectives, to_chips(): lax.all_to_all(blocks, 'wide', split_axis=0, concat_axis=0, axis_index_gr...  32.1 us
    ppermute x18, starting transfers between devices, grp_shift(): return lax.ppermute(value, 'grp', [(i, (i + step) % n) for i in range(n)])  26.3 us
    pallas_call x3, Pallas kernels, weighted_sums(): pl.pallas_call(functools.partial(pass_kernel, len(centroids)), grid=(tile...  14.8 us
    ppermute x18, waiting for transfers between devices, grp_shift(): return lax.ppermute(value, 'grp', [(i, (i + step) % n) for i in range(n)])  12.6 us
    pallas_call x1, Pallas kernels, label_pass(): pl.pallas_call(label_kernel, grid=(tiles + 1,), in_specs=[pl.BlockSpec((t...  10.5 us
    pallas_call x1, Pallas kernels, label_counts(): pl.pallas_call(counts_kernel, grid=(lab_dev // TILE,), in_specs=[pl.Block...  5.8 us
  transfers between devices with their start and end apart: 29, of which 11 were waited for; matrix products, arithmetic and copies ran while one was open for 3% of the time, Pallas kernels for 14%

profile of v3, /device:TPU:6, one launch (start us, length us, event | category | flops | bytes accessed | tf_op | source)
XLA Modules:
  0.0 216.2 jit_solution(7563279655346907671)
XLA Ops:
  2.0 3.6 %sender.1 = bf16[1024,896]{1,0:T(8,128)(2,1)} custom-call(s32[8,1024]{1,0:T(8,128)} %bitcast.22, bf16[1024,768]{1,0:T(8,128)(2,1)} %rows_ref.1, s32[32,1]{1,0:T(8,128)} %copy.13.seeds_ref), custom_call_target="tpu_custom_call" | custom-call | tf_op jit(solution)/shard_map/sender/pallas_call | solution.py:79
  5.6 12.3 %all-to-all-start = ((bf16[64,16,896]{2,1,0:T(8,128)(2,1)}), bf16[64,16,896]{2,1,0:T(8,128)(2,1)S(1)}, u32[]{:S(2)}, u32[]{:S(2)}) async-start(bf16[64,16,896]{2,1,0:T(8,128)(2,1)} %bitcast.16), calls=%async_computation | async-start | bytes 3670016 | tf_op jit(solution)/shard_map/all_to_all | solution.py:252
  18.6 42.4 %all-to-all-done = bf16[64,16,896]{2,1,0:T(8,128)(2,1)S(1)} async-done(((bf16[64,16,896]{2,1,0:T(8,128)(2,1)}), bf16[64,16,896]{2,1,0:T(8,128)(2,1)S(1)}, u32[]{:S(2)}, u32[]{:S(2)}) %all-to-all-start) | async-done | bytes 1835040 | tf_op jit(solution)/shard_map/all_to_all | solution.py:252
  61.2 1.6 collective-permute-start.4
  62.8 2.9 %collective-permute-start.5 = (f32[1,384]{1,0:T(1,128)S(1)}, f32[1,384]{1,0:T(1,128)S(1)}, u32[]{:S(2)}, u32[]{:S(2)}) collective-permute-start(f32[1,384]{1,0:T(1,128)S(1)} %reshape.161), channel_id=1, source_target_pairs={{0,2},{1,3},{2,0},{3,1},{4,6},{5,7},{6,4},{7,5},{8,10},{9,11},{10,... | collective-permute-start | bytes 4616 | tf_op jit(solution)/shard_map/ppermute | solution.py:274
  67.0 5.8 %label_counts.1.counts_ref = bf16[2048,1024]{1,0:T(8,128)(2,1)} custom-call(bf16[1024,896]{1,0:T(8,128)(2,1)} %bitcast.14), custom_call_target="tpu_custom_call" | custom-call | flops 50331648 | bytes 4194304 | tf_op jit(solution)/shard_map/label_counts/pallas_call | solution.py:112
  73.6 8.4 %all-to-all-start.1 = ((f32[64,1,384]{2,1,0:T(1,128)}), f32[64,1,384]{2,1,0:T(1,128)S(1)}, u32[]{:S(2)}, u32[]{:S(2)}) async-start(f32[64,1,384]{2,1,0:T(1,128)} %broadcast_in_dim.14), calls=%async_computation.1 | async-start | bytes 196608 | tf_op jit(solution)/shard_map/all_to_all | solution.py:252
  82.0 10.5 %label_pass.1 = (bf16[2048,768]{1,0:T(8,128)(2,1)}, bf16[256,768]{1,0:T(8,128)(2,1)}, bf16[256,768]{1,0:T(8,128)(2,1)}) custom-call(bf16[2048,1024]{1,0:T(8,128)(2,1)} %label_counts.1.counts_ref, bf16[1024,896]{1,0:T(8,128)(2,1)} %bitcast.15, s32[4,1,512]{2,1,0:T(1,128)} %bitcast.26), custom_call_target="tpu_custom_call" | custom-call | flops 4831838208 | bytes 7340032 | tf_op jit(solution)/shard_map/label_pass/pallas_call | solution.py:173
  94.8 3.9 %first_pass.1 = bf16[32,768]{1,0:T(8,128)(2,1)} custom-call(bf16[2048,768]{1,0:T(8,128)(2,1)} %get-tuple-element.9.lv_ref, s32[2,1,1024]{2,1,0:T(1,128)} %bitcast.25, bf16[32,768]{1,0:T(8,128)(2,1)} %multiply_convert_fusion.1.rest_0_), custom_call_target="tpu_custom_call" | custom-call | flops 201326592 | bytes 3145728 | tf_op jit(solution)/shard_map/first_pass/pallas_call | solution.py:232
  100.2 1.9 collective-permute-start.9
  103.2 2.2 collective-permute-start.2
  105.4 2.5 %collective-permute-start.3 = (bf16[64,768]{1,0:T(8,128)(2,1)S(1)}, bf16[64,768]{1,0:T(8,128)(2,1)S(1)}, u32[]{:S(2)}, u32[]{:S(2)}) collective-permute-start(bf16[64,768]{1,0:T(8,128)(2,1)S(1)} %get-tuple-element.32), channel_id=1, source_target_pairs={{0,3},{1,0},{2,1},{3,2},{4,7},{5,4},{6,5},{7,6},{8,11},{9,8},{10,9... | collective-permute-start | bytes 294920 | tf_op jit(solution)/shard_map/ppermute | solution.py:274
  111.1 18.2 %all_to_all.30 = bf16[32,2,1152]{2,1,0:T(2,128)(2,1)S(1)} all-to-all(bf16[32,2,1152]{2,1,0:T(2,128)(2,1)S(1)} %pad_maximum_fusion.1), channel_id=1, replica_groups={{0,8,16,24,32,40,48,56,64,72,80,88,96,104,112,120,128,136,144,152,160,1..., dimensions={0} | all-to-all | bytes 294912 | tf_op jit(solution)/shard_map/all_to_all | solution.py:258
  129.7 13.9 %all_to_all.31 = bf16[32,2,1152]{2,1,0:T(2,128)(2,1)S(1)} all-to-all(bf16[32,2,1152]{2,1,0:T(2,128)(2,1)S(1)} %broadcast_in_dim.15), channel_id=1, replica_groups={{0,8,16,24,32,40,48,56,64,72,80,88,96,104,112,120,128,136,144,152,160,1..., dimensions={0} | all-to-all | bytes 294912 | tf_op jit(solution)/shard_map/all_to_all | solution.py:258
  143.9 3.1 %collective-permute-start.11 = (bf16[64,768]{1,0:T(8,128)(2,1)S(1)}, bf16[64,768]{1,0:T(8,128)(2,1)S(1)}, u32[]{:S(2)}, u32[]{:S(2)}) collective-permute-start(bf16[64,768]{1,0:T(8,128)(2,1)S(1)} %reshape.165.rest_0_), channel_id=1, source_target_pairs={{0,3},{1,0},{2,1},{3,2},{4,7},{5,4},{6,5},{7,6},{8,11},{9,8},{10,9... | collective-permute-start | bytes 294920 | tf_op jit(solution)/shard_map/ppermute | solution.py:274
  148.8 4.0 %second_pass.1 = f32[64,1,384]{2,1,0:T(1,128)} custom-call(bf16[2048,768]{1,0:T(8,128)(2,1)} %get-tuple-element.9.lv_ref, s32[2,1,1024]{2,1,0:T(1,128)} %bitcast.23, bf16[32,768]{1,0:T(8,128)(2,1)} %multiply_convert_fusion.rest_0_), custom_call_target="tpu_custom_call" | custom-call | flops 201326592 | bytes 3145728 | tf_op jit(solution)/shard_map/second_pass/pallas_call | solution.py:232
  156.6 6.5 %all-to-all-start.4 = ((f32[64,1,384]{2,1,0:T(1,128)}), f32[64,1,384]{2,1,0:T(1,128)S(1)}, u32[]{:S(2)}, u32[]{:S(2)}) async-start(f32[64,1,384]{2,1,0:T(1,128)} %second_pass.1), calls=%async_computation.4 | async-start | bytes 196608 | tf_op jit(solution)/shard_map/all_to_all | solution.py:252
  163.8 6.9 %sub_pass.1 = (bf16[256,768]{1,0:T(8,128)(2,1)}, bf16[256,768]{1,0:T(8,128)(2,1)}) custom-call(bf16[2048,768]{1,0:T(8,128)(2,1)} %get-tuple-element.9.lv_ref, s32[2,1,1024]{2,1,0:T(1,128)} %bitcast.27, bf16[64,768]{1,0:T(8,128)(2,1)} %copy-done.2, bf16[64,768]{1,0:T(8,128)(2,1)} %copy-done.6, bf16[64,768]{1,0:T(8,128)(2,1)} %copy-done.7, ...), custom_call_target="tpu_custom_call" | custom-call | flops 3221225472 | bytes 3145728 | tf_op jit(solution)/shard_map/sub_pass/pallas_call | solution.py:232
  173.9 2.0 collective-permute-start.20
  177.3 5.3 %collective-permute-done.19 = bf16[72,768]{1,0:T(8,128)(2,1)S(1)} collective-permute-done((bf16[72,768]{1,0:T(8,128)(2,1)S(1)}, bf16[72,768]{1,0:T(8,128)(2,1)S(1)}, u32[]{:S(2)}, u32[]{:S(2)}) %collective-permute-start.19) | collective-permute-done | bytes 110624 | tf_op jit(solution)/shard_map/ppermute | solution.py:274
  184.7 10.3 %all-to-all-start.5 = ((bf16[64,2,1152]{2,1,0:T(2,128)(2,1)}), bf16[64,2,1152]{2,1,0:T(2,128)(2,1)S(1)}, u32[]{:S(2)}, u32[]{:S(2)}) async-start(bf16[64,2,1152]{2,1,0:T(2,128)(2,1)} %pad_maximum_fusion), calls=%async_computation.5 | async-start | bytes 589824 | tf_op jit(solution)/shard_map/all_to_all | solution.py:252
  195.0 12.2 %all-to-all-done.5 = bf16[64,2,1152]{2,1,0:T(2,128)(2,1)S(1)} async-done(((bf16[64,2,1152]{2,1,0:T(2,128)(2,1)}), bf16[64,2,1152]{2,1,0:T(2,128)(2,1)S(1)}, u32[]{:S(2)}, u32[]{:S(2)}) %all-to-all-start.5) | async-done | bytes 294944 | tf_op jit(solution)/shard_map/all_to_all | solution.py:252
  208.1 3.5 %collective-permute-start.23 = (f32[4,768]{1,0:T(4,128)S(1)}, f32[4,768]{1,0:T(4,128)S(1)}, u32[]{:S(2)}, u32[]{:S(2)}) collective-permute-start(f32[4,768]{1,0:T(4,128)S(1)} %broadcast_multiply_fusion.1), channel_id=1, source_target_pairs={{0,2},{1,3},{2,0},{3,1},{4,6},{5,7},{6,4},{7,5},{8,10},{9,11},{10,... | collective-permute-start | bytes 36872 | tf_op jit(solution)/shard_map/ppermute | solution.py:274
  213.4 1.9 collective-permute-done.24
  (148 shorter events, 29.2 us)
Async XLA Ops:
  5.6 55.4 %all-to-all-start = ((bf16[64,16,896]{2,1,0:T(8,128)(2,1)}), bf16[64,16,896]{2,1,0:T(8,128)(2,1)S(1)}, u32[]{:S(2)}, u32[]{:S(2)}) async-start(bf16[64,16,896]{2,1,0:T(8,128)(2,1)} %bitcast.16), calls=%async_computation | async-start | bytes 3670016 | tf_op jit(solution)/shard_map/all_to_all | solution.py:252
  61.2 11.7 %collective-permute-start.4 = (f32[1,384]{1,0:T(1,128)S(1)}, f32[1,384]{1,0:T(1,128)S(1)}, u32[]{:S(2)}, u32[]{:S(2)}) collective-permute-start(f32[1,384]{1,0:T(1,128)S(1)} %reshape.161), channel_id=1, source_target_pairs={{0,1},{1,2},{2,3},{3,0},{4,5},{5,6},{6,7},{7,4},{8,9},{9,10},{10,1... | collective-permute-start | bytes 4616 | tf_op jit(solution)/shard_map/ppermute | solution.py:274
  62.8 10.1 %collective-permute-start.5 = (f32[1,384]{1,0:T(1,128)S(1)}, f32[1,384]{1,0:T(1,128)S(1)}, u32[]{:S(2)}, u32[]{:S(2)}) collective-permute-start(f32[1,384]{1,0:T(1,128)S(1)} %reshape.161), channel_id=1, source_target_pairs={{0,2},{1,3},{2,0},{3,1},{4,6},{5,7},{6,4},{7,5},{8,10},{9,11},{10,... | collective-permute-start | bytes 4616 | tf_op jit(solution)/shard_map/ppermute | solution.py:274
  65.7 7.2 %collective-permute-start.6 = (f32[1,384]{1,0:T(1,128)S(1)}, f32[1,384]{1,0:T(1,128)S(1)}, u32[]{:S(2)}, u32[]{:S(2)}) collective-permute-start(f32[1,384]{1,0:T(1,128)S(1)} %reshape.161), channel_id=1, source_target_pairs={{0,3},{1,0},{2,1},{3,2},{4,7},{5,4},{6,5},{7,6},{8,11},{9,8},{10,9... | collective-permute-start | bytes 4616 | tf_op jit(solution)/shard_map/ppermute | solution.py:274
  73.6 19.0 %all-to-all-start.1 = ((f32[64,1,384]{2,1,0:T(1,128)}), f32[64,1,384]{2,1,0:T(1,128)S(1)}, u32[]{:S(2)}, u32[]{:S(2)}) async-start(f32[64,1,384]{2,1,0:T(1,128)} %broadcast_in_dim.14), calls=%async_computation.1 | async-start | bytes 196608 | tf_op jit(solution)/shard_map/all_to_all | solution.py:252
  92.5 9.6 %collective-permute-start = (bf16[256,768]{1,0:T(8,128)(2,1)}, bf16[256,768]{1,0:T(8,128)(2,1)S(1)}, u32[]{:S(2)}, u32[]{:S(2)}) collective-permute-start(bf16[256,768]{1,0:T(8,128)(2,1)} %get-tuple-element.14), channel_id=1, source_target_pairs={{0,4},{4,0},{8,12},{12,8},{16,20},{20,16},{24,28},{28,24},{32,36},... | collective-permute-start | bytes 1179656 | tf_op jit(solution)/shard_map/ppermute | solution.py:265
  98.7 6.7 %collective-permute-start.7 = (bf16[32,768]{1,0:T(8,128)(2,1)}, bf16[32,768]{1,0:T(8,128)(2,1)S(1)}, u32[]{:S(2)}, u32[]{:S(2)}) collective-permute-start(bf16[32,768]{1,0:T(8,128)(2,1)} %first_pass.1), channel_id=1, source_target_pairs={{0,1},{1,2},{2,3},{3,0},{4,5},{5,6},{6,7},{7,4},{8,9},{9,10},{10,1... | collective-permute-start | bytes 147464 | tf_op jit(solution)/shard_map/ppermute | solution.py:274
  99.4 8.5 %collective-permute-start.8 = (bf16[32,768]{1,0:T(8,128)(2,1)}, bf16[32,768]{1,0:T(8,128)(2,1)S(1)}, u32[]{:S(2)}, u32[]{:S(2)}) collective-permute-start(bf16[32,768]{1,0:T(8,128)(2,1)} %first_pass.1), channel_id=1, source_target_pairs={{0,2},{1,3},{2,0},{3,1},{4,6},{5,7},{6,4},{7,5},{8,10},{9,11},{10,... | collective-permute-start | bytes 147464 | tf_op jit(solution)/shard_map/ppermute | solution.py:274
  100.2 7.7 %collective-permute-start.9 = (bf16[32,768]{1,0:T(8,128)(2,1)}, bf16[32,768]{1,0:T(8,128)(2,1)S(1)}, u32[]{:S(2)}, u32[]{:S(2)}) collective-permute-start(bf16[32,768]{1,0:T(8,128)(2,1)} %first_pass.1), channel_id=1, source_target_pairs={{0,3},{1,0},{2,1},{3,2},{4,7},{5,4},{6,5},{7,6},{8,11},{9,8},{10,9... | collective-permute-start | bytes 147464 | tf_op jit(solution)/shard_map/ppermute | solution.py:274
  102.2 8.1 %collective-permute-start.1 = (bf16[64,768]{1,0:T(8,128)(2,1)S(1)}, bf16[64,768]{1,0:T(8,128)(2,1)S(1)}, u32[]{:S(2)}, u32[]{:S(2)}) collective-permute-start(bf16[64,768]{1,0:T(8,128)(2,1)S(1)} %get-tuple-element.31), channel_id=1, source_target_pairs={{0,1},{1,2},{2,3},{3,0},{4,5},{5,6},{6,7},{7,4},{8,9},{9,10},{10,1... | collective-permute-start | bytes 294920 | tf_op jit(solution)/shard_map/ppermute | solution.py:274
  103.2 7.1 %collective-permute-start.2 = (bf16[64,768]{1,0:T(8,128)(2,1)S(1)}, bf16[64,768]{1,0:T(8,128)(2,1)S(1)}, u32[]{:S(2)}, u32[]{:S(2)}) collective-permute-start(bf16[64,768]{1,0:T(8,128)(2,1)S(1)} %get-tuple-element.33), channel_id=1, source_target_pairs={{0,2},{1,3},{2,0},{3,1},{4,6},{5,7},{6,4},{7,5},{8,10},{9,11},{10,... | collective-permute-start | bytes 294920 | tf_op jit(solution)/shard_map/ppermute | solution.py:274
  143.9 8.9 %collective-permute-start.11 = (bf16[64,768]{1,0:T(8,128)(2,1)S(1)}, bf16[64,768]{1,0:T(8,128)(2,1)S(1)}, u32[]{:S(2)}, u32[]{:S(2)}) collective-permute-start(bf16[64,768]{1,0:T(8,128)(2,1)S(1)} %reshape.165.rest_0_), channel_id=1, source_target_pairs={{0,3},{1,0},{2,1},{3,2},{4,7},{5,4},{6,5},{7,6},{8,11},{9,8},{10,9... | collective-permute-start | bytes 294920 | tf_op jit(solution)/shard_map/ppermute | solution.py:274
  147.0 7.1 %collective-permute-start.12 = (bf16[64,768]{1,0:T(8,128)(2,1)S(1)}, bf16[64,768]{1,0:T(8,128)(2,1)S(1)}, u32[]{:S(2)}, u32[]{:S(2)}) collective-permute-start(bf16[64,768]{1,0:T(8,128)(2,1)S(1)} %reshape.165.rest_0_), channel_id=1, source_target_pairs={{0,2},{1,3},{2,0},{3,1},{4,6},{5,7},{6,4},{7,5},{8,10},{9,11},{10,... | collective-permute-start | bytes 294920 | tf_op jit(solution)/shard_map/ppermute | solution.py:274
  147.8 7.7 %collective-permute-start.13 = (bf16[64,768]{1,0:T(8,128)(2,1)S(1)}, bf16[64,768]{1,0:T(8,128)(2,1)S(1)}, u32[]{:S(2)}, u32[]{:S(2)}) collective-permute-start(bf16[64,768]{1,0:T(8,128)(2,1)S(1)} %reshape.165.rest_0_), channel_id=1, source_target_pairs={{0,1},{1,2},{2,3},{3,0},{4,5},{5,6},{6,7},{7,4},{8,9},{9,10},{10,1... | collective-permute-start | bytes 294920 | tf_op jit(solution)/shard_map/ppermute | solution.py:274
  155.6 7.5 %collective-permute-start.14 = (bf16[64,768]{1,0:T(8,128)(2,1)S(1)}, bf16[64,768]{1,0:T(8,128)(2,1)S(1)}, u32[]{:S(2)}, u32[]{:S(2)}) collective-permute-start(bf16[64,768]{1,0:T(8,128)(2,1)S(1)} %reshape.165.rest_0_), channel_id=1, source_target_pairs={{0,4},{4,0},{8,12},{12,8},{16,20},{20,16},{24,28},{28,24},{32,36},... | collective-permute-start | bytes 294920 | tf_op jit(solution)/shard_map/ppermute | solution.py:265
  155.6 7.5 %collective-permute-start.15 = (bf16[64,768]{1,0:T(8,128)(2,1)S(1)}, bf16[64,768]{1,0:T(8,128)(2,1)S(1)}, u32[]{:S(2)}, u32[]{:S(2)}) collective-permute-start(bf16[64,768]{1,0:T(8,128)(2,1)S(1)} %collective-permute-done.11.rest_1_), channel_id=1, source_target_pairs={{0,4},{4,0},{8,12},{12,8},{16,20},{20,16},{24,28},{28,24},{32,36},... | collective-permute-start | bytes 294920 | tf_op jit(solution)/shard_map/ppermute | solution.py:265
  156.1 7.0 %collective-permute-start.16 = (bf16[64,768]{1,0:T(8,128)(2,1)S(1)}, bf16[64,768]{1,0:T(8,128)(2,1)S(1)}, u32[]{:S(2)}, u32[]{:S(2)}) collective-permute-start(bf16[64,768]{1,0:T(8,128)(2,1)S(1)} %collective-permute-done.12.rest_2_), channel_id=1, source_target_pairs={{0,4},{4,0},{8,12},{12,8},{16,20},{20,16},{24,28},{28,24},{32,36},... | collective-permute-start | bytes 294920 | tf_op jit(solution)/shard_map/ppermute | solution.py:265
  156.1 7.0 %collective-permute-start.17 = (bf16[64,768]{1,0:T(8,128)(2,1)S(1)}, bf16[64,768]{1,0:T(8,128)(2,1)S(1)}, u32[]{:S(2)}, u32[]{:S(2)}) collective-permute-start(bf16[64,768]{1,0:T(8,128)(2,1)S(1)} %collective-permute-done.13.rest_3_), channel_id=1, source_target_pairs={{0,4},{4,0},{8,12},{12,8},{16,20},{20,16},{24,28},{28,24},{32,36},... | collective-permute-start | bytes 294920 | tf_op jit(solution)/shard_map/ppermute | solution.py:265
  156.6 14.7 %all-to-all-start.4 = ((f32[64,1,384]{2,1,0:T(1,128)}), f32[64,1,384]{2,1,0:T(1,128)S(1)}, u32[]{:S(2)}, u32[]{:S(2)}) async-start(f32[64,1,384]{2,1,0:T(1,128)} %second_pass.1), calls=%async_computation.4 | async-start | bytes 196608 | tf_op jit(solution)/shard_map/all_to_all | solution.py:252
  173.8 8.8 %collective-permute-start.19 = (bf16[72,768]{1,0:T(8,128)(2,1)S(1)}, bf16[72,768]{1,0:T(8,128)(2,1)S(1)}, u32[]{:S(2)}, u32[]{:S(2)}) collective-permute-start(bf16[72,768]{1,0:T(8,128)(2,1)S(1)} %get-tuple-element.38), channel_id=1, source_target_pairs={{0,1},{1,2},{2,3},{3,0},{4,5},{5,6},{6,7},{7,4},{8,9},{9,10},{10,1... | collective-permute-start | bytes 331784 | tf_op jit(solution)/shard_map/ppermute | solution.py:274
  173.9 8.7 %collective-permute-start.20 = (bf16[72,768]{1,0:T(8,128)(2,1)S(1)}, bf16[72,768]{1,0:T(8,128)(2,1)S(1)}, u32[]{:S(2)}, u32[]{:S(2)}) collective-permute-start(bf16[72,768]{1,0:T(8,128)(2,1)S(1)} %get-tuple-element.39), channel_id=1, source_target_pairs={{0,2},{1,3},{2,0},{3,1},{4,6},{5,7},{6,4},{7,5},{8,10},{9,11},{10,... | collective-permute-start | bytes 331784 | tf_op jit(solution)/shard_map/ppermute | solution.py:274
  175.9 7.3 %collective-permute-start.21 = (bf16[72,768]{1,0:T(8,128)(2,1)S(1)}, bf16[72,768]{1,0:T(8,128)(2,1)S(1)}, u32[]{:S(2)}, u32[]{:S(2)}) collective-permute-start(bf16[72,768]{1,0:T(8,128)(2,1)S(1)} %get-tuple-element.40), channel_id=1, source_target_pairs={{0,3},{1,0},{2,1},{3,2},{4,7},{5,4},{6,5},{7,6},{8,11},{9,8},{10,9... | collective-permute-start | bytes 331784 | tf_op jit(solution)/shard_map/ppermute | solution.py:274
  184.7 22.6 %all-to-all-start.5 = ((bf16[64,2,1152]{2,1,0:T(2,128)(2,1)}), bf16[64,2,1152]{2,1,0:T(2,128)(2,1)S(1)}, u32[]{:S(2)}, u32[]{:S(2)}) async-start(bf16[64,2,1152]{2,1,0:T(2,128)(2,1)} %pad_maximum_fusion), calls=%async_computation.5 | async-start | bytes 589824 | tf_op jit(solution)/shard_map/all_to_all | solution.py:252
  207.8 5.6 %collective-permute-start.22 = (f32[4,768]{1,0:T(4,128)S(1)}, f32[4,768]{1,0:T(4,128)S(1)}, u32[]{:S(2)}, u32[]{:S(2)}) collective-permute-start(f32[4,768]{1,0:T(4,128)S(1)} %broadcast_multiply_fusion.1), channel_id=1, source_target_pairs={{0,1},{1,2},{2,3},{3,0},{4,5},{5,6},{6,7},{7,4},{8,9},{9,10},{10,1... | collective-permute-start | bytes 36872 | tf_op jit(solution)/shard_map/ppermute | solution.py:274
  (18 other events, 114.0 us)

commit v4 on v3

--- a/solution.py
+++ b/solution.py
@@ -33,13 +33,25 @@
     return pl.BlockSpec(shape, lambda i: (0,) * len(shape))
 
 
-def sender_kernel(per_dest, span, labels_ref, rows_ref, seeds_ref, out_ref):
+def halved(rows, per_dest):
+    total, width = rows.shape
+    half = per_dest // 2
+    parts = rows.astype(F32).reshape(total // per_dest, 2, half, width)
+    return [parts[:, i].reshape(total // 2, width) for i in range(2)]
+
+
+def sender_kernel(per_dest, lab_dev, labels_ref, rows_ref, seeds_ref, out_ref):
     slots, row_total = labels_ref.shape
     width = rows_ref.shape[1]
-    coarse = seeds_ref.shape[0]
+    coarse = seeds_ref.shape[1]
     labels = labels_ref[...]
+    diagonal = lax.broadcasted_iota(jnp.int32, (coarse, coarse), 0)
+    diagonal = diagonal == lax.broadcasted_iota(jnp.int32, (coarse, coarse), 1)
+    seeds = jnp.where(diagonal, seeds_ref[...].astype(F32), 0.0)
+    seeds = jnp.sum(seeds, axis=1, keepdims=True).astype(jnp.int32)
     block = lax.broadcasted_iota(jnp.int32, (coarse, row_total), 1) // per_dest
-    wanted = seeds_ref[...] - block * span
+    owner = block * lax.axis_size("grp") + lax.axis_index("grp")
+    wanted = seeds - owner * lab_dev
     counts = jnp.zeros((coarse, row_total), F32)
     for slot in range(slots):
         counts = counts + jnp.where(labels[slot : slot + 1, :] == wanted, 1.0, 0.0)
@@ -54,34 +66,39 @@
             chunk = value[:, index * PIECE : (index + 1) * PIECE]
             table.append(jnp.concatenate([chunk, filler], axis=1))
     table = jnp.concatenate(table, axis=0)
-    row = lax.broadcasted_iota(jnp.int32, (row_total, 1), 0)
-    dest, place = row // per_dest, row % per_dest
+    half = per_dest // 2
+    row = lax.broadcasted_iota(jnp.int32, (row_total // 2, 1), 0)
+    dest, place = row // half, row % half
     each = pieces // 2
     index = (place // each * pieces + dest % 2 * each + place % each) * coarse + dest // 2
-    index = jnp.where(place < 2 * each, index, -1)
-    picked = lax.broadcasted_iota(jnp.int32, (row_total, table.shape[0]), 1) == index
+    picked = lax.broadcasted_iota(jnp.int32, (row_total // 2, table.shape[0]), 1) == index
     beside = jnp.dot(
         jnp.where(picked, 1.0, 0.0).astype(BF16), table, preferred_element_type=F32
     )
     digits = jnp.concatenate([labels // 256, labels % 256], axis=0).astype(F32)
-    digits = digits.T.astype(BF16)
-    shift = lax.broadcasted_iota(jnp.int32, (2 * slots, LANES), 0) + PIECE
-    shift = shift == lax.broadcasted_iota(jnp.int32, (2 * slots, LANES), 1)
-    beside = beside + jnp.dot(
-        digits, jnp.where(shift, 1.0, 0.0).astype(BF16), preferred_element_type=F32
-    )
-    out_ref[:, :width] = rows_ref[...]
-    out_ref[:, width:] = beside.astype(BF16)
-
-
-def sender(labels, rows, seeds, per_dest, span):
+    shape = (2 * slots, LANES)
+    for index, part in enumerate(halved(digits.T, per_dest)):
+        shift = lax.broadcasted_iota(jnp.int32, shape, 0) + PIECE + index * 2 * slots
+        shift = shift == lax.broadcasted_iota(jnp.int32, shape, 1)
+        beside = beside + jnp.dot(
+            part.astype(BF16),
+            jnp.where(shift, 1.0, 0.0).astype(BF16),
+            preferred_element_type=F32,
+        )
+    for index, part in enumerate(halved(rows_ref[...], per_dest)):
+        out_ref[:, index * width : (index + 1) * width] = part.astype(BF16)
+    out_ref[:, 2 * width :] = beside.astype(BF16)
+
+
+def sender(labels, rows, seeds, per_dest, lab_dev):
     row_total, width = rows.shape
+    shape = (row_total // 2, 2 * width + LANES)
     return pl.pallas_call(
-        functools.partial(sender_kernel, per_dest, span),
+        functools.partial(sender_kernel, per_dest, lab_dev),
         grid=(1,),
         in_specs=[whole(labels.shape), whole(rows.shape), whole(seeds.shape)],
-        out_specs=whole((row_total, width + LANES)),
-        out_shape=jax.ShapeDtypeStruct((row_total, width + LANES), BF16),
+        out_specs=whole(shape),
+        out_shape=jax.ShapeDtypeStruct(shape, BF16),
         compiler_params=params(),
         name="sender",
     )(labels, rows, seeds)
@@ -94,8 +111,12 @@
     @pl.when(pl.program_id(0) == 0)
     def _():
         turned = beside_ref[...].astype(F32).T
-        labels = turned[PIECE : PIECE + slots] * 256.0 + turned[PIECE + slots : PIECE + 2 * slots]
-        labels_ref[...] = labels.astype(jnp.int32)
+        half = turned.shape[1]
+        for index in range(2):
+            first = PIECE + index * 2 * slots
+            labels = turned[first : first + slots] * 256.0
+            labels = labels + turned[first + slots : first + 2 * slots]
+            labels_ref[:, index * half : (index + 1) * half] = labels.astype(jnp.int32)
 
     labels = (labels_ref[...] - pl.program_id(0) * shape[0]).astype(jnp.int16)
     label = lax.broadcasted_iota(jnp.int32, shape, 0).astype(jnp.int16)
@@ -108,11 +129,12 @@
 
 
 def label_counts(received, slots, lab_dev):
-    rows, full = received.shape
+    half, full = received.shape
+    rows = 2 * half
     return pl.pallas_call(
         counts_kernel,
         grid=(lab_dev // TILE,),
-        in_specs=[pl.BlockSpec((rows, LANES), lambda i: (0, full // LANES - 1))],
+        in_specs=[pl.BlockSpec((half, LANES), lambda i: (0, full // LANES - 1))],
         out_specs=pl.BlockSpec((TILE, rows), lambda i: (i, 0)),
         out_shape=jax.ShapeDtypeStruct((lab_dev, rows), BF16),
         scratch_shapes=[pltpu.VMEM((slots, rows), jnp.int32)],
@@ -134,38 +156,54 @@
     return jnp.where(member, weight, 0.0).astype(BF16)
 
 
-def label_kernel(counts_ref, rows_ref, sub_ref, lv_ref, *rest):
-    blocks, (acc, before) = rest[:-2], rest[-2:]
-    step = pl.program_id(0)
+def label_kernel(
+    counts_ref, rows_ref, sub_ref, lv_ref, own_ref, other_ref, acc, before
+):
+    step, last = pl.program_id(0), pl.num_programs(0) - 1
     sub_total, width = acc.shape
-    quarter = sub_total // len(blocks)
+
+    def label_part():
+        half = rows_ref.shape[0]
+        sums = jnp.dot(counts_ref[:, :half], rows_ref[:, :width], preferred_element_type=F32)
+        sums = sums + jnp.dot(
+            counts_ref[:, half:], rows_ref[:, width : 2 * width], preferred_element_type=F32
+        )
+        return rms_rows(sums).astype(BF16)
+
+    def sums_part():
+        vectors = before[...]
+        member = sub_ref[0] == lax.broadcasted_iota(jnp.int32, (sub_total, vectors.shape[0]), 0)
+        return jnp.dot(
+            jnp.where(member, 1.0, 0.0).astype(BF16), vectors, preferred_element_type=F32
+        )
 
     @pl.when(step == 0)
     def _():
         acc[...] = jnp.zeros_like(acc)
-        before[...] = jnp.zeros_like(before)
-
-    vectors = before[...]
-    member = sub_ref[0] == lax.broadcasted_iota(jnp.int32, (sub_total, vectors.shape[0]), 0)
-    sums = jnp.dot(counts_ref[...], rows_ref[:, :width], preferred_element_type=F32)
-    acc[...] += jnp.dot(
-        jnp.where(member, 1.0, 0.0).astype(BF16), vectors, preferred_element_type=F32
-    )
-    fresh = rms_rows(sums).astype(BF16)
-    lv_ref[...] = fresh
-    before[...] = fresh
-
-    @pl.when(step == pl.num_programs(0) - 1)
-    def _():
-        for index, block in enumerate(blocks):
-            block[...] = acc[index * quarter : (index + 1) * quarter].astype(BF16)
-
-
-def label_pass(counts, rows, sub, width, sub_total, blocks):
+        fresh = label_part()
+        lv_ref[...] = fresh
+        before[...] = fresh
+
+    @pl.when(jnp.logical_and(step > 0, step < last))
+    def _():
+        fresh = label_part()
+        acc[...] += sums_part()
+        lv_ref[...] = fresh
+        before[...] = fresh
+
+    @pl.when(step == last)
+    def _():
+        total = acc[...] + sums_part()
+        half = sub_total // 2
+        own_ref[...] = total[:half].astype(BF16)
+        other_ref[...] = total[half:].astype(BF16)
+
+
+def label_pass(counts, rows, sub, width, sub_total):
     lab_dev, row_total = counts.shape
     tile = 512
     tiles = lab_dev // tile
-    each = sub_total // blocks
+    half = sub_total // 2
 
     def now(i):
         return (jnp.minimum(i, tiles - 1), 0)
@@ -178,13 +216,13 @@
             whole(rows.shape),
             pl.BlockSpec((1, 1, tile), lambda i: (jnp.maximum(i - 1, 0), 0, 0)),
         ],
-        out_specs=[pl.BlockSpec((tile, width), now)] + [whole((each, width))] * blocks,
-        out_shape=[jax.ShapeDtypeStruct((lab_dev, width), BF16)]
-        + [jax.ShapeDtypeStruct((each, width), BF16)] * blocks,
-        scratch_shapes=[
-            pltpu.VMEM((sub_total, width), F32),
-            pltpu.VMEM((tile, width), BF16),
+        out_specs=[pl.BlockSpec((tile, width), now), whole((half, width)), whole((half, width))],
+        out_shape=[
+            jax.ShapeDtypeStruct((lab_dev, width), BF16),
+            jax.ShapeDtypeStruct((half, width), BF16),
+            jax.ShapeDtypeStruct((half, width), BF16),
         ],
+        scratch_shapes=[pltpu.VMEM((sub_total, width), F32), pltpu.VMEM((tile, width), BF16)],
         compiler_params=params(),
         cost_estimate=pl.CostEstimate(
             flops=2 * lab_dev * width * (row_total + sub_total),
@@ -195,6 +233,96 @@
     )(counts, rows, sub.reshape(tiles, 1, tile))
 
 
+def first_kernel(seed_ref, lv_ref, ids_ref, out_ref, acc, start):
+    step = pl.program_id(0)
+
+    @pl.when(step == 0)
+    def _():
+        acc[...] = jnp.zeros_like(acc)
+        vectors = seed_ref[...].astype(BF16).astype(F32)
+        start[...] = rms_rows(vectors).astype(BF16)
+
+    vectors = lv_ref[...]
+    acc[...] += jnp.dot(
+        weight_rows(start[...], vectors, ids_ref[0]), vectors, preferred_element_type=F32
+    )
+
+    @pl.when(step == pl.num_programs(0) - 1)
+    def _():
+        out_ref[...] = acc[...].astype(BF16)
+
+
+def first_pass(seeds, vectors, ids, coarse):
+    lab_dev, width = vectors.shape
+    tile = 1024
+    tiles = lab_dev // tile
+    return pl.pallas_call(
+        first_kernel,
+        grid=(tiles,),
+        in_specs=[
+            whole(seeds.shape),
+            pl.BlockSpec((tile, width), lambda i: (i, 0)),
+            pl.BlockSpec((1, 1, tile), lambda i: (i, 0, 0)),
+        ],
+        out_specs=whole((coarse, width)),
+        out_shape=jax.ShapeDtypeStruct((coarse, width), BF16),
+        scratch_shapes=[pltpu.VMEM((coarse, width), F32), pltpu.VMEM((coarse, width), BF16)],
+        compiler_params=params(),
+        cost_estimate=pl.CostEstimate(
+            flops=4 * coarse * lab_dev * width, bytes_accessed=2 * lab_dev * width, transcendentals=0
+        ),
+        name="first_pass",
+    )(seeds, vectors, ids.reshape(tiles, 1, tile))
+
+
+def second_kernel(mine_ref, theirs_ref, lv_ref, ids_ref, out_ref, acc, cent):
+    step = pl.program_id(0)
+
+    @pl.when(step == 0)
+    def _():
+        acc[...] = jnp.zeros_like(acc)
+        total = mine_ref[...].astype(F32) + theirs_ref[...].astype(F32)
+        cent[...] = rms_rows(total).astype(BF16)
+
+    vectors = lv_ref[...]
+    acc[...] += jnp.dot(
+        weight_rows(cent[...], vectors, ids_ref[0]), vectors, preferred_element_type=F32
+    )
+
+    @pl.when(step == pl.num_programs(0) - 1)
+    def _():
+        piece = out_ref.shape[2]
+        per_row = acc.shape[1] // piece
+        for place in range(out_ref.shape[0]):
+            row, col = place // per_row, place % per_row * piece
+            out_ref[place] = acc[row : row + 1, col : col + piece]
+
+
+def second_pass(mine, theirs, vectors, ids, shape):
+    lab_dev, width = vectors.shape
+    coarse = mine.shape[0]
+    tile = 1024
+    tiles = lab_dev // tile
+    return pl.pallas_call(
+        second_kernel,
+        grid=(tiles,),
+        in_specs=[
+            whole((coarse, width)),
+            whole((coarse, width)),
+            pl.BlockSpec((tile, width), lambda i: (i, 0)),
+            pl.BlockSpec((1, 1, tile), lambda i: (i, 0, 0)),
+        ],
+        out_specs=whole(shape),
+        out_shape=jax.ShapeDtypeStruct(shape, F32),
+        scratch_shapes=[pltpu.VMEM((coarse, width), F32), pltpu.VMEM((coarse, width), BF16)],
+        compiler_params=params(),
+        cost_estimate=pl.CostEstimate(
+            flops=4 * coarse * lab_dev * width, bytes_accessed=2 * lab_dev * width, transcendentals=0
+        ),
+        name="second_pass",
+    )(mine, theirs, vectors, ids.reshape(tiles, 1, tile))
+
+
 def pass_kernel(cent_total, lv_ref, ids_ref, *rest):
     cents, outs, acc = rest[:cent_total], rest[cent_total:-1], rest[-1]
     step = pl.program_id(0)
@@ -213,16 +341,10 @@
     def _():
         each = acc.shape[0] // len(outs)
         for index, out in enumerate(outs):
-            if len(out.shape) == 2:
-                out[...] = acc[index * each : (index + 1) * each].astype(out.dtype)
-            else:
-                per_row = acc.shape[1] // out.shape[2]
-                for place in range(out.shape[0]):
-                    row, start = place // per_row, place % per_row * out.shape[2]
-                    out[place] = acc[row : row + 1, start : start + out.shape[2]]
-
-
-def weighted_sums(centroids, vectors, ids, outs, kind, name, shape=None):
+            out[...] = acc[index * each : (index + 1) * each].astype(out.dtype)
+
+
+def weighted_sums(centroids, vectors, ids, outs, kind, name):
     lab_dev, width = vectors.shape
     each = centroids[0].shape[0]
     total = each * len(centroids)
@@ -237,8 +359,8 @@
             pl.BlockSpec((1, 1, tile), lambda i: (i, 0, 0)),
         ]
         + [whole((each, width))] * len(centroids),
-        out_specs=[whole(shape or (share, width))] * outs,
-        out_shape=[jax.ShapeDtypeStruct(shape or (share, width), kind)] * outs,
+        out_specs=[whole((share, width))] * outs,
+        out_shape=[jax.ShapeDtypeStruct((share, width), kind)] * outs,
         scratch_shapes=[pltpu.VMEM((total, width), F32)],
         compiler_params=params(),
         cost_estimate=pl.CostEstimate(
@@ -312,20 +434,16 @@
     lanes = LANES
     chunk_m = piece // lanes
 
-    sent = sender(
-        inst_labels.T, inst_rows, (seed_labels - me_grp * lab_dev)[:, None], per_dest,
-        n_grp * lab_dev,
-    )
-    received = to_all(sent.reshape(n_wide, per_dest, width + lanes))
-    beside = received[:, :, width:].astype(F32)
-    received = received.reshape(row_total, width + lanes)
+    sent = sender(inst_labels.T, inst_rows, seed_labels[None], per_dest, lab_dev)
+    received = to_all(sent.reshape(n_wide, per_dest // 2, 2 * width + lanes))
+    beside = received[:, :, 2 * width :].astype(F32)
+    received = received.reshape(row_total // 2, 2 * width + lanes)
     seed_piece = jnp.sum(beside, axis=0)[:, :PIECE]
     each = piece // PIECE
     seed_piece = (seed_piece[:each] + seed_piece[each : 2 * each]).reshape(1, piece)
     seed_piece = grp_sum(seed_piece)
     counts = label_counts(received, slots, lab_dev)
-    seed_sums = to_all(spread(seed_piece, n_wide)).reshape(coarse, width)
-    start = rms_rows(lax.reduce_precision(rms_rows(seed_sums), 8, 7)).astype(BF16)
+    seed_sums = to_all(spread(seed_piece, n_wide))
 
     me_core = lax.rem(lax.axis_index("wide"), 2)
     second = coarse_second.reshape(lab_dev)
@@ -335,9 +453,7 @@
     core_turn = (sub_assign // (SUB // 2)) ^ me_core
     grp_turn = lax.rem(sub_assign // share + (n_grp - me_grp), n_grp)
     sub_ids = (core_turn * n_grp + grp_turn) * each + second * share + sub_assign % share
-    label_vectors, own_half, other_half = label_pass(
-        counts, received, sub_ids, width, sub_total, 2
-    )
+    label_vectors, own_half, other_half = label_pass(counts, received, sub_ids, width, sub_total)
 
     def reduced(own, other, *more):
         half = (own.astype(F32) + core_swap(other).astype(F32)).astype(BF16)
@@ -345,9 +461,9 @@
             [jnp.concatenate([half[i * each : (i + 1) * each], *more]) for i in range(n_grp)]
         )
 
-    (m_one,) = weighted_sums([start], label_vectors, coarse_first, 1, BF16, "first_pass")
-    sub_mine = reduced(own_half, other_half).astype(BF16)
-    m_one = grp_sum(m_one).astype(BF16)
+    m_one = first_pass(rms_rows(seed_sums.reshape(coarse, width)), label_vectors, coarse_first, coarse)
+    parts = reduced(own_half, other_half, m_one).astype(BF16)
+    sub_mine, m_one = parts[:each], parts[each:]
     chips = n_wide // 2
     sent = jnp.concatenate(
         [sub_mine.reshape(chips, share, width), m_one.reshape(chips, share, piece)], axis=2
@@ -357,11 +473,10 @@
     sent = jnp.concatenate([rms_rows(got[:, :width]), got[:, width:]], axis=1).astype(BF16)
     got = to_chips(spread(sent, chips))
     first = got[:, :, width:].reshape(coarse, width)
-    first = rms_rows(first.astype(F32) + core_swap(first).astype(F32)).astype(BF16)
     sub_own = got[:, :, :width].reshape(each, width)
 
-    (m_two,) = weighted_sums(
-        [first], label_vectors, second, 1, F32, "second_pass", (n_wide, 1, piece)
+    m_two = second_pass(
+        first, core_swap(first), label_vectors, second, (n_wide, 1, piece)
     )
     two_parts = to_all(m_two).reshape(n_wide, piece)
 

time: 217 us -> 210 us (0.968)
  other arithmetic: 9.74 us -> 7.18 us
    pallas_call x1 -> x3, Pallas kernels: 3.63 us -> 11.7 us  [the longest x1 4.07 us: second_pass(): pl.pallas_call(second_kernel, grid=(tiles,), in_specs=[whole((coarse, wid...]
    pallas_call x3 -> x1, Pallas kernels: 14.8 us -> 6.9 us  [weighted_sums(): pl.pallas_call(functools.partial(pass_kernel, len(centroids)), grid=(tile...]
    all_to_all x4, waiting for transfers between devices: 55 us -> 52.3 us  [to_all(): lax.all_to_all(blocks, 'wide', split_axis=0, concat_axis=0, tiled=True)]
    convert_element_type x4 -> x1, other arithmetic: 2.29 us -> 0.08 us  [shards(): parts = reduced(own_half, other_half, m_one).astype(BF16)]
    ppermute x18 -> x15, starting transfers between devices: 26.3 us -> 24.2 us  [grp_shift(): return lax.ppermute(value, 'grp', [(i, (i + step) % n) for i in range(n)])]
    ppermute x18 -> x15, waiting for transfers between devices: 12.6 us -> 13 us  [grp_shift(): return lax.ppermute(value, 'grp', [(i, (i + step) % n) for i in range(n)])]
  transfers between devices with their start and end apart: 29 -> 26, of which waited for: 11 -> 11; matrix products, arithmetic and copies ran while one was open for 3% -> 2% of each run, Pallas kernels for 14% -> 14%
where the time goes in v4:
time: 210 us
  waiting for transfers between devices  67.7 us (32%)
  starting transfers between devices  63.2 us (30%)
  Pallas kernels  33.5 us (16%)
  blocking collectives  32.2 us (15%)
  other arithmetic  7.18 us (3%)
  local copies, waits for them, and re-layouts  4.5 us (2%)
    all_to_all x4, waiting for transfers between devices, to_all(): lax.all_to_all(blocks, 'wide', split_axis=0, concat_axis=0, tiled=True)  52.3 us
    all_to_all x4, starting transfers between devices, to_all(): lax.all_to_all(blocks, 'wide', split_axis=0, concat_axis=0, tiled=True)  37.4 us
    all_to_all x2, blocking collectives, to_chips(): lax.all_to_all(blocks, 'wide', split_axis=0, concat_axis=0, axis_index_gr...  32.2 us
    ppermute x15, starting transfers between devices, grp_shift(): return lax.ppermute(value, 'grp', [(i, (i + step) % n) for i in range(n)])  24.2 us
    ppermute x15, waiting for transfers between devices, grp_shift(): return lax.ppermute(value, 'grp', [(i, (i + step) % n) for i in range(n)])  13 us
    pallas_call x1, Pallas kernels, label_pass(): pl.pallas_call(label_kernel, grid=(tiles + 1,), in_specs=[pl.BlockSpec((t...  9.17 us
    pallas_call x1, Pallas kernels, weighted_sums(): pl.pallas_call(functools.partial(pass_kernel, len(centroids)), grid=(tile...  6.9 us
    pallas_call x1, Pallas kernels, label_counts(): pl.pallas_call(counts_kernel, grid=(lab_dev // TILE,), in_specs=[pl.Block...  5.72 us
  transfers between devices with their start and end apart: 26, of which 11 were waited for; matrix products, arithmetic and copies ran while one was open for 2% of the time, Pallas kernels for 14%

profile of v4, /device:TPU:6, one launch (start us, length us, event | category | flops | bytes accessed | tf_op | source)
XLA Modules:
  0.0 209.6 jit_solution(2747522149756578580)
XLA Ops:
  0.6 3.6 %sender.1 = bf16[512,1664]{1,0:T(8,128)(2,1)} custom-call(s32[8,1024]{1,0:T(8,128)} %bitcast.20, bf16[1024,768]{1,0:T(8,128)(2,1)} %rows_ref.1, s32[1,32]{1,0:T(1,128)} %bitcast.26), custom_call_target="tpu_custom_call" | custom-call | tf_op jit(solution)/shard_map/sender/pallas_call | solution.py:96
  4.2 12.3 %all-to-all-start = ((bf16[64,8,1664]{2,1,0:T(8,128)(2,1)}), bf16[64,8,1664]{2,1,0:T(8,128)(2,1)S(1)}, u32[]{:S(2)}, u32[]{:S(2)}) async-start(bf16[64,8,1664]{2,1,0:T(8,128)(2,1)} %bitcast.15), calls=%async_computation | async-start | bytes 3407872 | tf_op jit(solution)/shard_map/all_to_all | solution.py:374
  17.2 39.7 %all-to-all-done = bf16[64,8,1664]{2,1,0:T(8,128)(2,1)S(1)} async-done(((bf16[64,8,1664]{2,1,0:T(8,128)(2,1)}), bf16[64,8,1664]{2,1,0:T(8,128)(2,1)S(1)}, u32[]{:S(2)}, u32[]{:S(2)}) %all-to-all-start) | async-done | bytes 1703968 | tf_op jit(solution)/shard_map/all_to_all | solution.py:374
  57.0 1.6 collective-permute-start.1
  58.6 2.9 %collective-permute-start.2 = (f32[1,384]{1,0:T(1,128)S(1)}, f32[1,384]{1,0:T(1,128)S(1)}, u32[]{:S(2)}, u32[]{:S(2)}) collective-permute-start(f32[1,384]{1,0:T(1,128)S(1)} %reshape.141), channel_id=1, source_target_pairs={{0,2},{1,3},{2,0},{3,1},{4,6},{5,7},{6,4},{7,5},{8,10},{9,11},{10,... | collective-permute-start | bytes 4616 | tf_op jit(solution)/shard_map/ppermute | solution.py:396
  62.9 5.7 %label_counts.1.counts_ref = bf16[2048,1024]{1,0:T(8,128)(2,1)} custom-call(bf16[512,1664]{1,0:T(8,128)(2,1)} %bitcast.13), custom_call_target="tpu_custom_call" | custom-call | flops 50331648 | bytes 4194304 | tf_op jit(solution)/shard_map/label_counts/pallas_call | solution.py:134
  69.3 8.4 %all-to-all-start.1 = ((f32[64,1,384]{2,1,0:T(1,128)}), f32[64,1,384]{2,1,0:T(1,128)S(1)}, u32[]{:S(2)}, u32[]{:S(2)}) async-start(f32[64,1,384]{2,1,0:T(1,128)} %broadcast_in_dim.14), calls=%async_computation.1 | async-start | bytes 196608 | tf_op jit(solution)/shard_map/all_to_all | solution.py:374
  77.7 9.2 %label_pass.1 = (bf16[2048,768]{1,0:T(8,128)(2,1)}, bf16[256,768]{1,0:T(8,128)(2,1)}, bf16[256,768]{1,0:T(8,128)(2,1)}) custom-call(bf16[2048,1024]{1,0:T(8,128)(2,1)} %label_counts.1.counts_ref, bf16[512,1664]{1,0:T(8,128)(2,1)} %bitcast.14, s32[4,1,512]{2,1,0:T(1,128)} %bitcast.24), custom_call_target="tpu_custom_call" | custom-call | flops 4831838208 | bytes 7340032 | tf_op jit(solution)/shard_map/label_pass/pallas_call | solution.py:211
  88.6 4.0 %first_pass.1 = bf16[32,768]{1,0:T(8,128)(2,1)} custom-call(f32[32,768]{1,0:T(8,128)} %broadcast_multiply_fusion.1.seed_ref, bf16[2048,768]{1,0:T(8,128)(2,1)} %get-tuple-element.9.lv_ref, s32[2,1,1024]{2,1,0:T(1,128)} %bitcast.23), custom_call_target="tpu_custom_call" | custom-call | flops 201326592 | bytes 3145728 | tf_op jit(solution)/shard_map/first_pass/pallas_call | solution.py:259
  95.0 2.2 %collective-permute-start.6 = (bf16[96,768]{1,0:T(8,128)(2,1)S(1)}, bf16[96,768]{1,0:T(8,128)(2,1)S(1)}, u32[]{:S(2)}, u32[]{:S(2)}) collective-permute-start(bf16[96,768]{1,0:T(8,128)(2,1)S(1)} %get-tuple-element.41), channel_id=1, source_target_pairs={{0,3},{1,0},{2,1},{3,2},{4,7},{5,4},{6,5},{7,6},{8,11},{9,8},{10,9... | collective-permute-start | bytes 442376 | tf_op jit(solution)/shard_map/ppermute | solution.py:396
  97.2 6.8 %collective-permute-done.4 = bf16[96,768]{1,0:T(8,128)(2,1)S(1)} collective-permute-done((bf16[96,768]{1,0:T(8,128)(2,1)S(1)}, bf16[96,768]{1,0:T(8,128)(2,1)S(1)}, u32[]{:S(2)}, u32[]{:S(2)}) %collective-permute-start.4) | collective-permute-done | bytes 147488 | tf_op jit(solution)/shard_map/ppermute | solution.py:396
  104.9 18.2 %all_to_all.30 = bf16[32,2,1152]{2,1,0:T(2,128)(2,1)S(1)} all-to-all(bf16[32,2,1152]{2,1,0:T(2,128)(2,1)S(1)} %pad_maximum_fusion.5), channel_id=1, replica_groups={{0,8,16,24,32,40,48,56,64,72,80,88,96,104,112,120,128,136,144,152,160,1..., dimensions={0} | all-to-all | bytes 294912 | tf_op jit(solution)/shard_map/all_to_all | solution.py:380
  123.6 14.0 %all_to_all.31 = bf16[32,2,1152]{2,1,0:T(2,128)(2,1)S(1)} all-to-all(bf16[32,2,1152]{2,1,0:T(2,128)(2,1)S(1)} %broadcast_in_dim.15), channel_id=1, replica_groups={{0,8,16,24,32,40,48,56,64,72,80,88,96,104,112,120,128,136,144,152,160,1..., dimensions={0} | all-to-all | bytes 294912 | tf_op jit(solution)/shard_map/all_to_all | solution.py:380
  138.8 2.2 %collective-permute-start.8 = (bf16[64,768]{1,0:T(8,128)(2,1)S(1)}, bf16[64,768]{1,0:T(8,128)(2,1)S(1)}, u32[]{:S(2)}, u32[]{:S(2)}) collective-permute-start(bf16[64,768]{1,0:T(8,128)(2,1)S(1)} %reshape.147.rest_0_), channel_id=1, source_target_pairs={{0,3},{1,0},{2,1},{3,2},{4,7},{5,4},{6,5},{7,6},{8,11},{9,8},{10,9... | collective-permute-start | bytes 294920 | tf_op jit(solution)/shard_map/ppermute | solution.py:396
  144.3 4.1 %second_pass.1 = f32[64,1,384]{2,1,0:T(1,128)} custom-call(bf16[32,768]{1,0:T(8,128)(2,1)} %bitcast.19, bf16[32,768]{1,0:T(8,128)(2,1)} %copy-done.5, bf16[2048,768]{1,0:T(8,128)(2,1)} %get-tuple-element.9.lv_ref, s32[2,1,1024]{2,1,0:T(1,128)} %bitcast.21), custom_call_target="tpu_custom_call" | custom-call | flops 201326592 | bytes 3145728 | tf_op jit(solution)/shard_map/second_pass/pallas_call | solution.py:306
  149.5 6.4 %all-to-all-start.4 = ((f32[64,1,384]{2,1,0:T(1,128)}), f32[64,1,384]{2,1,0:T(1,128)S(1)}, u32[]{:S(2)}, u32[]{:S(2)}) async-start(f32[64,1,384]{2,1,0:T(1,128)} %second_pass.1), calls=%async_computation.4 | async-start | bytes 196608 | tf_op jit(solution)/shard_map/all_to_all | solution.py:374
  156.8 6.9 %sub_pass.1 = (bf16[256,768]{1,0:T(8,128)(2,1)}, bf16[256,768]{1,0:T(8,128)(2,1)}) custom-call(bf16[2048,768]{1,0:T(8,128)(2,1)} %get-tuple-element.9.lv_ref, s32[2,1,1024]{2,1,0:T(1,128)} %bitcast.25, bf16[64,768]{1,0:T(8,128)(2,1)} %copy-done.4, bf16[64,768]{1,0:T(8,128)(2,1)} %copy-done.10, bf16[64,768]{1,0:T(8,128)(2,1)} %copy-done.11, ...), custom_call_target="tpu_custom_call" | custom-call | flops 3221225472 | bytes 3145728 | tf_op jit(solution)/shard_map/sub_pass/pallas_call | solution.py:354
  166.8 1.7 collective-permute-start.16
  169.8 2.2 %collective-permute-start.18 = (bf16[72,768]{1,0:T(8,128)(2,1)S(1)}, bf16[72,768]{1,0:T(8,128)(2,1)S(1)}, u32[]{:S(2)}, u32[]{:S(2)}) collective-permute-start(bf16[72,768]{1,0:T(8,128)(2,1)S(1)} %get-tuple-element.44), channel_id=1, source_target_pairs={{0,3},{1,0},{2,1},{3,2},{4,7},{5,4},{6,5},{7,6},{8,11},{9,8},{10,9... | collective-permute-start | bytes 331784 | tf_op jit(solution)/shard_map/ppermute | solution.py:396
  172.0 3.8 %collective-permute-done.16 = bf16[72,768]{1,0:T(8,128)(2,1)S(1)} collective-permute-done((bf16[72,768]{1,0:T(8,128)(2,1)S(1)}, bf16[72,768]{1,0:T(8,128)(2,1)S(1)}, u32[]{:S(2)}, u32[]{:S(2)}) %collective-permute-start.16) | collective-permute-done | bytes 110624 | tf_op jit(solution)/shard_map/ppermute | solution.py:396
  177.8 10.3 %all-to-all-start.5 = ((bf16[64,2,1152]{2,1,0:T(2,128)(2,1)}), bf16[64,2,1152]{2,1,0:T(2,128)(2,1)S(1)}, u32[]{:S(2)}, u32[]{:S(2)}) async-start(bf16[64,2,1152]{2,1,0:T(2,128)(2,1)} %pad_maximum_fusion), calls=%async_computation.5 | async-start | bytes 589824 | tf_op jit(solution)/shard_map/all_to_all | solution.py:374
  188.2 12.2 %all-to-all-done.5 = bf16[64,2,1152]{2,1,0:T(2,128)(2,1)S(1)} async-done(((bf16[64,2,1152]{2,1,0:T(2,128)(2,1)}), bf16[64,2,1152]{2,1,0:T(2,128)(2,1)S(1)}, u32[]{:S(2)}, u32[]{:S(2)}) %all-to-all-start.5) | async-done | bytes 294944 | tf_op jit(solution)/shard_map/all_to_all | solution.py:374
  200.9 1.7 collective-permute-start.19
  202.6 2.5 %collective-permute-start.20 = (f32[4,768]{1,0:T(4,128)S(1)}, f32[4,768]{1,0:T(4,128)S(1)}, u32[]{:S(2)}, u32[]{:S(2)}) collective-permute-start(f32[4,768]{1,0:T(4,128)S(1)} %broadcast_multiply_fusion.2), channel_id=1, source_target_pairs={{0,2},{1,3},{2,0},{3,1},{4,6},{5,7},{6,4},{7,5},{8,10},{9,11},{10,... | collective-permute-start | bytes 36872 | tf_op jit(solution)/shard_map/ppermute | solution.py:396
  (139 shorter events, 25.9 us)
Async XLA Ops:
  4.2 52.6 %all-to-all-start = ((bf16[64,8,1664]{2,1,0:T(8,128)(2,1)}), bf16[64,8,1664]{2,1,0:T(8,128)(2,1)S(1)}, u32[]{:S(2)}, u32[]{:S(2)}) async-start(bf16[64,8,1664]{2,1,0:T(8,128)(2,1)} %bitcast.15), calls=%async_computation | async-start | bytes 3407872 | tf_op jit(solution)/shard_map/all_to_all | solution.py:374
  57.0 11.6 %collective-permute-start.1 = (f32[1,384]{1,0:T(1,128)S(1)}, f32[1,384]{1,0:T(1,128)S(1)}, u32[]{:S(2)}, u32[]{:S(2)}) collective-permute-start(f32[1,384]{1,0:T(1,128)S(1)} %reshape.141), channel_id=1, source_target_pairs={{0,1},{1,2},{2,3},{3,0},{4,5},{5,6},{6,7},{7,4},{8,9},{9,10},{10,1... | collective-permute-start | bytes 4616 | tf_op jit(solution)/shard_map/ppermute | solution.py:396
  58.6 10.0 %collective-permute-start.2 = (f32[1,384]{1,0:T(1,128)S(1)}, f32[1,384]{1,0:T(1,128)S(1)}, u32[]{:S(2)}, u32[]{:S(2)}) collective-permute-start(f32[1,384]{1,0:T(1,128)S(1)} %reshape.141), channel_id=1, source_target_pairs={{0,2},{1,3},{2,0},{3,1},{4,6},{5,7},{6,4},{7,5},{8,10},{9,11},{10,... | collective-permute-start | bytes 4616 | tf_op jit(solution)/shard_map/ppermute | solution.py:396
  61.5 7.1 %collective-permute-start.3 = (f32[1,384]{1,0:T(1,128)S(1)}, f32[1,384]{1,0:T(1,128)S(1)}, u32[]{:S(2)}, u32[]{:S(2)}) collective-permute-start(f32[1,384]{1,0:T(1,128)S(1)} %reshape.141), channel_id=1, source_target_pairs={{0,3},{1,0},{2,1},{3,2},{4,7},{5,4},{6,5},{7,6},{8,11},{9,8},{10,9... | collective-permute-start | bytes 4616 | tf_op jit(solution)/shard_map/ppermute | solution.py:396
  69.3 17.7 %all-to-all-start.1 = ((f32[64,1,384]{2,1,0:T(1,128)}), f32[64,1,384]{2,1,0:T(1,128)S(1)}, u32[]{:S(2)}, u32[]{:S(2)}) async-start(f32[64,1,384]{2,1,0:T(1,128)} %broadcast_in_dim.14), calls=%async_computation.1 | async-start | bytes 196608 | tf_op jit(solution)/shard_map/all_to_all | solution.py:374
  86.9 5.7 %collective-permute-start = (bf16[256,768]{1,0:T(8,128)(2,1)}, bf16[256,768]{1,0:T(8,128)(2,1)S(1)}, u32[]{:S(2)}, u32[]{:S(2)}) collective-permute-start(bf16[256,768]{1,0:T(8,128)(2,1)} %get-tuple-element.14), channel_id=1, source_target_pairs={{0,4},{4,0},{8,12},{12,8},{16,20},{20,16},{24,28},{28,24},{32,36},... | collective-permute-start | bytes 1179656 | tf_op jit(solution)/shard_map/ppermute | solution.py:387
  93.4 10.6 %collective-permute-start.4 = (bf16[96,768]{1,0:T(8,128)(2,1)S(1)}, bf16[96,768]{1,0:T(8,128)(2,1)S(1)}, u32[]{:S(2)}, u32[]{:S(2)}) collective-permute-start(bf16[96,768]{1,0:T(8,128)(2,1)S(1)} %get-tuple-element.39), channel_id=1, source_target_pairs={{0,1},{1,2},{2,3},{3,0},{4,5},{5,6},{6,7},{7,4},{8,9},{9,10},{10,1... | collective-permute-start | bytes 442376 | tf_op jit(solution)/shard_map/ppermute | solution.py:396
  94.2 9.8 %collective-permute-start.5 = (bf16[96,768]{1,0:T(8,128)(2,1)S(1)}, bf16[96,768]{1,0:T(8,128)(2,1)S(1)}, u32[]{:S(2)}, u32[]{:S(2)}) collective-permute-start(bf16[96,768]{1,0:T(8,128)(2,1)S(1)} %get-tuple-element.40), channel_id=1, source_target_pairs={{0,2},{1,3},{2,0},{3,1},{4,6},{5,7},{6,4},{7,5},{8,10},{9,11},{10,... | collective-permute-start | bytes 442376 | tf_op jit(solution)/shard_map/ppermute | solution.py:396
  95.0 9.6 %collective-permute-start.6 = (bf16[96,768]{1,0:T(8,128)(2,1)S(1)}, bf16[96,768]{1,0:T(8,128)(2,1)S(1)}, u32[]{:S(2)}, u32[]{:S(2)}) collective-permute-start(bf16[96,768]{1,0:T(8,128)(2,1)S(1)} %get-tuple-element.41), channel_id=1, source_target_pairs={{0,3},{1,0},{2,1},{3,2},{4,7},{5,4},{6,5},{7,6},{8,11},{9,8},{10,9... | collective-permute-start | bytes 442376 | tf_op jit(solution)/shard_map/ppermute | solution.py:396
  137.7 10.7 %collective-permute-start.10 = (bf16[64,768]{1,0:T(8,128)(2,1)S(1)}, bf16[64,768]{1,0:T(8,128)(2,1)S(1)}, u32[]{:S(2)}, u32[]{:S(2)}) collective-permute-start(bf16[64,768]{1,0:T(8,128)(2,1)S(1)} %reshape.147.rest_0_), channel_id=1, source_target_pairs={{0,1},{1,2},{2,3},{3,0},{4,5},{5,6},{6,7},{7,4},{8,9},{9,10},{10,1... | collective-permute-start | bytes 294920 | tf_op jit(solution)/shard_map/ppermute | solution.py:396
  138.8 9.6 %collective-permute-start.8 = (bf16[64,768]{1,0:T(8,128)(2,1)S(1)}, bf16[64,768]{1,0:T(8,128)(2,1)S(1)}, u32[]{:S(2)}, u32[]{:S(2)}) collective-permute-start(bf16[64,768]{1,0:T(8,128)(2,1)S(1)} %reshape.147.rest_0_), channel_id=1, source_target_pairs={{0,3},{1,0},{2,1},{3,2},{4,7},{5,4},{6,5},{7,6},{8,11},{9,8},{10,9... | collective-permute-start | bytes 294920 | tf_op jit(solution)/shard_map/ppermute | solution.py:396
  141.0 7.4 %collective-permute-start.9 = (bf16[64,768]{1,0:T(8,128)(2,1)S(1)}, bf16[64,768]{1,0:T(8,128)(2,1)S(1)}, u32[]{:S(2)}, u32[]{:S(2)}) collective-permute-start(bf16[64,768]{1,0:T(8,128)(2,1)S(1)} %reshape.147.rest_0_), channel_id=1, source_target_pairs={{0,2},{1,3},{2,0},{3,1},{4,6},{5,7},{6,4},{7,5},{8,10},{9,11},{10,... | collective-permute-start | bytes 294920 | tf_op jit(solution)/shard_map/ppermute | solution.py:396
  148.4 7.6 %collective-permute-start.11 = (bf16[64,768]{1,0:T(8,128)(2,1)S(1)}, bf16[64,768]{1,0:T(8,128)(2,1)S(1)}, u32[]{:S(2)}, u32[]{:S(2)}) collective-permute-start(bf16[64,768]{1,0:T(8,128)(2,1)S(1)} %reshape.147.rest_0_), channel_id=1, source_target_pairs={{0,4},{4,0},{8,12},{12,8},{16,20},{20,16},{24,28},{28,24},{32,36},... | collective-permute-start | bytes 294920 | tf_op jit(solution)/shard_map/ppermute | solution.py:387
  148.7 7.3 %collective-permute-start.12 = (bf16[64,768]{1,0:T(8,128)(2,1)S(1)}, bf16[64,768]{1,0:T(8,128)(2,1)S(1)}, u32[]{:S(2)}, u32[]{:S(2)}) collective-permute-start(bf16[64,768]{1,0:T(8,128)(2,1)S(1)} %collective-permute-done.8.rest_1_), channel_id=1, source_target_pairs={{0,4},{4,0},{8,12},{12,8},{16,20},{20,16},{24,28},{28,24},{32,36},... | collective-permute-start | bytes 294920 | tf_op jit(solution)/shard_map/ppermute | solution.py:387
  149.0 7.0 %collective-permute-start.13 = (bf16[64,768]{1,0:T(8,128)(2,1)S(1)}, bf16[64,768]{1,0:T(8,128)(2,1)S(1)}, u32[]{:S(2)}, u32[]{:S(2)}) collective-permute-start(bf16[64,768]{1,0:T(8,128)(2,1)S(1)} %collective-permute-done.9.rest_2_), channel_id=1, source_target_pairs={{0,4},{4,0},{8,12},{12,8},{16,20},{20,16},{24,28},{28,24},{32,36},... | collective-permute-start | bytes 294920 | tf_op jit(solution)/shard_map/ppermute | solution.py:387
  149.2 6.9 %collective-permute-start.14 = (bf16[64,768]{1,0:T(8,128)(2,1)S(1)}, bf16[64,768]{1,0:T(8,128)(2,1)S(1)}, u32[]{:S(2)}, u32[]{:S(2)}) collective-permute-start(bf16[64,768]{1,0:T(8,128)(2,1)S(1)} %collective-permute-done.10.rest_3_), channel_id=1, source_target_pairs={{0,4},{4,0},{8,12},{12,8},{16,20},{20,16},{24,28},{28,24},{32,36},... | collective-permute-start | bytes 294920 | tf_op jit(solution)/shard_map/ppermute | solution.py:387
  149.5 14.7 %all-to-all-start.4 = ((f32[64,1,384]{2,1,0:T(1,128)}), f32[64,1,384]{2,1,0:T(1,128)S(1)}, u32[]{:S(2)}, u32[]{:S(2)}) async-start(f32[64,1,384]{2,1,0:T(1,128)} %second_pass.1), calls=%async_computation.4 | async-start | bytes 196608 | tf_op jit(solution)/shard_map/all_to_all | solution.py:374
  166.8 9.0 %collective-permute-start.16 = (bf16[72,768]{1,0:T(8,128)(2,1)S(1)}, bf16[72,768]{1,0:T(8,128)(2,1)S(1)}, u32[]{:S(2)}, u32[]{:S(2)}) collective-permute-start(bf16[72,768]{1,0:T(8,128)(2,1)S(1)} %get-tuple-element.42), channel_id=1, source_target_pairs={{0,1},{1,2},{2,3},{3,0},{4,5},{5,6},{6,7},{7,4},{8,9},{9,10},{10,1... | collective-permute-start | bytes 331784 | tf_op jit(solution)/shard_map/ppermute | solution.py:396
  168.5 7.3 %collective-permute-start.17 = (bf16[72,768]{1,0:T(8,128)(2,1)S(1)}, bf16[72,768]{1,0:T(8,128)(2,1)S(1)}, u32[]{:S(2)}, u32[]{:S(2)}) collective-permute-start(bf16[72,768]{1,0:T(8,128)(2,1)S(1)} %get-tuple-element.43), channel_id=1, source_target_pairs={{0,2},{1,3},{2,0},{3,1},{4,6},{5,7},{6,4},{7,5},{8,10},{9,11},{10,... | collective-permute-start | bytes 331784 | tf_op jit(solution)/shard_map/ppermute | solution.py:396
  169.8 6.6 %collective-permute-start.18 = (bf16[72,768]{1,0:T(8,128)(2,1)S(1)}, bf16[72,768]{1,0:T(8,128)(2,1)S(1)}, u32[]{:S(2)}, u32[]{:S(2)}) collective-permute-start(bf16[72,768]{1,0:T(8,128)(2,1)S(1)} %get-tuple-element.44), channel_id=1, source_target_pairs={{0,3},{1,0},{2,1},{3,2},{4,7},{5,4},{6,5},{7,6},{8,11},{9,8},{10,9... | collective-permute-start | bytes 331784 | tf_op jit(solution)/shard_map/ppermute | solution.py:396
  177.8 22.6 %all-to-all-start.5 = ((bf16[64,2,1152]{2,1,0:T(2,128)(2,1)}), bf16[64,2,1152]{2,1,0:T(2,128)(2,1)S(1)}, u32[]{:S(2)}, u32[]{:S(2)}) async-start(bf16[64,2,1152]{2,1,0:T(2,128)(2,1)} %pad_maximum_fusion), calls=%async_computation.5 | async-start | bytes 589824 | tf_op jit(solution)/shard_map/all_to_all | solution.py:374
  200.9 6.7 %collective-permute-start.19 = (f32[4,768]{1,0:T(4,128)S(1)}, f32[4,768]{1,0:T(4,128)S(1)}, u32[]{:S(2)}, u32[]{:S(2)}) collective-permute-start(f32[4,768]{1,0:T(4,128)S(1)} %broadcast_multiply_fusion.2), channel_id=1, source_target_pairs={{0,1},{1,2},{2,3},{3,0},{4,5},{5,6},{6,7},{7,4},{8,9},{9,10},{10,1... | collective-permute-start | bytes 36872 | tf_op jit(solution)/shard_map/ppermute | solution.py:396
  202.6 5.2 %collective-permute-start.20 = (f32[4,768]{1,0:T(4,128)S(1)}, f32[4,768]{1,0:T(4,128)S(1)}, u32[]{:S(2)}, u32[]{:S(2)}) collective-permute-start(f32[4,768]{1,0:T(4,128)S(1)} %broadcast_multiply_fusion.2), channel_id=1, source_target_pairs={{0,2},{1,3},{2,0},{3,1},{4,6},{5,7},{6,4},{7,5},{8,10},{9,11},{10,... | collective-permute-start | bytes 36872 | tf_op jit(solution)/shard_map/ppermute | solution.py:396
  205.1 3.7 %collective-permute-start.21 = (f32[4,768]{1,0:T(4,128)S(1)}, f32[4,768]{1,0:T(4,128)S(1)}, u32[]{:S(2)}, u32[]{:S(2)}) collective-permute-start(f32[4,768]{1,0:T(4,128)S(1)} %broadcast_multiply_fusion.2), channel_id=1, source_target_pairs={{0,3},{1,0},{2,1},{3,2},{4,7},{5,4},{6,5},{7,6},{8,11},{9,8},{10,9... | collective-permute-start | bytes 36872 | tf_op jit(solution)/shard_map/ppermute | solution.py:396
  (18 other events, 88.8 us)

commit v5 on v4

--- a/solution.py
+++ b/solution.py
@@ -396,12 +396,13 @@
     return lax.ppermute(value, "grp", [(i, (i + step) % n) for i in range(n)])
 
 
+def total_of(own, others):
+    own, first, second, third = (value.astype(F32) for value in (own, *others))
+    return (own + second) + (first + third)
+
+
 def grp_sum(value):
-    others = [grp_shift(value, step) for step in range(1, lax.axis_size("grp"))]
-    total = value.astype(F32)
-    for other in others:
-        total = total + other.astype(F32)
-    return total
+    return total_of(value, [grp_shift(value, step) for step in (1, 2, 3)])
 
 
 def grp_gather(value):
@@ -410,10 +411,7 @@
 
 
 def grp_scatter(blocks):
-    total = blocks[0].astype(F32)
-    for step in range(1, len(blocks)):
-        total = total + grp_shift(blocks[step], step).astype(F32)
-    return total
+    return total_of(blocks[0], [grp_shift(blocks[step], step) for step in (1, 2, 3)])
 
 
 def halves(value):
@@ -475,9 +473,8 @@
     first = got[:, :, width:].reshape(coarse, width)
     sub_own = got[:, :, :width].reshape(each, width)
 
-    m_two = second_pass(
-        first, core_swap(first), label_vectors, second, (n_wide, 1, piece)
-    )
+    theirs, sub_own = lax.optimization_barrier((core_swap(first), sub_own))
+    m_two = second_pass(first, theirs, label_vectors, second, (n_wide, 1, piece))
     two_parts = to_all(m_two).reshape(n_wide, piece)
 
     sub_start = grp_gather(sub_own)

time: 210 us -> 210 us (level)
  transfers between devices with their start and end apart: 26 -> 26, of which waited for: 11 -> 12; matrix products, arithmetic and copies ran while one was open for 2% -> 2% of each run, Pallas kernels for 14% -> 14%
where the time goes in v5:
time: 210 us; the launch traced here: 209 us
  waiting for transfers between devices  69.2 us (33%)
  starting transfers between devices  61.6 us (29%)
  Pallas kernels  33.5 us (16%)
  blocking collectives  32.6 us (16%)
  other arithmetic  7.18 us (3%)
  local copies, waits for them, and re-layouts  3.88 us (2%)
    all_to_all x4, waiting for transfers between devices, to_all(): lax.all_to_all(blocks, 'wide', split_axis=0, concat_axis=0, tiled=True)  52.3 us
    all_to_all x4, starting transfers between devices, to_all(): lax.all_to_all(blocks, 'wide', split_axis=0, concat_axis=0, tiled=True)  37.4 us
    all_to_all x2, blocking collectives, to_chips(): lax.all_to_all(blocks, 'wide', split_axis=0, concat_axis=0, axis_index_gr...  32.6 us
    ppermute x15, starting transfers between devices, grp_shift(): return lax.ppermute(value, 'grp', [(i, (i + step) % n) for i in range(n)])  22.7 us
    ppermute x15, waiting for transfers between devices, grp_shift(): return lax.ppermute(value, 'grp', [(i, (i + step) % n) for i in range(n)])  14.6 us
    pallas_call x1, Pallas kernels, label_pass(): pl.pallas_call(label_kernel, grid=(tiles + 1,), in_specs=[pl.BlockSpec((t...  9.18 us
    pallas_call x1, Pallas kernels, weighted_sums(): pl.pallas_call(functools.partial(pass_kernel, len(centroids)), grid=(tile...  6.89 us
    pallas_call x1, Pallas kernels, label_counts(): pl.pallas_call(counts_kernel, grid=(lab_dev // TILE,), in_specs=[pl.Block...  5.72 us
  transfers between devices with their start and end apart: 26, of which 12 were waited for; matrix products, arithmetic and copies ran while one was open for 2% of the time, Pallas kernels for 14%

profile of v5, /device:TPU:6, one launch (start us, length us, event | category | flops | bytes accessed | tf_op | source)
XLA Modules:
  0.0 209.3 jit_solution(11777779897390332046)
XLA Ops:
  0.6 3.6 %sender.1 = bf16[512,1664]{1,0:T(8,128)(2,1)} custom-call(s32[8,1024]{1,0:T(8,128)} %bitcast.20, bf16[1024,768]{1,0:T(8,128)(2,1)} %rows_ref.1, s32[1,32]{1,0:T(1,128)} %bitcast.26), custom_call_target="tpu_custom_call" | custom-call | tf_op jit(solution)/shard_map/sender/pallas_call | solution.py:96
  4.2 12.3 %all-to-all-start = ((bf16[64,8,1664]{2,1,0:T(8,128)(2,1)}), bf16[64,8,1664]{2,1,0:T(8,128)(2,1)S(1)}, u32[]{:S(2)}, u32[]{:S(2)}) async-start(bf16[64,8,1664]{2,1,0:T(8,128)(2,1)} %bitcast.15), calls=%async_computation | async-start | bytes 3407872 | tf_op jit(solution)/shard_map/all_to_all | solution.py:374
  17.2 39.7 %all-to-all-done = bf16[64,8,1664]{2,1,0:T(8,128)(2,1)S(1)} async-done(((bf16[64,8,1664]{2,1,0:T(8,128)(2,1)}), bf16[64,8,1664]{2,1,0:T(8,128)(2,1)S(1)}, u32[]{:S(2)}, u32[]{:S(2)}) %all-to-all-start) | async-done | bytes 1703968 | tf_op jit(solution)/shard_map/all_to_all | solution.py:374
  57.0 3.2 %collective-permute-start.1 = (f32[1,384]{1,0:T(1,128)S(1)}, f32[1,384]{1,0:T(1,128)S(1)}, u32[]{:S(2)}, u32[]{:S(2)}) collective-permute-start(f32[1,384]{1,0:T(1,128)S(1)} %reshape.141), channel_id=1, source_target_pairs={{0,2},{1,3},{2,0},{3,1},{4,6},{5,7},{6,4},{7,5},{8,10},{9,11},{10,... | collective-permute-start | bytes 4616 | tf_op jit(solution)/shard_map/ppermute | solution.py:396
  60.9 2.6 %collective-permute-start.3 = (f32[1,384]{1,0:T(1,128)S(1)}, f32[1,384]{1,0:T(1,128)S(1)}, u32[]{:S(2)}, u32[]{:S(2)}) collective-permute-start(f32[1,384]{1,0:T(1,128)S(1)} %reshape.141), channel_id=1, source_target_pairs={{0,3},{1,0},{2,1},{3,2},{4,7},{5,4},{6,5},{7,6},{8,11},{9,8},{10,9... | collective-permute-start | bytes 4616 | tf_op jit(solution)/shard_map/ppermute | solution.py:396
  63.5 5.7 %label_counts.1.counts_ref = bf16[2048,1024]{1,0:T(8,128)(2,1)} custom-call(bf16[512,1664]{1,0:T(8,128)(2,1)} %bitcast.13), custom_call_target="tpu_custom_call" | custom-call | flops 50331648 | bytes 4194304 | tf_op jit(solution)/shard_map/label_counts/pallas_call | solution.py:134
  69.9 8.4 %all-to-all-start.1 = ((f32[64,1,384]{2,1,0:T(1,128)}), f32[64,1,384]{2,1,0:T(1,128)S(1)}, u32[]{:S(2)}, u32[]{:S(2)}) async-start(f32[64,1,384]{2,1,0:T(1,128)} %broadcast_in_dim.14), calls=%async_computation.1 | async-start | bytes 196608 | tf_op jit(solution)/shard_map/all_to_all | solution.py:374
  78.3 9.2 %label_pass.1 = (bf16[2048,768]{1,0:T(8,128)(2,1)}, bf16[256,768]{1,0:T(8,128)(2,1)}, bf16[256,768]{1,0:T(8,128)(2,1)}) custom-call(bf16[2048,1024]{1,0:T(8,128)(2,1)} %label_counts.1.counts_ref, bf16[512,1664]{1,0:T(8,128)(2,1)} %bitcast.14, s32[4,1,512]{2,1,0:T(1,128)} %bitcast.24), custom_call_target="tpu_custom_call" | custom-call | flops 4831838208 | bytes 7340032 | tf_op jit(solution)/shard_map/label_pass/pallas_call | solution.py:211
  89.2 4.0 %first_pass.1 = bf16[32,768]{1,0:T(8,128)(2,1)} custom-call(f32[32,768]{1,0:T(8,128)} %broadcast_multiply_fusion.1.seed_ref, bf16[2048,768]{1,0:T(8,128)(2,1)} %get-tuple-element.11.lv_ref, s32[2,1,1024]{2,1,0:T(1,128)} %bitcast.23), custom_call_target="tpu_custom_call" | custom-call | flops 201326592 | bytes 3145728 | tf_op jit(solution)/shard_map/first_pass/pallas_call | solution.py:259
  95.0 2.6 %collective-permute-start.6 = (bf16[96,768]{1,0:T(8,128)(2,1)S(1)}, bf16[96,768]{1,0:T(8,128)(2,1)S(1)}, u32[]{:S(2)}, u32[]{:S(2)}) collective-permute-start(bf16[96,768]{1,0:T(8,128)(2,1)S(1)} %get-tuple-element.45), channel_id=1, source_target_pairs={{0,3},{1,0},{2,1},{3,2},{4,7},{5,4},{6,5},{7,6},{8,11},{9,8},{10,9... | collective-permute-start | bytes 442376 | tf_op jit(solution)/shard_map/ppermute | solution.py:396
  97.7 4.7 %collective-permute-done.4 = bf16[96,768]{1,0:T(8,128)(2,1)S(1)} collective-permute-done((bf16[96,768]{1,0:T(8,128)(2,1)S(1)}, bf16[96,768]{1,0:T(8,128)(2,1)S(1)}, u32[]{:S(2)}, u32[]{:S(2)}) %collective-permute-start.4) | collective-permute-done | bytes 147488 | tf_op jit(solution)/shard_map/ppermute | solution.py:396
  102.4 2.5 %collective-permute-done.5 = bf16[96,768]{1,0:T(8,128)(2,1)S(1)} collective-permute-done((bf16[96,768]{1,0:T(8,128)(2,1)S(1)}, bf16[96,768]{1,0:T(8,128)(2,1)S(1)}, u32[]{:S(2)}, u32[]{:S(2)}) %collective-permute-start.5) | collective-permute-done | bytes 147488 | tf_op jit(solution)/shard_map/ppermute | solution.py:396
  105.2 18.4 %all_to_all.30 = bf16[32,2,1152]{2,1,0:T(2,128)(2,1)S(1)} all-to-all(bf16[32,2,1152]{2,1,0:T(2,128)(2,1)S(1)} %pad_maximum_fusion.5), channel_id=1, replica_groups={{0,8,16,24,32,40,48,56,64,72,80,88,96,104,112,120,128,136,144,152,160,1..., dimensions={0} | all-to-all | bytes 294912 | tf_op jit(solution)/shard_map/all_to_all | solution.py:380
  124.1 14.2 %all_to_all.31 = bf16[32,2,1152]{2,1,0:T(2,128)(2,1)S(1)} all-to-all(bf16[32,2,1152]{2,1,0:T(2,128)(2,1)S(1)} %broadcast_in_dim.15), channel_id=1, replica_groups={{0,8,16,24,32,40,48,56,64,72,80,88,96,104,112,120,128,136,144,152,160,1..., dimensions={0} | all-to-all | bytes 294912 | tf_op jit(solution)/shard_map/all_to_all | solution.py:380
  139.6 3.2 %collective-permute-start.8 = (bf16[64,768]{1,0:T(8,128)(2,1)S(1)}, bf16[64,768]{1,0:T(8,128)(2,1)S(1)}, u32[]{:S(2)}, u32[]{:S(2)}) collective-permute-start(bf16[64,768]{1,0:T(8,128)(2,1)S(1)} %reshape.147.rest_0_), channel_id=1, source_target_pairs={{0,3},{1,0},{2,1},{3,2},{4,7},{5,4},{6,5},{7,6},{8,11},{9,8},{10,9... | collective-permute-start | bytes 294920 | tf_op jit(solution)/shard_map/ppermute | solution.py:396
  142.9 4.1 %second_pass.1 = f32[64,1,384]{2,1,0:T(1,128)} custom-call(bf16[32,768]{1,0:T(8,128)(2,1)} %bitcast.19, bf16[32,768]{1,0:T(8,128)(2,1)} %copy-done.5, bf16[2048,768]{1,0:T(8,128)(2,1)} %get-tuple-element.11.lv_ref, s32[2,1,1024]{2,1,0:T(1,128)} %bitcast.21), custom_call_target="tpu_custom_call" | custom-call | flops 201326592 | bytes 3145728 | tf_op jit(solution)/shard_map/second_pass/pallas_call | solution.py:306
  150.0 6.4 %all-to-all-start.4 = ((f32[64,1,384]{2,1,0:T(1,128)}), f32[64,1,384]{2,1,0:T(1,128)S(1)}, u32[]{:S(2)}, u32[]{:S(2)}) async-start(f32[64,1,384]{2,1,0:T(1,128)} %second_pass.1), calls=%async_computation.4 | async-start | bytes 196608 | tf_op jit(solution)/shard_map/all_to_all | solution.py:374
  157.2 6.9 %sub_pass.1 = (bf16[256,768]{1,0:T(8,128)(2,1)}, bf16[256,768]{1,0:T(8,128)(2,1)}) custom-call(bf16[2048,768]{1,0:T(8,128)(2,1)} %get-tuple-element.11.lv_ref, s32[2,1,1024]{2,1,0:T(1,128)} %bitcast.25, bf16[64,768]{1,0:T(8,128)(2,1)} %copy-done.4, bf16[64,768]{1,0:T(8,128)(2,1)} %copy-done.10, bf16[64,768]{1,0:T(8,128)(2,1)} %copy-done.11, ...), custom_call_target="tpu_custom_call" | custom-call | flops 3221225472 | bytes 3145728 | tf_op jit(solution)/shard_map/sub_pass/pallas_call | solution.py:354
  167.2 1.9 collective-permute-start.16
  170.3 2.1 %collective-permute-start.18 = (bf16[72,768]{1,0:T(8,128)(2,1)S(1)}, bf16[72,768]{1,0:T(8,128)(2,1)S(1)}, u32[]{:S(2)}, u32[]{:S(2)}) collective-permute-start(bf16[72,768]{1,0:T(8,128)(2,1)S(1)} %get-tuple-element.48), channel_id=1, source_target_pairs={{0,3},{1,0},{2,1},{3,2},{4,7},{5,4},{6,5},{7,6},{8,11},{9,8},{10,9... | collective-permute-start | bytes 331784 | tf_op jit(solution)/shard_map/ppermute | solution.py:396
  172.4 2.5 %collective-permute-done.16 = bf16[72,768]{1,0:T(8,128)(2,1)S(1)} collective-permute-done((bf16[72,768]{1,0:T(8,128)(2,1)S(1)}, bf16[72,768]{1,0:T(8,128)(2,1)S(1)}, u32[]{:S(2)}, u32[]{:S(2)}) %collective-permute-start.16) | collective-permute-done | bytes 110624 | tf_op jit(solution)/shard_map/ppermute | solution.py:396
  178.0 10.3 %all-to-all-start.5 = ((bf16[64,2,1152]{2,1,0:T(2,128)(2,1)}), bf16[64,2,1152]{2,1,0:T(2,128)(2,1)S(1)}, u32[]{:S(2)}, u32[]{:S(2)}) async-start(bf16[64,2,1152]{2,1,0:T(2,128)(2,1)} %pad_maximum_fusion), calls=%async_computation.5 | async-start | bytes 589824 | tf_op jit(solution)/shard_map/all_to_all | solution.py:374
  188.4 12.2 %all-to-all-done.5 = bf16[64,2,1152]{2,1,0:T(2,128)(2,1)S(1)} async-done(((bf16[64,2,1152]{2,1,0:T(2,128)(2,1)}), bf16[64,2,1152]{2,1,0:T(2,128)(2,1)S(1)}, u32[]{:S(2)}, u32[]{:S(2)}) %all-to-all-start.5) | async-done | bytes 294944 | tf_op jit(solution)/shard_map/all_to_all | solution.py:374
  201.2 3.5 %collective-permute-start.20 = (f32[4,768]{1,0:T(4,128)S(1)}, f32[4,768]{1,0:T(4,128)S(1)}, u32[]{:S(2)}, u32[]{:S(2)}) collective-permute-start(f32[4,768]{1,0:T(4,128)S(1)} %broadcast_multiply_fusion.2), channel_id=1, source_target_pairs={{0,2},{1,3},{2,0},{3,1},{4,6},{5,7},{6,4},{7,5},{8,10},{9,11},{10,... | collective-permute-start | bytes 36872 | tf_op jit(solution)/shard_map/ppermute | solution.py:396
  (139 shorter events, 23.8 us)
Async XLA Ops:
  4.2 52.6 %all-to-all-start = ((bf16[64,8,1664]{2,1,0:T(8,128)(2,1)}), bf16[64,8,1664]{2,1,0:T(8,128)(2,1)S(1)}, u32[]{:S(2)}, u32[]{:S(2)}) async-start(bf16[64,8,1664]{2,1,0:T(8,128)(2,1)} %bitcast.15), calls=%async_computation | async-start | bytes 3407872 | tf_op jit(solution)/shard_map/all_to_all | solution.py:374
  57.0 12.2 %collective-permute-start.1 = (f32[1,384]{1,0:T(1,128)S(1)}, f32[1,384]{1,0:T(1,128)S(1)}, u32[]{:S(2)}, u32[]{:S(2)}) collective-permute-start(f32[1,384]{1,0:T(1,128)S(1)} %reshape.141), channel_id=1, source_target_pairs={{0,2},{1,3},{2,0},{3,1},{4,6},{5,7},{6,4},{7,5},{8,10},{9,11},{10,... | collective-permute-start | bytes 4616 | tf_op jit(solution)/shard_map/ppermute | solution.py:396
  60.2 9.0 %collective-permute-start.2 = (f32[1,384]{1,0:T(1,128)S(1)}, f32[1,384]{1,0:T(1,128)S(1)}, u32[]{:S(2)}, u32[]{:S(2)}) collective-permute-start(f32[1,384]{1,0:T(1,128)S(1)} %reshape.141), channel_id=1, source_target_pairs={{0,1},{1,2},{2,3},{3,0},{4,5},{5,6},{6,7},{7,4},{8,9},{9,10},{10,1... | collective-permute-start | bytes 4616 | tf_op jit(solution)/shard_map/ppermute | solution.py:396
  60.9 8.3 %collective-permute-start.3 = (f32[1,384]{1,0:T(1,128)S(1)}, f32[1,384]{1,0:T(1,128)S(1)}, u32[]{:S(2)}, u32[]{:S(2)}) collective-permute-start(f32[1,384]{1,0:T(1,128)S(1)} %reshape.141), channel_id=1, source_target_pairs={{0,3},{1,0},{2,1},{3,2},{4,7},{5,4},{6,5},{7,6},{8,11},{9,8},{10,9... | collective-permute-start | bytes 4616 | tf_op jit(solution)/shard_map/ppermute | solution.py:396
  69.9 17.7 %all-to-all-start.1 = ((f32[64,1,384]{2,1,0:T(1,128)}), f32[64,1,384]{2,1,0:T(1,128)S(1)}, u32[]{:S(2)}, u32[]{:S(2)}) async-start(f32[64,1,384]{2,1,0:T(1,128)} %broadcast_in_dim.14), calls=%async_computation.1 | async-start | bytes 196608 | tf_op jit(solution)/shard_map/all_to_all | solution.py:374
  87.5 5.7 %collective-permute-start = (bf16[256,768]{1,0:T(8,128)(2,1)}, bf16[256,768]{1,0:T(8,128)(2,1)S(1)}, u32[]{:S(2)}, u32[]{:S(2)}) collective-permute-start(bf16[256,768]{1,0:T(8,128)(2,1)} %get-tuple-element.16), channel_id=1, source_target_pairs={{0,4},{4,0},{8,12},{12,8},{16,20},{20,16},{24,28},{28,24},{32,36},... | collective-permute-start | bytes 1179656 | tf_op jit(solution)/shard_map/ppermute | solution.py:387
  94.1 8.3 %collective-permute-start.4 = (bf16[96,768]{1,0:T(8,128)(2,1)S(1)}, bf16[96,768]{1,0:T(8,128)(2,1)S(1)}, u32[]{:S(2)}, u32[]{:S(2)}) collective-permute-start(bf16[96,768]{1,0:T(8,128)(2,1)S(1)} %get-tuple-element.43), channel_id=1, source_target_pairs={{0,2},{1,3},{2,0},{3,1},{4,6},{5,7},{6,4},{7,5},{8,10},{9,11},{10,... | collective-permute-start | bytes 442376 | tf_op jit(solution)/shard_map/ppermute | solution.py:396
  94.2 10.7 %collective-permute-start.5 = (bf16[96,768]{1,0:T(8,128)(2,1)S(1)}, bf16[96,768]{1,0:T(8,128)(2,1)S(1)}, u32[]{:S(2)}, u32[]{:S(2)}) collective-permute-start(bf16[96,768]{1,0:T(8,128)(2,1)S(1)} %get-tuple-element.44), channel_id=1, source_target_pairs={{0,1},{1,2},{2,3},{3,0},{4,5},{5,6},{6,7},{7,4},{8,9},{9,10},{10,1... | collective-permute-start | bytes 442376 | tf_op jit(solution)/shard_map/ppermute | solution.py:396
  95.0 9.9 %collective-permute-start.6 = (bf16[96,768]{1,0:T(8,128)(2,1)S(1)}, bf16[96,768]{1,0:T(8,128)(2,1)S(1)}, u32[]{:S(2)}, u32[]{:S(2)}) collective-permute-start(bf16[96,768]{1,0:T(8,128)(2,1)S(1)} %get-tuple-element.45), channel_id=1, source_target_pairs={{0,3},{1,0},{2,1},{3,2},{4,7},{5,4},{6,5},{7,6},{8,11},{9,8},{10,9... | collective-permute-start | bytes 442376 | tf_op jit(solution)/shard_map/ppermute | solution.py:396
  139.6 7.3 %collective-permute-start.10 = (bf16[64,768]{1,0:T(8,128)(2,1)S(1)}, bf16[64,768]{1,0:T(8,128)(2,1)S(1)}, u32[]{:S(2)}, u32[]{:S(2)}) collective-permute-start(bf16[64,768]{1,0:T(8,128)(2,1)S(1)} %reshape.147.rest_0_), channel_id=1, source_target_pairs={{0,1},{1,2},{2,3},{3,0},{4,5},{5,6},{6,7},{7,4},{8,9},{9,10},{10,1... | collective-permute-start | bytes 294920 | tf_op jit(solution)/shard_map/ppermute | solution.py:396
  139.6 7.4 %collective-permute-start.8 = (bf16[64,768]{1,0:T(8,128)(2,1)S(1)}, bf16[64,768]{1,0:T(8,128)(2,1)S(1)}, u32[]{:S(2)}, u32[]{:S(2)}) collective-permute-start(bf16[64,768]{1,0:T(8,128)(2,1)S(1)} %reshape.147.rest_0_), channel_id=1, source_target_pairs={{0,3},{1,0},{2,1},{3,2},{4,7},{5,4},{6,5},{7,6},{8,11},{9,8},{10,9... | collective-permute-start | bytes 294920 | tf_op jit(solution)/shard_map/ppermute | solution.py:396
  142.9 6.1 %collective-permute-start.9 = (bf16[64,768]{1,0:T(8,128)(2,1)S(1)}, bf16[64,768]{1,0:T(8,128)(2,1)S(1)}, u32[]{:S(2)}, u32[]{:S(2)}) collective-permute-start(bf16[64,768]{1,0:T(8,128)(2,1)S(1)} %reshape.147.rest_0_), channel_id=1, source_target_pairs={{0,2},{1,3},{2,0},{3,1},{4,6},{5,7},{6,4},{7,5},{8,10},{9,11},{10,... | collective-permute-start | bytes 294920 | tf_op jit(solution)/shard_map/ppermute | solution.py:396
  149.0 7.5 %collective-permute-start.11 = (bf16[64,768]{1,0:T(8,128)(2,1)S(1)}, bf16[64,768]{1,0:T(8,128)(2,1)S(1)}, u32[]{:S(2)}, u32[]{:S(2)}) collective-permute-start(bf16[64,768]{1,0:T(8,128)(2,1)S(1)} %reshape.147.rest_0_), channel_id=1, source_target_pairs={{0,4},{4,0},{8,12},{12,8},{16,20},{20,16},{24,28},{28,24},{32,36},... | collective-permute-start | bytes 294920 | tf_op jit(solution)/shard_map/ppermute | solution.py:387
  149.0 7.5 %collective-permute-start.12 = (bf16[64,768]{1,0:T(8,128)(2,1)S(1)}, bf16[64,768]{1,0:T(8,128)(2,1)S(1)}, u32[]{:S(2)}, u32[]{:S(2)}) collective-permute-start(bf16[64,768]{1,0:T(8,128)(2,1)S(1)} %collective-permute-done.8.rest_1_), channel_id=1, source_target_pairs={{0,4},{4,0},{8,12},{12,8},{16,20},{20,16},{24,28},{28,24},{32,36},... | collective-permute-start | bytes 294920 | tf_op jit(solution)/shard_map/ppermute | solution.py:387
  149.5 7.0 %collective-permute-start.13 = (bf16[64,768]{1,0:T(8,128)(2,1)S(1)}, bf16[64,768]{1,0:T(8,128)(2,1)S(1)}, u32[]{:S(2)}, u32[]{:S(2)}) collective-permute-start(bf16[64,768]{1,0:T(8,128)(2,1)S(1)} %collective-permute-done.9.rest_2_), channel_id=1, source_target_pairs={{0,4},{4,0},{8,12},{12,8},{16,20},{20,16},{24,28},{28,24},{32,36},... | collective-permute-start | bytes 294920 | tf_op jit(solution)/shard_map/ppermute | solution.py:387
  149.5 7.0 %collective-permute-start.14 = (bf16[64,768]{1,0:T(8,128)(2,1)S(1)}, bf16[64,768]{1,0:T(8,128)(2,1)S(1)}, u32[]{:S(2)}, u32[]{:S(2)}) collective-permute-start(bf16[64,768]{1,0:T(8,128)(2,1)S(1)} %collective-permute-done.10.rest_3_), channel_id=1, source_target_pairs={{0,4},{4,0},{8,12},{12,8},{16,20},{20,16},{24,28},{28,24},{32,36},... | collective-permute-start | bytes 294920 | tf_op jit(solution)/shard_map/ppermute | solution.py:387
  150.0 14.7 %all-to-all-start.4 = ((f32[64,1,384]{2,1,0:T(1,128)}), f32[64,1,384]{2,1,0:T(1,128)S(1)}, u32[]{:S(2)}, u32[]{:S(2)}) async-start(f32[64,1,384]{2,1,0:T(1,128)} %second_pass.1), calls=%async_computation.4 | async-start | bytes 196608 | tf_op jit(solution)/shard_map/all_to_all | solution.py:374
  167.2 7.7 %collective-permute-start.16 = (bf16[72,768]{1,0:T(8,128)(2,1)S(1)}, bf16[72,768]{1,0:T(8,128)(2,1)S(1)}, u32[]{:S(2)}, u32[]{:S(2)}) collective-permute-start(bf16[72,768]{1,0:T(8,128)(2,1)S(1)} %get-tuple-element.46), channel_id=1, source_target_pairs={{0,2},{1,3},{2,0},{3,1},{4,6},{5,7},{6,4},{7,5},{8,10},{9,11},{10,... | collective-permute-start | bytes 331784 | tf_op jit(solution)/shard_map/ppermute | solution.py:396
  169.2 7.4 %collective-permute-start.17 = (bf16[72,768]{1,0:T(8,128)(2,1)S(1)}, bf16[72,768]{1,0:T(8,128)(2,1)S(1)}, u32[]{:S(2)}, u32[]{:S(2)}) collective-permute-start(bf16[72,768]{1,0:T(8,128)(2,1)S(1)} %get-tuple-element.47), channel_id=1, source_target_pairs={{0,1},{1,2},{2,3},{3,0},{4,5},{5,6},{6,7},{7,4},{8,9},{9,10},{10,1... | collective-permute-start | bytes 331784 | tf_op jit(solution)/shard_map/ppermute | solution.py:396
  170.3 6.3 %collective-permute-start.18 = (bf16[72,768]{1,0:T(8,128)(2,1)S(1)}, bf16[72,768]{1,0:T(8,128)(2,1)S(1)}, u32[]{:S(2)}, u32[]{:S(2)}) collective-permute-start(bf16[72,768]{1,0:T(8,128)(2,1)S(1)} %get-tuple-element.48), channel_id=1, source_target_pairs={{0,3},{1,0},{2,1},{3,2},{4,7},{5,4},{6,5},{7,6},{8,11},{9,8},{10,9... | collective-permute-start | bytes 331784 | tf_op jit(solution)/shard_map/ppermute | solution.py:396
  178.0 22.6 %all-to-all-start.5 = ((bf16[64,2,1152]{2,1,0:T(2,128)(2,1)}), bf16[64,2,1152]{2,1,0:T(2,128)(2,1)S(1)}, u32[]{:S(2)}, u32[]{:S(2)}) async-start(bf16[64,2,1152]{2,1,0:T(2,128)(2,1)} %pad_maximum_fusion), calls=%async_computation.5 | async-start | bytes 589824 | tf_op jit(solution)/shard_map/all_to_all | solution.py:374
  201.1 6.1 %collective-permute-start.19 = (f32[4,768]{1,0:T(4,128)S(1)}, f32[4,768]{1,0:T(4,128)S(1)}, u32[]{:S(2)}, u32[]{:S(2)}) collective-permute-start(f32[4,768]{1,0:T(4,128)S(1)} %broadcast_multiply_fusion.2), channel_id=1, source_target_pairs={{0,1},{1,2},{2,3},{3,0},{4,5},{5,6},{6,7},{7,4},{8,9},{9,10},{10,1... | collective-permute-start | bytes 36872 | tf_op jit(solution)/shard_map/ppermute | solution.py:396
  201.2 5.9 %collective-permute-start.20 = (f32[4,768]{1,0:T(4,128)S(1)}, f32[4,768]{1,0:T(4,128)S(1)}, u32[]{:S(2)}, u32[]{:S(2)}) collective-permute-start(f32[4,768]{1,0:T(4,128)S(1)} %broadcast_multiply_fusion.2), channel_id=1, source_target_pairs={{0,2},{1,3},{2,0},{3,1},{4,6},{5,7},{6,4},{7,5},{8,10},{9,11},{10,... | collective-permute-start | bytes 36872 | tf_op jit(solution)/shard_map/ppermute | solution.py:396
  204.7 3.7 %collective-permute-start.21 = (f32[4,768]{1,0:T(4,128)S(1)}, f32[4,768]{1,0:T(4,128)S(1)}, u32[]{:S(2)}, u32[]{:S(2)}) collective-permute-start(f32[4,768]{1,0:T(4,128)S(1)} %broadcast_multiply_fusion.2), channel_id=1, source_target_pairs={{0,3},{1,0},{2,1},{3,2},{4,7},{5,4},{6,5},{7,6},{8,11},{9,8},{10,9... | collective-permute-start | bytes 36872 | tf_op jit(solution)/shard_map/ppermute | solution.py:396
  (18 other events, 99.3 us)

commit v6 on v5

--- a/solution.py
+++ b/solution.py
@@ -441,7 +441,14 @@
     seed_piece = (seed_piece[:each] + seed_piece[each : 2 * each]).reshape(1, piece)
     seed_piece = grp_sum(seed_piece)
     counts = label_counts(received, slots, lab_dev)
-    seed_sums = to_all(spread(seed_piece, n_wide))
+    seed_piece, _ = lax.optimization_barrier((seed_piece, counts))
+    theirs = core_swap(seed_piece)
+    mine_first = lax.rem(lax.axis_index("wide"), 2) == 0
+    seed_row = jnp.concatenate(
+        [jnp.where(mine_first, seed_piece, theirs), jnp.where(mine_first, theirs, seed_piece)],
+        axis=1,
+    )
+    seed_sums = to_chips(spread(seed_row, n_wide // 2))
 
     me_core = lax.rem(lax.axis_index("wide"), 2)
     second = coarse_second.reshape(lab_dev)

time: 210 us -> 207 us (0.986)
  starting transfers between devices: 61.6 us -> 57.9 us
    all_to_all x4 -> x3, starting transfers between devices: 37.4 us -> 29.1 us  [to_all(): lax.all_to_all(blocks, 'wide', split_axis=0, concat_axis=0, tiled=True)]
    all_to_all x0 -> x1, starting transfers between devices: none -> 6.71 us  [to_chips(): lax.all_to_all(blocks, 'wide', split_axis=0, concat_axis=0, axis_index_gr...]
    ppermute x15, starting transfers between devices: 22.7 us -> 19.4 us  [grp_shift(): return lax.ppermute(value, 'grp', [(i, (i + step) % n) for i in range(n)])]
    all_to_all x4 -> x3, waiting for transfers between devices: 52.3 us -> 52.9 us  [to_all(): lax.all_to_all(blocks, 'wide', split_axis=0, concat_axis=0, tiled=True)]
  transfers between devices with their start and end apart: 26 -> 27, of which waited for: 12 -> 13; matrix products, arithmetic and copies ran while one was open for 2% -> 2% of each run, Pallas kernels for 14% -> 14%
where the time goes in v6:
time: 207 us
  waiting for transfers between devices  71.3 us (34%)
  starting transfers between devices  57.9 us (28%)
  Pallas kernels  33.5 us (16%)
  blocking collectives  32.1 us (16%)
  other arithmetic  6.63 us (3%)
  local copies, waits for them, and re-layouts  3.76 us (2%)
    all_to_all x3, waiting for transfers between devices, to_all(): lax.all_to_all(blocks, 'wide', split_axis=0, concat_axis=0, tiled=True)  52.9 us
    all_to_all x2, blocking collectives, to_chips(): lax.all_to_all(blocks, 'wide', split_axis=0, concat_axis=0, axis_index_gr...  32.1 us
    all_to_all x3, starting transfers between devices, to_all(): lax.all_to_all(blocks, 'wide', split_axis=0, concat_axis=0, tiled=True)  29.1 us
    ppermute x15, starting transfers between devices, grp_shift(): return lax.ppermute(value, 'grp', [(i, (i + step) % n) for i in range(n)])  19.4 us
    ppermute x15, waiting for transfers between devices, grp_shift(): return lax.ppermute(value, 'grp', [(i, (i + step) % n) for i in range(n)])  15.9 us
    pallas_call x1, Pallas kernels, label_pass(): pl.pallas_call(label_kernel, grid=(tiles + 1,), in_specs=[pl.BlockSpec((t...  9.17 us
    pallas_call x1, Pallas kernels, weighted_sums(): pl.pallas_call(functools.partial(pass_kernel, len(centroids)), grid=(tile...  6.88 us
    all_to_all x1, starting transfers between devices, to_chips(): lax.all_to_all(blocks, 'wide', split_axis=0, concat_axis=0, axis_index_gr...  6.71 us
  transfers between devices with their start and end apart: 27, of which 13 were waited for; matrix products, arithmetic and copies ran while one was open for 2% of the time, Pallas kernels for 14%

profile of v6, /device:TPU:6, one launch (start us, length us, event | category | flops | bytes accessed | tf_op | source)
XLA Modules:
  0.0 206.6 jit_solution(9706153629082960965)
XLA Ops:
  0.6 3.6 %sender.1 = bf16[512,1664]{1,0:T(8,128)(2,1)} custom-call(s32[8,1024]{1,0:T(8,128)} %bitcast.25, bf16[1024,768]{1,0:T(8,128)(2,1)} %rows_ref.1, s32[1,32]{1,0:T(1,128)} %bitcast.31), custom_call_target="tpu_custom_call" | custom-call | tf_op jit(solution)/shard_map/sender/pallas_call | solution.py:96
  4.2 12.3 %all-to-all-start = ((bf16[64,8,1664]{2,1,0:T(8,128)(2,1)}), bf16[64,8,1664]{2,1,0:T(8,128)(2,1)S(1)}, u32[]{:S(2)}, u32[]{:S(2)}) async-start(bf16[64,8,1664]{2,1,0:T(8,128)(2,1)} %bitcast.20), calls=%async_computation | async-start | bytes 3407872 | tf_op jit(solution)/shard_map/all_to_all | solution.py:374
  16.6 40.3 %all-to-all-done = bf16[64,8,1664]{2,1,0:T(8,128)(2,1)S(1)} async-done(((bf16[64,8,1664]{2,1,0:T(8,128)(2,1)}), bf16[64,8,1664]{2,1,0:T(8,128)(2,1)S(1)}, u32[]{:S(2)}, u32[]{:S(2)}) %all-to-all-start) | async-done | bytes 1703968 | tf_op jit(solution)/shard_map/all_to_all | solution.py:374
  57.0 1.6 collective-permute-start.2
  58.6 1.7 collective-permute-start.3
  60.3 2.0 collective-permute-start.1
  62.3 5.7 %label_counts.1.counts_ref = bf16[2048,1024]{1,0:T(8,128)(2,1)} custom-call(bf16[512,1664]{1,0:T(8,128)(2,1)} %bitcast.18), custom_call_target="tpu_custom_call" | custom-call | flops 50331648 | bytes 4194304 | tf_op jit(solution)/shard_map/label_counts/pallas_call | solution.py:134
  71.1 6.7 %all-to-all-start.1 = ((f32[32,1,768]{2,1,0:T(1,128)}), f32[32,1,768]{2,1,0:T(1,128)S(1)}, u32[]{:S(2)}, u32[]{:S(2)}) async-start(f32[32,1,768]{2,1,0:T(1,128)} %broadcast_in_dim.14), calls=%async_computation.1 | async-start | bytes 196608 | tf_op jit(solution)/shard_map/all_to_all | solution.py:380
  77.8 9.2 %label_pass.1 = (bf16[2048,768]{1,0:T(8,128)(2,1)}, bf16[256,768]{1,0:T(8,128)(2,1)}, bf16[256,768]{1,0:T(8,128)(2,1)}) custom-call(bf16[2048,1024]{1,0:T(8,128)(2,1)} %label_counts.1.counts_ref, bf16[512,1664]{1,0:T(8,128)(2,1)} %bitcast.19, s32[4,1,512]{2,1,0:T(1,128)} %bitcast.29), custom_call_target="tpu_custom_call" | custom-call | flops 4831838208 | bytes 7340032 | tf_op jit(solution)/shard_map/label_pass/pallas_call | solution.py:211
  87.8 4.0 %first_pass.1 = bf16[32,768]{1,0:T(8,128)(2,1)} custom-call(f32[32,768]{1,0:T(8,128)} %bitcast_multiply_fusion.seed_ref, bf16[2048,768]{1,0:T(8,128)(2,1)} %get-tuple-element.12.lv_ref, s32[2,1,1024]{2,1,0:T(1,128)} %bitcast.28), custom_call_target="tpu_custom_call" | custom-call | flops 201326592 | bytes 3145728 | tf_op jit(solution)/shard_map/first_pass/pallas_call | solution.py:259
  94.8 1.5 collective-permute-start.5
  96.3 3.1 %collective-permute-done.7 = bf16[96,768]{1,0:T(8,128)(2,1)S(1)} collective-permute-done((bf16[96,768]{1,0:T(8,128)(2,1)S(1)}, bf16[96,768]{1,0:T(8,128)(2,1)S(1)}, u32[]{:S(2)}, u32[]{:S(2)}) %collective-permute-start.7) | collective-permute-done | bytes 147488 | tf_op jit(solution)/shard_map/ppermute | solution.py:396
  99.4 4.8 %collective-permute-done.6 = bf16[96,768]{1,0:T(8,128)(2,1)S(1)} collective-permute-done((bf16[96,768]{1,0:T(8,128)(2,1)S(1)}, bf16[96,768]{1,0:T(8,128)(2,1)S(1)}, u32[]{:S(2)}, u32[]{:S(2)}) %collective-permute-start.6) | collective-permute-done | bytes 147488 | tf_op jit(solution)/shard_map/ppermute | solution.py:396
  104.5 18.1 %all_to_all.30 = bf16[32,2,1152]{2,1,0:T(2,128)(2,1)S(1)} all-to-all(bf16[32,2,1152]{2,1,0:T(2,128)(2,1)S(1)} %pad_maximum_fusion.5), channel_id=1, replica_groups={{0,8,16,24,32,40,48,56,64,72,80,88,96,104,112,120,128,136,144,152,160,1..., dimensions={0} | all-to-all | bytes 294912 | tf_op jit(solution)/shard_map/all_to_all | solution.py:380
  123.1 14.0 %all_to_all.31 = bf16[32,2,1152]{2,1,0:T(2,128)(2,1)S(1)} all-to-all(bf16[32,2,1152]{2,1,0:T(2,128)(2,1)S(1)} %broadcast_in_dim.15), channel_id=1, replica_groups={{0,8,16,24,32,40,48,56,64,72,80,88,96,104,112,120,128,136,144,152,160,1..., dimensions={0} | all-to-all | bytes 294912 | tf_op jit(solution)/shard_map/all_to_all | solution.py:380
  141.2 4.1 %second_pass.1 = f32[64,1,384]{2,1,0:T(1,128)} custom-call(bf16[32,768]{1,0:T(8,128)(2,1)} %bitcast.24, bf16[32,768]{1,0:T(8,128)(2,1)} %copy-done.5, bf16[2048,768]{1,0:T(8,128)(2,1)} %get-tuple-element.12.lv_ref, s32[2,1,1024]{2,1,0:T(1,128)} %bitcast.26), custom_call_target="tpu_custom_call" | custom-call | flops 201326592 | bytes 3145728 | tf_op jit(solution)/shard_map/second_pass/pallas_call | solution.py:306
  148.4 6.4 %all-to-all-start.4 = ((f32[64,1,384]{2,1,0:T(1,128)}), f32[64,1,384]{2,1,0:T(1,128)S(1)}, u32[]{:S(2)}, u32[]{:S(2)}) async-start(f32[64,1,384]{2,1,0:T(1,128)} %second_pass.1), calls=%async_computation.4 | async-start | bytes 196608 | tf_op jit(solution)/shard_map/all_to_all | solution.py:374
  155.6 6.9 %sub_pass.1 = (bf16[256,768]{1,0:T(8,128)(2,1)}, bf16[256,768]{1,0:T(8,128)(2,1)}) custom-call(bf16[2048,768]{1,0:T(8,128)(2,1)} %get-tuple-element.12.lv_ref, s32[2,1,1024]{2,1,0:T(1,128)} %bitcast.30, bf16[64,768]{1,0:T(8,128)(2,1)} %copy-done.4, bf16[64,768]{1,0:T(8,128)(2,1)} %copy-done.9, bf16[64,768]{1,0:T(8,128)(2,1)} %copy-done.10, ...), custom_call_target="tpu_custom_call" | custom-call | flops 3221225472 | bytes 3145728 | tf_op jit(solution)/shard_map/sub_pass/pallas_call | solution.py:354
  169.1 1.7 collective-permute-done.19
  170.9 4.0 %collective-permute-done.18 = bf16[72,768]{1,0:T(8,128)(2,1)S(1)} collective-permute-done((bf16[72,768]{1,0:T(8,128)(2,1)S(1)}, bf16[72,768]{1,0:T(8,128)(2,1)S(1)}, u32[]{:S(2)}, u32[]{:S(2)}) %collective-permute-start.18) | collective-permute-done | bytes 110624 | tf_op jit(solution)/shard_map/ppermute | solution.py:396
  176.4 10.3 %all-to-all-start.5 = ((bf16[64,2,1152]{2,1,0:T(2,128)(2,1)}), bf16[64,2,1152]{2,1,0:T(2,128)(2,1)S(1)}, u32[]{:S(2)}, u32[]{:S(2)}) async-start(bf16[64,2,1152]{2,1,0:T(2,128)(2,1)} %pad_maximum_fusion), calls=%async_computation.5 | async-start | bytes 589824 | tf_op jit(solution)/shard_map/all_to_all | solution.py:374
  186.7 12.2 %all-to-all-done.5 = bf16[64,2,1152]{2,1,0:T(2,128)(2,1)S(1)} async-done(((bf16[64,2,1152]{2,1,0:T(2,128)(2,1)}), bf16[64,2,1152]{2,1,0:T(2,128)(2,1)S(1)}, u32[]{:S(2)}, u32[]{:S(2)}) %all-to-all-start.5) | async-done | bytes 294944 | tf_op jit(solution)/shard_map/all_to_all | solution.py:374
  199.5 2.5 %collective-permute-start.21 = (f32[4,768]{1,0:T(4,128)S(1)}, f32[4,768]{1,0:T(4,128)S(1)}, u32[]{:S(2)}, u32[]{:S(2)}) collective-permute-start(f32[4,768]{1,0:T(4,128)S(1)} %broadcast_multiply_fusion.1), channel_id=1, source_target_pairs={{0,2},{1,3},{2,0},{3,1},{4,6},{5,7},{6,4},{7,5},{8,10},{9,11},{10,... | collective-permute-start | bytes 36872 | tf_op jit(solution)/shard_map/ppermute | solution.py:396
  202.0 1.7 collective-permute-start.22
  (140 shorter events, 27.0 us)
Async XLA Ops:
  4.2 52.6 %all-to-all-start = ((bf16[64,8,1664]{2,1,0:T(8,128)(2,1)}), bf16[64,8,1664]{2,1,0:T(8,128)(2,1)S(1)}, u32[]{:S(2)}, u32[]{:S(2)}) async-start(bf16[64,8,1664]{2,1,0:T(8,128)(2,1)} %bitcast.20), calls=%async_computation | async-start | bytes 3407872 | tf_op jit(solution)/shard_map/all_to_all | solution.py:374
  57.0 10.9 %collective-permute-start.2 = (f32[1,384]{1,0:T(1,128)S(1)}, f32[1,384]{1,0:T(1,128)S(1)}, u32[]{:S(2)}, u32[]{:S(2)}) collective-permute-start(f32[1,384]{1,0:T(1,128)S(1)} %reshape.140), channel_id=1, source_target_pairs={{0,1},{1,2},{2,3},{3,0},{4,5},{5,6},{6,7},{7,4},{8,9},{9,10},{10,1... | collective-permute-start | bytes 4616 | tf_op jit(solution)/shard_map/ppermute | solution.py:396
  58.6 9.4 %collective-permute-start.3 = (f32[1,384]{1,0:T(1,128)S(1)}, f32[1,384]{1,0:T(1,128)S(1)}, u32[]{:S(2)}, u32[]{:S(2)}) collective-permute-start(f32[1,384]{1,0:T(1,128)S(1)} %reshape.140), channel_id=1, source_target_pairs={{0,3},{1,0},{2,1},{3,2},{4,7},{5,4},{6,5},{7,6},{8,11},{9,8},{10,9... | collective-permute-start | bytes 4616 | tf_op jit(solution)/shard_map/ppermute | solution.py:396
  60.3 7.7 %collective-permute-start.1 = (f32[1,384]{1,0:T(1,128)S(1)}, f32[1,384]{1,0:T(1,128)S(1)}, u32[]{:S(2)}, u32[]{:S(2)}) collective-permute-start(f32[1,384]{1,0:T(1,128)S(1)} %reshape.140), channel_id=1, source_target_pairs={{0,2},{1,3},{2,0},{3,1},{4,6},{5,7},{6,4},{7,5},{8,10},{9,11},{10,... | collective-permute-start | bytes 4616 | tf_op jit(solution)/shard_map/ppermute | solution.py:396
  71.1 15.9 %all-to-all-start.1 = ((f32[32,1,768]{2,1,0:T(1,128)}), f32[32,1,768]{2,1,0:T(1,128)S(1)}, u32[]{:S(2)}, u32[]{:S(2)}) async-start(f32[32,1,768]{2,1,0:T(1,128)} %broadcast_in_dim.14), calls=%async_computation.1 | async-start | bytes 196608 | tf_op jit(solution)/shard_map/all_to_all | solution.py:380
  86.9 4.9 %collective-permute-start = (bf16[256,768]{1,0:T(8,128)(2,1)}, bf16[256,768]{1,0:T(8,128)(2,1)S(1)}, u32[]{:S(2)}, u32[]{:S(2)}) collective-permute-start(bf16[256,768]{1,0:T(8,128)(2,1)} %get-tuple-element.17), channel_id=1, source_target_pairs={{0,4},{4,0},{8,12},{12,8},{16,20},{20,16},{24,28},{28,24},{32,36},... | collective-permute-start | bytes 1179656 | tf_op jit(solution)/shard_map/ppermute | solution.py:387
  92.7 6.7 %collective-permute-start.7 = (bf16[96,768]{1,0:T(8,128)(2,1)S(1)}, bf16[96,768]{1,0:T(8,128)(2,1)S(1)}, u32[]{:S(2)}, u32[]{:S(2)}) collective-permute-start(bf16[96,768]{1,0:T(8,128)(2,1)S(1)} %get-tuple-element.45), channel_id=1, source_target_pairs={{0,3},{1,0},{2,1},{3,2},{4,7},{5,4},{6,5},{7,6},{8,11},{9,8},{10,9... | collective-permute-start | bytes 442376 | tf_op jit(solution)/shard_map/ppermute | solution.py:396
  93.8 10.3 %collective-permute-start.6 = (bf16[96,768]{1,0:T(8,128)(2,1)S(1)}, bf16[96,768]{1,0:T(8,128)(2,1)S(1)}, u32[]{:S(2)}, u32[]{:S(2)}) collective-permute-start(bf16[96,768]{1,0:T(8,128)(2,1)S(1)} %get-tuple-element.44), channel_id=1, source_target_pairs={{0,1},{1,2},{2,3},{3,0},{4,5},{5,6},{6,7},{7,4},{8,9},{9,10},{10,1... | collective-permute-start | bytes 442376 | tf_op jit(solution)/shard_map/ppermute | solution.py:396
  94.8 9.4 %collective-permute-start.5 = (bf16[96,768]{1,0:T(8,128)(2,1)S(1)}, bf16[96,768]{1,0:T(8,128)(2,1)S(1)}, u32[]{:S(2)}, u32[]{:S(2)}) collective-permute-start(bf16[96,768]{1,0:T(8,128)(2,1)S(1)} %get-tuple-element.43), channel_id=1, source_target_pairs={{0,2},{1,3},{2,0},{3,1},{4,6},{5,7},{6,4},{7,5},{8,10},{9,11},{10,... | collective-permute-start | bytes 442376 | tf_op jit(solution)/shard_map/ppermute | solution.py:396
  138.4 6.9 %collective-permute-start.9 = (bf16[64,768]{1,0:T(8,128)(2,1)S(1)}, bf16[64,768]{1,0:T(8,128)(2,1)S(1)}, u32[]{:S(2)}, u32[]{:S(2)}) collective-permute-start(bf16[64,768]{1,0:T(8,128)(2,1)S(1)} %reshape.146.rest_0_), channel_id=1, source_target_pairs={{0,3},{1,0},{2,1},{3,2},{4,7},{5,4},{6,5},{7,6},{8,11},{9,8},{10,9... | collective-permute-start | bytes 294920 | tf_op jit(solution)/shard_map/ppermute | solution.py:396
  139.2 6.8 %collective-permute-start.10 = (bf16[64,768]{1,0:T(8,128)(2,1)S(1)}, bf16[64,768]{1,0:T(8,128)(2,1)S(1)}, u32[]{:S(2)}, u32[]{:S(2)}) collective-permute-start(bf16[64,768]{1,0:T(8,128)(2,1)S(1)} %reshape.146.rest_0_), channel_id=1, source_target_pairs={{0,2},{1,3},{2,0},{3,1},{4,6},{5,7},{6,4},{7,5},{8,10},{9,11},{10,... | collective-permute-start | bytes 294920 | tf_op jit(solution)/shard_map/ppermute | solution.py:396
  139.8 7.6 %collective-permute-start.11 = (bf16[64,768]{1,0:T(8,128)(2,1)S(1)}, bf16[64,768]{1,0:T(8,128)(2,1)S(1)}, u32[]{:S(2)}, u32[]{:S(2)}) collective-permute-start(bf16[64,768]{1,0:T(8,128)(2,1)S(1)} %reshape.146.rest_0_), channel_id=1, source_target_pairs={{0,1},{1,2},{2,3},{3,0},{4,5},{5,6},{6,7},{7,4},{8,9},{9,10},{10,1... | collective-permute-start | bytes 294920 | tf_op jit(solution)/shard_map/ppermute | solution.py:396
  147.4 7.5 %collective-permute-start.12 = (bf16[64,768]{1,0:T(8,128)(2,1)S(1)}, bf16[64,768]{1,0:T(8,128)(2,1)S(1)}, u32[]{:S(2)}, u32[]{:S(2)}) collective-permute-start(bf16[64,768]{1,0:T(8,128)(2,1)S(1)} %reshape.146.rest_0_), channel_id=1, source_target_pairs={{0,4},{4,0},{8,12},{12,8},{16,20},{20,16},{24,28},{28,24},{32,36},... | collective-permute-start | bytes 294920 | tf_op jit(solution)/shard_map/ppermute | solution.py:387
  147.4 7.5 %collective-permute-start.13 = (bf16[64,768]{1,0:T(8,128)(2,1)S(1)}, bf16[64,768]{1,0:T(8,128)(2,1)S(1)}, u32[]{:S(2)}, u32[]{:S(2)}) collective-permute-start(bf16[64,768]{1,0:T(8,128)(2,1)S(1)} %collective-permute-done.9.rest_1_), channel_id=1, source_target_pairs={{0,4},{4,0},{8,12},{12,8},{16,20},{20,16},{24,28},{28,24},{32,36},... | collective-permute-start | bytes 294920 | tf_op jit(solution)/shard_map/ppermute | solution.py:387
  147.9 7.0 %collective-permute-start.14 = (bf16[64,768]{1,0:T(8,128)(2,1)S(1)}, bf16[64,768]{1,0:T(8,128)(2,1)S(1)}, u32[]{:S(2)}, u32[]{:S(2)}) collective-permute-start(bf16[64,768]{1,0:T(8,128)(2,1)S(1)} %collective-permute-done.10.rest_2_), channel_id=1, source_target_pairs={{0,4},{4,0},{8,12},{12,8},{16,20},{20,16},{24,28},{28,24},{32,36},... | collective-permute-start | bytes 294920 | tf_op jit(solution)/shard_map/ppermute | solution.py:387
  147.9 7.0 %collective-permute-start.15 = (bf16[64,768]{1,0:T(8,128)(2,1)S(1)}, bf16[64,768]{1,0:T(8,128)(2,1)S(1)}, u32[]{:S(2)}, u32[]{:S(2)}) collective-permute-start(bf16[64,768]{1,0:T(8,128)(2,1)S(1)} %collective-permute-done.11.rest_3_), channel_id=1, source_target_pairs={{0,4},{4,0},{8,12},{12,8},{16,20},{20,16},{24,28},{28,24},{32,36},... | collective-permute-start | bytes 294920 | tf_op jit(solution)/shard_map/ppermute | solution.py:387
  148.4 14.7 %all-to-all-start.4 = ((f32[64,1,384]{2,1,0:T(1,128)}), f32[64,1,384]{2,1,0:T(1,128)S(1)}, u32[]{:S(2)}, u32[]{:S(2)}) async-start(f32[64,1,384]{2,1,0:T(1,128)} %second_pass.1), calls=%async_computation.4 | async-start | bytes 196608 | tf_op jit(solution)/shard_map/all_to_all | solution.py:374
  165.6 5.2 %collective-permute-start.19 = (bf16[72,768]{1,0:T(8,128)(2,1)S(1)}, bf16[72,768]{1,0:T(8,128)(2,1)S(1)}, u32[]{:S(2)}, u32[]{:S(2)}) collective-permute-start(bf16[72,768]{1,0:T(8,128)(2,1)S(1)} %get-tuple-element.48), channel_id=1, source_target_pairs={{0,3},{1,0},{2,1},{3,2},{4,7},{5,4},{6,5},{7,6},{8,11},{9,8},{10,9... | collective-permute-start | bytes 331784 | tf_op jit(solution)/shard_map/ppermute | solution.py:396
  166.5 8.4 %collective-permute-start.18 = (bf16[72,768]{1,0:T(8,128)(2,1)S(1)}, bf16[72,768]{1,0:T(8,128)(2,1)S(1)}, u32[]{:S(2)}, u32[]{:S(2)}) collective-permute-start(bf16[72,768]{1,0:T(8,128)(2,1)S(1)} %get-tuple-element.47), channel_id=1, source_target_pairs={{0,1},{1,2},{2,3},{3,0},{4,5},{5,6},{6,7},{7,4},{8,9},{9,10},{10,1... | collective-permute-start | bytes 331784 | tf_op jit(solution)/shard_map/ppermute | solution.py:396
  167.7 7.1 %collective-permute-start.17 = (bf16[72,768]{1,0:T(8,128)(2,1)S(1)}, bf16[72,768]{1,0:T(8,128)(2,1)S(1)}, u32[]{:S(2)}, u32[]{:S(2)}) collective-permute-start(bf16[72,768]{1,0:T(8,128)(2,1)S(1)} %get-tuple-element.46), channel_id=1, source_target_pairs={{0,2},{1,3},{2,0},{3,1},{4,6},{5,7},{6,4},{7,5},{8,10},{9,11},{10,... | collective-permute-start | bytes 331784 | tf_op jit(solution)/shard_map/ppermute | solution.py:396
  176.4 22.5 %all-to-all-start.5 = ((bf16[64,2,1152]{2,1,0:T(2,128)(2,1)}), bf16[64,2,1152]{2,1,0:T(2,128)(2,1)S(1)}, u32[]{:S(2)}, u32[]{:S(2)}) async-start(bf16[64,2,1152]{2,1,0:T(2,128)(2,1)} %pad_maximum_fusion), calls=%async_computation.5 | async-start | bytes 589824 | tf_op jit(solution)/shard_map/all_to_all | solution.py:374
  199.5 6.0 %collective-permute-start.20 = (f32[4,768]{1,0:T(4,128)S(1)}, f32[4,768]{1,0:T(4,128)S(1)}, u32[]{:S(2)}, u32[]{:S(2)}) collective-permute-start(f32[4,768]{1,0:T(4,128)S(1)} %broadcast_multiply_fusion.1), channel_id=1, source_target_pairs={{0,1},{1,2},{2,3},{3,0},{4,5},{5,6},{6,7},{7,4},{8,9},{9,10},{10,1... | collective-permute-start | bytes 36872 | tf_op jit(solution)/shard_map/ppermute | solution.py:396
  199.5 6.0 %collective-permute-start.21 = (f32[4,768]{1,0:T(4,128)S(1)}, f32[4,768]{1,0:T(4,128)S(1)}, u32[]{:S(2)}, u32[]{:S(2)}) collective-permute-start(f32[4,768]{1,0:T(4,128)S(1)} %broadcast_multiply_fusion.1), channel_id=1, source_target_pairs={{0,2},{1,3},{2,0},{3,1},{4,6},{5,7},{6,4},{7,5},{8,10},{9,11},{10,... | collective-permute-start | bytes 36872 | tf_op jit(solution)/shard_map/ppermute | solution.py:396
  202.0 3.7 %collective-permute-start.22 = (f32[4,768]{1,0:T(4,128)S(1)}, f32[4,768]{1,0:T(4,128)S(1)}, u32[]{:S(2)}, u32[]{:S(2)}) collective-permute-start(f32[4,768]{1,0:T(4,128)S(1)} %broadcast_multiply_fusion.1), channel_id=1, source_target_pairs={{0,3},{1,0},{2,1},{3,2},{4,7},{5,4},{6,5},{7,6},{8,11},{9,8},{10,9... | collective-permute-start | bytes 36872 | tf_op jit(solution)/shard_map/ppermute | solution.py:396
  (19 other events, 93.6 us)

commit v7 on v6

--- a/solution.py
+++ b/solution.py
@@ -481,14 +481,16 @@
     sub_own = got[:, :, :width].reshape(each, width)
 
     theirs, sub_own = lax.optimization_barrier((core_swap(first), sub_own))
-    m_two = second_pass(first, theirs, label_vectors, second, (n_wide, 1, piece))
-    two_parts = to_all(m_two).reshape(n_wide, piece)
+    m_two = second_pass(first, theirs, label_vectors, second, (chips, 1, width))
+    two_parts = to_chips(m_two).reshape(chips, width)
 
     sub_start = grp_gather(sub_own)
     _, *sub_start = lax.optimization_barrier((m_two, *sub_start))
     sub_start = sub_start + [core_swap(block) for block in sub_start]
     w_own, w_other = weighted_sums(sub_start, label_vectors, sub_ids, 2, BF16, "sub_pass")
-    high, low = halves(jnp.sum(two_parts, axis=0))
+    two_sum = jnp.sum(two_parts, axis=0)
+    two_sum = two_sum + core_swap(two_sum)
+    high, low = halves(jnp.where(me_core == 0, two_sum[:piece], two_sum[piece:]))
     two_row = jnp.concatenate([high, low])[None]
     w_mine = reduced(w_own, w_other, jnp.pad(two_row, ((0, 7), (0, 0))))
     two_piece = w_mine[each, :piece] + w_mine[each, piece:]

time: 207 us -> 207 us (level)
    all_to_all x3 -> x2, starting transfers between devices: 29.1 us -> 22.4 us  [to_all(): lax.all_to_all(blocks, 'wide', split_axis=0, concat_axis=0, tiled=True)]
    all_to_all x1 -> x2, starting transfers between devices: 6.71 us -> 12.4 us  [to_chips(): lax.all_to_all(blocks, 'wide', split_axis=0, concat_axis=0, axis_index_gr...]
    all_to_all x3 -> x2, waiting for transfers between devices: 52.9 us -> 52.5 us  [to_all(): lax.all_to_all(blocks, 'wide', split_axis=0, concat_axis=0, tiled=True)]
  transfers between devices with their start and end apart: 27 -> 28, of which waited for: 13 -> 13; matrix products, arithmetic and copies ran while one was open for 2% -> 2% of each run, Pallas kernels for 14% -> 15%
where the time goes in v7:
time: 207 us; the launch traced here: 206 us
  waiting for transfers between devices  71.5 us (35%)
  starting transfers between devices  57.1 us (28%)
  Pallas kernels  33.5 us (16%)
  blocking collectives  32.1 us (16%)
  other arithmetic  6.61 us (3%)
  local copies, waits for them, and re-layouts  3.77 us (2%)
    all_to_all x2, waiting for transfers between devices, to_all(): lax.all_to_all(blocks, 'wide', split_axis=0, concat_axis=0, tiled=True)  52.5 us
    all_to_all x2, blocking collectives, to_chips(): lax.all_to_all(blocks, 'wide', split_axis=0, concat_axis=0, axis_index_gr...  32.1 us
    all_to_all x2, starting transfers between devices, to_all(): lax.all_to_all(blocks, 'wide', split_axis=0, concat_axis=0, tiled=True)  22.4 us
    ppermute x15, starting transfers between devices, grp_shift(): return lax.ppermute(value, 'grp', [(i, (i + step) % n) for i in range(n)])  19.5 us
    ppermute x15, waiting for transfers between devices, grp_shift(): return lax.ppermute(value, 'grp', [(i, (i + step) % n) for i in range(n)])  15.9 us
    all_to_all x2, starting transfers between devices, to_chips(): lax.all_to_all(blocks, 'wide', split_axis=0, concat_axis=0, axis_index_gr...  12.4 us
    pallas_call x1, Pallas kernels, label_pass(): pl.pallas_call(label_kernel, grid=(tiles + 1,), in_specs=[pl.BlockSpec((t...  9.17 us
    pallas_call x1, Pallas kernels, weighted_sums(): pl.pallas_call(functools.partial(pass_kernel, len(centroids)), grid=(tile...  6.89 us
  transfers between devices with their start and end apart: 28, of which 13 were waited for; matrix products, arithmetic and copies ran while one was open for 2% of the time, Pallas kernels for 15%

profile of v7, /device:TPU:6, one launch (start us, length us, event | category | flops | bytes accessed | tf_op | source)
XLA Modules:
  0.0 205.9 jit_solution(9718405779882701868)
XLA Ops:
  0.6 3.6 %sender.1 = bf16[512,1664]{1,0:T(8,128)(2,1)} custom-call(s32[8,1024]{1,0:T(8,128)} %bitcast.25, bf16[1024,768]{1,0:T(8,128)(2,1)} %rows_ref.1, s32[1,32]{1,0:T(1,128)} %bitcast.31), custom_call_target="tpu_custom_call" | custom-call | tf_op jit(solution)/shard_map/sender/pallas_call | solution.py:96
  4.2 12.3 %all-to-all-start = ((bf16[64,8,1664]{2,1,0:T(8,128)(2,1)}), bf16[64,8,1664]{2,1,0:T(8,128)(2,1)S(1)}, u32[]{:S(2)}, u32[]{:S(2)}) async-start(bf16[64,8,1664]{2,1,0:T(8,128)(2,1)} %bitcast.20), calls=%async_computation | async-start | bytes 3407872 | tf_op jit(solution)/shard_map/all_to_all | solution.py:374
  16.6 40.3 %all-to-all-done = bf16[64,8,1664]{2,1,0:T(8,128)(2,1)S(1)} async-done(((bf16[64,8,1664]{2,1,0:T(8,128)(2,1)}), bf16[64,8,1664]{2,1,0:T(8,128)(2,1)S(1)}, u32[]{:S(2)}, u32[]{:S(2)}) %all-to-all-start) | async-done | bytes 1703968 | tf_op jit(solution)/shard_map/all_to_all | solution.py:374
  57.0 1.6 collective-permute-start.2
  58.6 1.7 collective-permute-start.3
  60.3 2.0 collective-permute-start.1
  62.3 5.7 %label_counts.1.counts_ref = bf16[2048,1024]{1,0:T(8,128)(2,1)} custom-call(bf16[512,1664]{1,0:T(8,128)(2,1)} %bitcast.18), custom_call_target="tpu_custom_call" | custom-call | flops 50331648 | bytes 4194304 | tf_op jit(solution)/shard_map/label_counts/pallas_call | solution.py:134
  71.1 6.7 %all-to-all-start.1 = ((f32[32,1,768]{2,1,0:T(1,128)}), f32[32,1,768]{2,1,0:T(1,128)S(1)}, u32[]{:S(2)}, u32[]{:S(2)}) async-start(f32[32,1,768]{2,1,0:T(1,128)} %broadcast_in_dim.14), calls=%async_computation.1 | async-start | bytes 196608 | tf_op jit(solution)/shard_map/all_to_all | solution.py:380
  77.8 9.2 %label_pass.1 = (bf16[2048,768]{1,0:T(8,128)(2,1)}, bf16[256,768]{1,0:T(8,128)(2,1)}, bf16[256,768]{1,0:T(8,128)(2,1)}) custom-call(bf16[2048,1024]{1,0:T(8,128)(2,1)} %label_counts.1.counts_ref, bf16[512,1664]{1,0:T(8,128)(2,1)} %bitcast.19, s32[4,1,512]{2,1,0:T(1,128)} %bitcast.29), custom_call_target="tpu_custom_call" | custom-call | flops 4831838208 | bytes 7340032 | tf_op jit(solution)/shard_map/label_pass/pallas_call | solution.py:211
  87.8 4.0 %first_pass.1 = bf16[32,768]{1,0:T(8,128)(2,1)} custom-call(f32[32,768]{1,0:T(8,128)} %bitcast_multiply_fusion.seed_ref, bf16[2048,768]{1,0:T(8,128)(2,1)} %get-tuple-element.12.lv_ref, s32[2,1,1024]{2,1,0:T(1,128)} %bitcast.28), custom_call_target="tpu_custom_call" | custom-call | flops 201326592 | bytes 3145728 | tf_op jit(solution)/shard_map/first_pass/pallas_call | solution.py:259
  94.8 1.5 collective-permute-start.5
  96.3 3.1 %collective-permute-done.7 = bf16[96,768]{1,0:T(8,128)(2,1)S(1)} collective-permute-done((bf16[96,768]{1,0:T(8,128)(2,1)S(1)}, bf16[96,768]{1,0:T(8,128)(2,1)S(1)}, u32[]{:S(2)}, u32[]{:S(2)}) %collective-permute-start.7) | collective-permute-done | bytes 147488 | tf_op jit(solution)/shard_map/ppermute | solution.py:396
  99.4 4.7 %collective-permute-done.6 = bf16[96,768]{1,0:T(8,128)(2,1)S(1)} collective-permute-done((bf16[96,768]{1,0:T(8,128)(2,1)S(1)}, bf16[96,768]{1,0:T(8,128)(2,1)S(1)}, u32[]{:S(2)}, u32[]{:S(2)}) %collective-permute-start.6) | collective-permute-done | bytes 147488 | tf_op jit(solution)/shard_map/ppermute | solution.py:396
  104.5 18.1 %all_to_all.30 = bf16[32,2,1152]{2,1,0:T(2,128)(2,1)S(1)} all-to-all(bf16[32,2,1152]{2,1,0:T(2,128)(2,1)S(1)} %pad_maximum_fusion.5), channel_id=1, replica_groups={{0,8,16,24,32,40,48,56,64,72,80,88,96,104,112,120,128,136,144,152,160,1..., dimensions={0} | all-to-all | bytes 294912 | tf_op jit(solution)/shard_map/all_to_all | solution.py:380
  123.1 14.0 %all_to_all.31 = bf16[32,2,1152]{2,1,0:T(2,128)(2,1)S(1)} all-to-all(bf16[32,2,1152]{2,1,0:T(2,128)(2,1)S(1)} %broadcast_in_dim.15), channel_id=1, replica_groups={{0,8,16,24,32,40,48,56,64,72,80,88,96,104,112,120,128,136,144,152,160,1..., dimensions={0} | all-to-all | bytes 294912 | tf_op jit(solution)/shard_map/all_to_all | solution.py:380
  141.2 4.1 %second_pass.1 = f32[32,1,768]{2,1,0:T(1,128)} custom-call(bf16[32,768]{1,0:T(8,128)(2,1)} %bitcast.24, bf16[32,768]{1,0:T(8,128)(2,1)} %copy-done.5, bf16[2048,768]{1,0:T(8,128)(2,1)} %get-tuple-element.12.lv_ref, s32[2,1,1024]{2,1,0:T(1,128)} %bitcast.26), custom_call_target="tpu_custom_call" | custom-call | flops 201326592 | bytes 3145728 | tf_op jit(solution)/shard_map/second_pass/pallas_call | solution.py:306
  148.4 5.7 %all-to-all-start.4 = ((f32[32,1,768]{2,1,0:T(1,128)}), f32[32,1,768]{2,1,0:T(1,128)S(1)}, u32[]{:S(2)}, u32[]{:S(2)}) async-start(f32[32,1,768]{2,1,0:T(1,128)} %second_pass.1), calls=%async_computation.4 | async-start | bytes 196608 | tf_op jit(solution)/shard_map/all_to_all | solution.py:380
  155.0 6.9 %sub_pass.1 = (bf16[256,768]{1,0:T(8,128)(2,1)}, bf16[256,768]{1,0:T(8,128)(2,1)}) custom-call(bf16[2048,768]{1,0:T(8,128)(2,1)} %get-tuple-element.12.lv_ref, s32[2,1,1024]{2,1,0:T(1,128)} %bitcast.30, bf16[64,768]{1,0:T(8,128)(2,1)} %copy-done.4, bf16[64,768]{1,0:T(8,128)(2,1)} %copy-done.9, bf16[64,768]{1,0:T(8,128)(2,1)} %copy-done.10, ...), custom_call_target="tpu_custom_call" | custom-call | flops 3221225472 | bytes 3145728 | tf_op jit(solution)/shard_map/sub_pass/pallas_call | solution.py:354
  168.7 1.6 collective-permute-done.20
  170.2 4.2 %collective-permute-done.19 = bf16[72,768]{1,0:T(8,128)(2,1)S(1)} collective-permute-done((bf16[72,768]{1,0:T(8,128)(2,1)S(1)}, bf16[72,768]{1,0:T(8,128)(2,1)S(1)}, u32[]{:S(2)}, u32[]{:S(2)}) %collective-permute-start.19) | collective-permute-done | bytes 110624 | tf_op jit(solution)/shard_map/ppermute | solution.py:396
  175.9 10.1 %all-to-all-start.5 = ((bf16[64,2,1152]{2,1,0:T(2,128)(2,1)}), bf16[64,2,1152]{2,1,0:T(2,128)(2,1)S(1)}, u32[]{:S(2)}, u32[]{:S(2)}) async-start(bf16[64,2,1152]{2,1,0:T(2,128)(2,1)} %pad_maximum_fusion), calls=%async_computation.5 | async-start | bytes 589824 | tf_op jit(solution)/shard_map/all_to_all | solution.py:374
  186.1 12.2 %all-to-all-done.5 = bf16[64,2,1152]{2,1,0:T(2,128)(2,1)S(1)} async-done(((bf16[64,2,1152]{2,1,0:T(2,128)(2,1)}), bf16[64,2,1152]{2,1,0:T(2,128)(2,1)S(1)}, u32[]{:S(2)}, u32[]{:S(2)}) %all-to-all-start.5) | async-done | bytes 294944 | tf_op jit(solution)/shard_map/all_to_all | solution.py:374
  198.8 2.6 %collective-permute-start.22 = (f32[4,768]{1,0:T(4,128)S(1)}, f32[4,768]{1,0:T(4,128)S(1)}, u32[]{:S(2)}, u32[]{:S(2)}) collective-permute-start(f32[4,768]{1,0:T(4,128)S(1)} %broadcast_multiply_fusion.1), channel_id=1, source_target_pairs={{0,2},{1,3},{2,0},{3,1},{4,6},{5,7},{6,4},{7,5},{8,10},{9,11},{10,... | collective-permute-start | bytes 36872 | tf_op jit(solution)/shard_map/ppermute | solution.py:396
  201.4 1.6 collective-permute-start.23
  (143 shorter events, 27.2 us)
Async XLA Ops:
  4.2 52.6 %all-to-all-start = ((bf16[64,8,1664]{2,1,0:T(8,128)(2,1)}), bf16[64,8,1664]{2,1,0:T(8,128)(2,1)S(1)}, u32[]{:S(2)}, u32[]{:S(2)}) async-start(bf16[64,8,1664]{2,1,0:T(8,128)(2,1)} %bitcast.20), calls=%async_computation | async-start | bytes 3407872 | tf_op jit(solution)/shard_map/all_to_all | solution.py:374
  57.0 10.9 %collective-permute-start.2 = (f32[1,384]{1,0:T(1,128)S(1)}, f32[1,384]{1,0:T(1,128)S(1)}, u32[]{:S(2)}, u32[]{:S(2)}) collective-permute-start(f32[1,384]{1,0:T(1,128)S(1)} %reshape.140), channel_id=1, source_target_pairs={{0,1},{1,2},{2,3},{3,0},{4,5},{5,6},{6,7},{7,4},{8,9},{9,10},{10,1... | collective-permute-start | bytes 4616 | tf_op jit(solution)/shard_map/ppermute | solution.py:396
  58.6 9.4 %collective-permute-start.3 = (f32[1,384]{1,0:T(1,128)S(1)}, f32[1,384]{1,0:T(1,128)S(1)}, u32[]{:S(2)}, u32[]{:S(2)}) collective-permute-start(f32[1,384]{1,0:T(1,128)S(1)} %reshape.140), channel_id=1, source_target_pairs={{0,3},{1,0},{2,1},{3,2},{4,7},{5,4},{6,5},{7,6},{8,11},{9,8},{10,9... | collective-permute-start | bytes 4616 | tf_op jit(solution)/shard_map/ppermute | solution.py:396
  60.3 7.7 %collective-permute-start.1 = (f32[1,384]{1,0:T(1,128)S(1)}, f32[1,384]{1,0:T(1,128)S(1)}, u32[]{:S(2)}, u32[]{:S(2)}) collective-permute-start(f32[1,384]{1,0:T(1,128)S(1)} %reshape.140), channel_id=1, source_target_pairs={{0,2},{1,3},{2,0},{3,1},{4,6},{5,7},{6,4},{7,5},{8,10},{9,11},{10,... | collective-permute-start | bytes 4616 | tf_op jit(solution)/shard_map/ppermute | solution.py:396
  71.1 15.9 %all-to-all-start.1 = ((f32[32,1,768]{2,1,0:T(1,128)}), f32[32,1,768]{2,1,0:T(1,128)S(1)}, u32[]{:S(2)}, u32[]{:S(2)}) async-start(f32[32,1,768]{2,1,0:T(1,128)} %broadcast_in_dim.14), calls=%async_computation.1 | async-start | bytes 196608 | tf_op jit(solution)/shard_map/all_to_all | solution.py:380
  86.9 4.9 %collective-permute-start = (bf16[256,768]{1,0:T(8,128)(2,1)}, bf16[256,768]{1,0:T(8,128)(2,1)S(1)}, u32[]{:S(2)}, u32[]{:S(2)}) collective-permute-start(bf16[256,768]{1,0:T(8,128)(2,1)} %get-tuple-element.17), channel_id=1, source_target_pairs={{0,4},{4,0},{8,12},{12,8},{16,20},{20,16},{24,28},{28,24},{32,36},... | collective-permute-start | bytes 1179656 | tf_op jit(solution)/shard_map/ppermute | solution.py:387
  92.7 6.7 %collective-permute-start.7 = (bf16[96,768]{1,0:T(8,128)(2,1)S(1)}, bf16[96,768]{1,0:T(8,128)(2,1)S(1)}, u32[]{:S(2)}, u32[]{:S(2)}) collective-permute-start(bf16[96,768]{1,0:T(8,128)(2,1)S(1)} %get-tuple-element.45), channel_id=1, source_target_pairs={{0,3},{1,0},{2,1},{3,2},{4,7},{5,4},{6,5},{7,6},{8,11},{9,8},{10,9... | collective-permute-start | bytes 442376 | tf_op jit(solution)/shard_map/ppermute | solution.py:396
  93.8 10.3 %collective-permute-start.6 = (bf16[96,768]{1,0:T(8,128)(2,1)S(1)}, bf16[96,768]{1,0:T(8,128)(2,1)S(1)}, u32[]{:S(2)}, u32[]{:S(2)}) collective-permute-start(bf16[96,768]{1,0:T(8,128)(2,1)S(1)} %get-tuple-element.44), channel_id=1, source_target_pairs={{0,1},{1,2},{2,3},{3,0},{4,5},{5,6},{6,7},{7,4},{8,9},{9,10},{10,1... | collective-permute-start | bytes 442376 | tf_op jit(solution)/shard_map/ppermute | solution.py:396
  94.8 9.4 %collective-permute-start.5 = (bf16[96,768]{1,0:T(8,128)(2,1)S(1)}, bf16[96,768]{1,0:T(8,128)(2,1)S(1)}, u32[]{:S(2)}, u32[]{:S(2)}) collective-permute-start(bf16[96,768]{1,0:T(8,128)(2,1)S(1)} %get-tuple-element.43), channel_id=1, source_target_pairs={{0,2},{1,3},{2,0},{3,1},{4,6},{5,7},{6,4},{7,5},{8,10},{9,11},{10,... | collective-permute-start | bytes 442376 | tf_op jit(solution)/shard_map/ppermute | solution.py:396
  138.4 6.9 %collective-permute-start.9 = (bf16[64,768]{1,0:T(8,128)(2,1)S(1)}, bf16[64,768]{1,0:T(8,128)(2,1)S(1)}, u32[]{:S(2)}, u32[]{:S(2)}) collective-permute-start(bf16[64,768]{1,0:T(8,128)(2,1)S(1)} %reshape.146.rest_0_), channel_id=1, source_target_pairs={{0,3},{1,0},{2,1},{3,2},{4,7},{5,4},{6,5},{7,6},{8,11},{9,8},{10,9... | collective-permute-start | bytes 294920 | tf_op jit(solution)/shard_map/ppermute | solution.py:396
  139.2 6.8 %collective-permute-start.10 = (bf16[64,768]{1,0:T(8,128)(2,1)S(1)}, bf16[64,768]{1,0:T(8,128)(2,1)S(1)}, u32[]{:S(2)}, u32[]{:S(2)}) collective-permute-start(bf16[64,768]{1,0:T(8,128)(2,1)S(1)} %reshape.146.rest_0_), channel_id=1, source_target_pairs={{0,2},{1,3},{2,0},{3,1},{4,6},{5,7},{6,4},{7,5},{8,10},{9,11},{10,... | collective-permute-start | bytes 294920 | tf_op jit(solution)/shard_map/ppermute | solution.py:396
  139.8 7.6 %collective-permute-start.11 = (bf16[64,768]{1,0:T(8,128)(2,1)S(1)}, bf16[64,768]{1,0:T(8,128)(2,1)S(1)}, u32[]{:S(2)}, u32[]{:S(2)}) collective-permute-start(bf16[64,768]{1,0:T(8,128)(2,1)S(1)} %reshape.146.rest_0_), channel_id=1, source_target_pairs={{0,1},{1,2},{2,3},{3,0},{4,5},{5,6},{6,7},{7,4},{8,9},{9,10},{10,1... | collective-permute-start | bytes 294920 | tf_op jit(solution)/shard_map/ppermute | solution.py:396
  147.4 6.8 %collective-permute-start.12 = (bf16[64,768]{1,0:T(8,128)(2,1)S(1)}, bf16[64,768]{1,0:T(8,128)(2,1)S(1)}, u32[]{:S(2)}, u32[]{:S(2)}) collective-permute-start(bf16[64,768]{1,0:T(8,128)(2,1)S(1)} %reshape.146.rest_0_), channel_id=1, source_target_pairs={{0,4},{4,0},{8,12},{12,8},{16,20},{20,16},{24,28},{28,24},{32,36},... | collective-permute-start | bytes 294920 | tf_op jit(solution)/shard_map/ppermute | solution.py:387
  147.4 6.8 %collective-permute-start.13 = (bf16[64,768]{1,0:T(8,128)(2,1)S(1)}, bf16[64,768]{1,0:T(8,128)(2,1)S(1)}, u32[]{:S(2)}, u32[]{:S(2)}) collective-permute-start(bf16[64,768]{1,0:T(8,128)(2,1)S(1)} %collective-permute-done.9.rest_1_), channel_id=1, source_target_pairs={{0,4},{4,0},{8,12},{12,8},{16,20},{20,16},{24,28},{28,24},{32,36},... | collective-permute-start | bytes 294920 | tf_op jit(solution)/shard_map/ppermute | solution.py:387
  147.9 6.3 %collective-permute-start.14 = (bf16[64,768]{1,0:T(8,128)(2,1)S(1)}, bf16[64,768]{1,0:T(8,128)(2,1)S(1)}, u32[]{:S(2)}, u32[]{:S(2)}) collective-permute-start(bf16[64,768]{1,0:T(8,128)(2,1)S(1)} %collective-permute-done.10.rest_2_), channel_id=1, source_target_pairs={{0,4},{4,0},{8,12},{12,8},{16,20},{20,16},{24,28},{28,24},{32,36},... | collective-permute-start | bytes 294920 | tf_op jit(solution)/shard_map/ppermute | solution.py:387
  147.9 6.3 %collective-permute-start.15 = (bf16[64,768]{1,0:T(8,128)(2,1)S(1)}, bf16[64,768]{1,0:T(8,128)(2,1)S(1)}, u32[]{:S(2)}, u32[]{:S(2)}) collective-permute-start(bf16[64,768]{1,0:T(8,128)(2,1)S(1)} %collective-permute-done.11.rest_3_), channel_id=1, source_target_pairs={{0,4},{4,0},{8,12},{12,8},{16,20},{20,16},{24,28},{28,24},{32,36},... | collective-permute-start | bytes 294920 | tf_op jit(solution)/shard_map/ppermute | solution.py:387
  148.4 14.0 %all-to-all-start.4 = ((f32[32,1,768]{2,1,0:T(1,128)}), f32[32,1,768]{2,1,0:T(1,128)S(1)}, u32[]{:S(2)}, u32[]{:S(2)}) async-start(f32[32,1,768]{2,1,0:T(1,128)} %second_pass.1), calls=%async_computation.4 | async-start | bytes 196608 | tf_op jit(solution)/shard_map/all_to_all | solution.py:380
  165.0 5.2 %collective-permute-start.20 = (bf16[72,768]{1,0:T(8,128)(2,1)S(1)}, bf16[72,768]{1,0:T(8,128)(2,1)S(1)}, u32[]{:S(2)}, u32[]{:S(2)}) collective-permute-start(bf16[72,768]{1,0:T(8,128)(2,1)S(1)} %get-tuple-element.50), channel_id=1, source_target_pairs={{0,3},{1,0},{2,1},{3,2},{4,7},{5,4},{6,5},{7,6},{8,11},{9,8},{10,9... | collective-permute-start | bytes 331784 | tf_op jit(solution)/shard_map/ppermute | solution.py:396
  166.0 8.4 %collective-permute-start.19 = (bf16[72,768]{1,0:T(8,128)(2,1)S(1)}, bf16[72,768]{1,0:T(8,128)(2,1)S(1)}, u32[]{:S(2)}, u32[]{:S(2)}) collective-permute-start(bf16[72,768]{1,0:T(8,128)(2,1)S(1)} %get-tuple-element.49), channel_id=1, source_target_pairs={{0,1},{1,2},{2,3},{3,0},{4,5},{5,6},{6,7},{7,4},{8,9},{9,10},{10,1... | collective-permute-start | bytes 331784 | tf_op jit(solution)/shard_map/ppermute | solution.py:396
  167.1 7.3 %collective-permute-start.18 = (bf16[72,768]{1,0:T(8,128)(2,1)S(1)}, bf16[72,768]{1,0:T(8,128)(2,1)S(1)}, u32[]{:S(2)}, u32[]{:S(2)}) collective-permute-start(bf16[72,768]{1,0:T(8,128)(2,1)S(1)} %get-tuple-element.48), channel_id=1, source_target_pairs={{0,2},{1,3},{2,0},{3,1},{4,6},{5,7},{6,4},{7,5},{8,10},{9,11},{10,... | collective-permute-start | bytes 331784 | tf_op jit(solution)/shard_map/ppermute | solution.py:396
  175.9 22.4 %all-to-all-start.5 = ((bf16[64,2,1152]{2,1,0:T(2,128)(2,1)}), bf16[64,2,1152]{2,1,0:T(2,128)(2,1)S(1)}, u32[]{:S(2)}, u32[]{:S(2)}) async-start(bf16[64,2,1152]{2,1,0:T(2,128)(2,1)} %pad_maximum_fusion), calls=%async_computation.5 | async-start | bytes 589824 | tf_op jit(solution)/shard_map/all_to_all | solution.py:374
  198.8 6.0 %collective-permute-start.21 = (f32[4,768]{1,0:T(4,128)S(1)}, f32[4,768]{1,0:T(4,128)S(1)}, u32[]{:S(2)}, u32[]{:S(2)}) collective-permute-start(f32[4,768]{1,0:T(4,128)S(1)} %broadcast_multiply_fusion.1), channel_id=1, source_target_pairs={{0,1},{1,2},{2,3},{3,0},{4,5},{5,6},{6,7},{7,4},{8,9},{9,10},{10,1... | collective-permute-start | bytes 36872 | tf_op jit(solution)/shard_map/ppermute | solution.py:396
  198.8 6.0 %collective-permute-start.22 = (f32[4,768]{1,0:T(4,128)S(1)}, f32[4,768]{1,0:T(4,128)S(1)}, u32[]{:S(2)}, u32[]{:S(2)}) collective-permute-start(f32[4,768]{1,0:T(4,128)S(1)} %broadcast_multiply_fusion.1), channel_id=1, source_target_pairs={{0,2},{1,3},{2,0},{3,1},{4,6},{5,7},{6,4},{7,5},{8,10},{9,11},{10,... | collective-permute-start | bytes 36872 | tf_op jit(solution)/shard_map/ppermute | solution.py:396
  201.4 3.7 %collective-permute-start.23 = (f32[4,768]{1,0:T(4,128)S(1)}, f32[4,768]{1,0:T(4,128)S(1)}, u32[]{:S(2)}, u32[]{:S(2)}) collective-permute-start(f32[4,768]{1,0:T(4,128)S(1)} %broadcast_multiply_fusion.1), channel_id=1, source_target_pairs={{0,3},{1,0},{2,1},{3,2},{4,7},{5,4},{6,5},{7,6},{8,11},{9,8},{10,9... | collective-permute-start | bytes 36872 | tf_op jit(solution)/shard_map/ppermute | solution.py:396
  (20 other events, 93.0 us)
